TPU v7x, 32 devices: a whole 2x2x4 slice. The times are simulated.
32 devices in a mesh: tile: 8 (over y, x, core), depth: 4 (over z).
Axes of the slice: x: 2, y: 2, z: 4, core: 2. Of those that a mesh axis runs over, the one named last changes fastest.
Arguments:
- estimate: float32 [8, 256, 1024], P('depth', 'tile'), may hold values from 0.25 to 4
- views: bfloat16 [8, 8, 256, 1024], P(None, 'depth', 'tile'), may hold values from 0.19921875 to 5
- kernel_x: float32 [8, 31], replicated, may hold values from 0.01 to 1
- kernel_y: float32 [8, 31], replicated, may hold values from 0.01 to 1
- kernel_z: float32 [8, 31], replicated, may hold values from 0.01 to 1
- offsets: int32 [8], replicated, may hold values from 16 to 96
Outputs:
- updated: float32 [8, 256, 1024], P('depth', 'tile')
All inputs are finite; a program needn't handle non-finite values.
Results may differ from a plain program's by a relative error of at most 0.0007.
Values may be sent and summed in bfloat16 or wider, within the bound.
No kernel may reach another device: no remote copies, remote signals or barrier semaphores. Data moves between devices by JAX's collectives and lax.ppermute only.
A program may use at most 128 MiB of HBM per device.

v0:
```python
import functools
import jax
import jax.numpy as jnp
from jax import lax
from jax.experimental import pallas as pl
from jax.experimental.pallas import tpu as pltpu
from jax.sharding import PartitionSpec as P

F32, BF16 = jnp.float32, jnp.bfloat16
HALO = 16
LANES = 128
WIDE = 256
INFO = 4
VMEM_LIMIT = 40 * 1024 * 1024


def select_taps(index, kernel):
    total = jnp.zeros((kernel.shape[0],) + index.shape[1:], F32)
    for tap in range(kernel.shape[1]):
        total = total + jnp.where(index == tap, kernel[:, tap : tap + 1], 0.0)
    return total


def slanted(row, rows):
    spread = jnp.broadcast_to(row, (rows, row.shape[1]))
    return pltpu.roll(spread, 0, 1, stride=1, stride_axis=0)


def matrices_kernel(planes, strip, device_ref, kernels_ref, w_ref, wt_ref, tf_ref, tb_ref):
    views, taps = kernels_ref.shape[1:]
    margin = taps // 2
    extent = strip + 2 * HALO
    kx, ky, kz = [kernels_ref[n] / jnp.sum(kernels_ref[n], axis=1, keepdims=True) for n in range(3)]
    lane = lax.broadcasted_iota(jnp.int32, (1, LANES), 1)
    x_row = select_taps(lane % extent - (HALO - margin), kx)
    near = jnp.where(lane < LANES // 2, lane, lane - LANES)
    forward_row = select_taps(margin - near, ky)
    backward_row = select_taps(margin + near, ky)
    column = lax.broadcasted_iota(jnp.int32, (1, w_ref.shape[1]), 1) // extent
    device, odd = device_ref[0], device_ref[1] == 1
    plane = (device ^ (column // planes)) * planes + column % planes
    spot = lax.broadcasted_iota(jnp.int32, (strip, LANES), 1) % extent
    z_rows = [select_taps(plane - (device * planes + own) + margin, kz) for own in range(planes)]
    for view in range(views):
        x_block = slanted(x_row[view : view + 1], strip)
        turned = x_block
        for quarter in range(extent // HALO):
            shift = extent - (2 * quarter + 1) * HALO
            moved = pltpu.roll(x_block, (LANES - shift) % LANES, 1)
            here = jnp.logical_and(spot // HALO == quarter, jnp.logical_not(odd))
            turned = jnp.where(here, moved, turned)
        x_block = turned
        x_block = jnp.concatenate([x_block] * (w_ref.shape[1] // LANES), axis=1)
        for own in range(planes):
            first = (view * planes + own) * strip
            block = x_block * z_rows[own][view : view + 1]
            w_ref[first : first + strip, :] = block.astype(BF16)
    wt_ref[...] = w_ref[...].astype(F32).T.astype(BF16)
    i = lax.broadcasted_iota(jnp.int32, (LANES, LANES), 0)
    j = lax.broadcasted_iota(jnp.int32, (LANES, LANES), 1)
    zeros = jnp.zeros((LANES, LANES), BF16)
    for view in range(views):
        for row, out in ((forward_row, tf_ref), (backward_row, tb_ref)):
            circle = slanted(row[view : view + 1], LANES)
            middle = jnp.where(jnp.abs(j - i) < LANES // 2, circle, 0.0).astype(BF16)
            earlier = jnp.where(i - j > LANES // 2, circle, 0.0).astype(BF16)
            later = jnp.where(j - i > LANES // 2, circle, 0.0).astype(BF16)
            grid = ((earlier, zeros), (middle, earlier), (later, middle), (zeros, later))
            for a, blocks in enumerate(grid):
                for b, block in enumerate(blocks):
                    out[view, a * LANES : (a + 1) * LANES, b * LANES : (b + 1) * LANES] = block


def write_coded(out_ref, where, values):
    pick = values.shape[-1] // 2 - LANES
    base = values[..., pick : pick + LANES].astype(BF16)
    wide = base.astype(F32)
    for first in range(0, values.shape[-1], LANES):
        part = values[..., first : first + LANES]
        part = base if first == pick else (part - wide).astype(BF16)
        out_ref[where + (slice(first, first + LANES),)] = part


def decoded(values, first):
    pick = values.shape[-1] // 2 - LANES
    base = values[..., pick : pick + LANES].astype(F32)
    if first == pick:
        return base
    return base + values[..., first : first + LANES].astype(F32)


def main_kernel(planes, view_rows, info_ref, *refs):
    quarters, (views_ref, w_ref, wt_ref, tf_ref, tb_ref) = refs[:4], refs[4:9]
    core_ref, inner_ref, *outer_refs, scale_ref, odd_ref = refs[9:17]
    ext_ref, pad_ref, back_ref, deep_ref = refs[17:]
    views = info_ref.shape[0] - INFO
    count = quarters[0].shape[0]
    extent = ext_ref.shape[0] // count
    strip = extent - 2 * HALO
    columns = ext_ref.shape[-1]
    group = planes * strip
    for p in range(count):
        for n, ref in enumerate(quarters[::-1]):
            ext_ref[p * extent + n * HALO : p * extent + (n + 1) * HALO, :] = ref[p]

    @pl.when(info_ref[2] == 0)
    def _():
        for p in range(count):
            ext_ref[(p + 1) * extent - HALO : (p + 1) * extent, :] = jnp.zeros((HALO, columns), BF16)

    for pad in (pad_ref, back_ref):
        pad[:, :LANES] = jnp.zeros((pad.shape[0], LANES), BF16)
        pad[:, LANES + columns :] = jnp.zeros((pad.shape[0], LANES), BF16)
    for first in range(0, columns, WIDE):
        block = jnp.dot(w_ref[...], ext_ref[:, first : first + WIDE], preferred_element_type=F32)
        pad_ref[:, LANES + first : LANES + first + WIDE] = block.astype(BF16)
    row = info_ref[3] + lax.broadcasted_iota(jnp.int32, (group, WIDE), 0) % strip
    coverage = jnp.zeros((strip, LANES), F32)
    starts = range(0, columns, WIDE)

    def windows(pad, rows):
        return jnp.concatenate([pad[rows, first : first + WIDE + 2 * LANES] for first in starts], axis=0)

    for view in range(views):
        rows = slice(view * group, (view + 1) * group)
        low = info_ref[INFO + view]
        inside = (row >= low) & (row < low + view_rows)
        coverage = coverage + jnp.where(inside[:strip, :LANES], 1.0, 0.0)
        blurred = jnp.dot(windows(pad_ref, rows), tf_ref[view], preferred_element_type=F32)
        for n, first in enumerate(starts):
            part = blurred[n * group : (n + 1) * group]
            seen = views_ref[rows, first : first + WIDE].astype(F32)
            correction = jnp.where(inside, seen / part - 1.0, 0.0)
            back_ref[rows, LANES + first : LANES + first + WIDE] = correction.astype(BF16)
        backward = jnp.dot(windows(back_ref, rows), tb_ref[view], preferred_element_type=F32)
        for n, first in enumerate(starts):
            deep_ref[rows, first : first + WIDE] = backward[n * group : (n + 1) * group].astype(BF16)
    for p in range(count):
        part = jnp.dot(wt_ref[p * extent : (p + 1) * extent], deep_ref[...], preferred_element_type=F32)
        write_coded(inner_ref, (p, slice(None)), part[:HALO])
        core_ref[p] = part[HALO : 2 * HALO]
        outer_refs[p // (count // 2)][p % (count // 2)] = part[2 * HALO : 3 * HALO]
        write_coded(outer_refs[2 + p // (count // 2)], (p % (count // 2), slice(None)), part[3 * HALO :])
    scale_ref[...] = 1.0 / jnp.maximum(coverage, 1.0)
    odd_ref[...] = jnp.full(odd_ref.shape, info_ref[1], jnp.int32)

    @pl.when(info_ref[2] == 0)
    def _():
        for ref in outer_refs[2:]:
            ref[...] = jnp.zeros(ref.shape, BF16)


def join_kernel(planes, kept, core_ref, other_ref, *outs):
    columns = core_ref.shape[2]
    for p in range(core_ref.shape[0]):
        other = other_ref[p]
        parts = []
        for first in range(0, columns, LANES):
            parts.append(core_ref[p, :, first : first + LANES] + decoded(other, first))
        whole = jnp.concatenate(parts, axis=1)
        if p < kept:
            outs[0][p] = whole
        else:
            write_coded(outs[p // planes], (p % planes, slice(None)), whole)


def update_kernel(estimate_ref, scale_ref, odd_ref, *refs):
    parts, out_ref = refs[:-1], refs[-1]
    planes, strip, columns = estimate_ref.shape
    half = len(parts) // 2
    odd = odd_ref[...] == 1
    for p in range(planes):
        for first in range(0, columns, LANES):
            lanes = slice(first, first + LANES)
            sums = []
            for own_ref, *others in (parts[:half], parts[half:]):
                total = own_ref[p, :, lanes]
                for ref in others:
                    total = total + decoded(ref[p], first)
                sums.append(total)
            inner, outer = sums
            for rows, total in (
                (slice(0, HALO), jnp.where(odd, inner, outer)),
                (slice(HALO, strip), jnp.where(odd, outer, inner)),
            ):
                out_ref[p, rows, lanes] = estimate_ref[p, rows, lanes] * (1.0 + total * scale_ref[rows, :])


def call(body, outs, scalars, arrays, scratch=(), flops=0, moved=0):
    return pl.pallas_call(
        body,
        out_shape=outs,
        in_specs=[pl.BlockSpec(memory_space=pltpu.SMEM)] * scalars
        + [pl.BlockSpec(memory_space=pltpu.VMEM)] * arrays,
        out_specs=jax.tree.map(lambda _: pl.BlockSpec(memory_space=pltpu.VMEM), outs),
        scratch_shapes=list(scratch),
        compiler_params=pltpu.CompilerParams(vmem_limit_bytes=VMEM_LIMIT),
        cost_estimate=pl.CostEstimate(flops=flops, bytes_accessed=moved, transcendentals=0),
    )


def shards(estimate, views, kernel_x, kernel_y, kernel_z, offsets):
    shape = jax.ShapeDtypeStruct
    depth, tiles = lax.axis_size("depth"), lax.axis_size("tile")
    planes, strip, columns = estimate.shape
    count = views.shape[0]
    extent = strip + 2 * HALO
    rows = count * planes * strip
    span = depth * planes * extent
    view_rows = 5 * strip * tiles // 8
    tile = lax.axis_index("tile").astype(jnp.int32)
    odd = tile % 2
    has_chip = ((tile > 0) & (tile < tiles - 1)).astype(jnp.int32)
    block_index = lax.axis_index("depth").astype(jnp.int32)
    info = jnp.concatenate([jnp.stack([block_index, odd, has_chip, tile * strip]), offsets])
    assert strip == 2 * HALO and tiles % 2 == 0

    def across(array, step):
        return lax.ppermute(array, "depth", [(i, i ^ step) for i in range(depth)])

    def beside(array):
        pairs = []
        for d in range(depth):
            pairs += [(i * depth + d, (i - 1 + 2 * (i % 2)) * depth + d) for i in range(1, tiles - 1)]
            pairs += [(i * depth + d, i * depth + (d ^ 1)) for i in (0, tiles - 1)]
        return lax.ppermute(array, ("tile", "depth"), pairs)

    def within(array):
        return lax.ppermute(array, "tile", [(i, i ^ 1) for i in range(tiles)])

    own = estimate.astype(BF16)
    early, late = own[:, :HALO], own[:, HALO:]
    outer_own, inner_own = jnp.where(odd == 1, late, early), jnp.where(odd == 1, early, late)
    outer = jnp.concatenate([outer_own] + [across(outer_own, step) for step in range(1, depth)], axis=0)
    other_chip = beside(outer)
    inner = jnp.concatenate([inner_own] + [across(inner_own, step) for step in range(1, depth)], axis=0)
    other_core = within(inner)
    w, wt, tf, tb = call(
        functools.partial(matrices_kernel, planes, strip),
        (shape((rows, span), BF16), shape((span, rows), BF16))
        + (shape((count, WIDE + 2 * LANES, WIDE), BF16),) * 2,
        1, 1, flops=10**8, moved=5 * 2**20,
    )(info, jnp.stack([kernel_x, kernel_y, kernel_z]))
    halves = (depth * planes, HALO, columns)
    quarter = (depth * planes // 2, HALO, columns)
    core, to_core, near, far, near_edge, far_edge, scale, odd_rows = call(
        functools.partial(main_kernel, planes, view_rows),
        (shape(halves, F32), shape(halves, BF16)) + (shape(quarter, F32),) * 2 + (shape(quarter, BF16),) * 2
        + (shape((strip, LANES), F32), shape((HALO, LANES), jnp.int32)),
        1, 9,
        scratch=(
            pltpu.VMEM((span, columns), BF16),
            pltpu.VMEM((rows, columns + 2 * LANES), BF16),
            pltpu.VMEM((rows, columns + 2 * LANES), BF16),
            pltpu.VMEM((rows, columns), BF16),
        ),
        flops=2 * 10**9, moved=10 * 2**20,
    )(info, other_chip, outer, inner, other_core, views.reshape(rows, columns), w, wt, tf, tb)
    block = (planes, HALO, columns)

    def joined(core, other, first, earlier=()):
        core, _ = lax.optimization_barrier((core, earlier))
        steps = range(first, first + core.shape[0] // planes)
        totals = call(
            functools.partial(join_kernel, planes, planes if first == 0 else 0),
            tuple(shape(block, BF16 if step else F32) for step in steps),
            0, 2, flops=10**6, moved=3 * 2**20,
        )(core, other)
        return totals, [across(total, step) if step else total for step, total in zip(steps, totals)]

    far_edge = beside(far_edge)
    totals, sums = joined(core, within(to_core), 0)
    totals, far = joined(far, far_edge, depth // 2, totals)
    sums += joined(near, beside(near_edge), 0, [totals, sums[2:]])[1] + far
    return call(
        update_kernel,
        shape(estimate.shape, F32),
        0, 3 + 2 * depth, flops=10**6, moved=2**20,
    )(estimate, scale, odd_rows, *sums)


def solution(mesh):
    in_specs = (P("depth", "tile", None), P(None, "depth", "tile", None), P(), P(), P(), P())
    out_specs = P("depth", "tile", None)
    return jax.shard_map(shards, mesh=mesh, in_specs=in_specs, out_specs=out_specs, check_vma=False)
```

profile of v0, /device:TPU:0, one launch (start us, length us, event | category | flops | bytes accessed | tf_op | source)
XLA Modules:
  0.0 46.2 jit_solution(7500448145239414278)
XLA Ops:
  0.0 0.0 copy-start.1
  0.0 1.1 %convert_element_type.4 = bf16[2,32,1024]{2,1,0:T(8,128)(2,1)S(1)} convert(f32[2,32,1024]{2,1,0:T(8,128)} %estimate_ref.1) | non-fusion elementwise | flops 65536 | bytes 393216 | tf_op jit(solution)/shard_map/convert_element_type | solution.py:231
  1.1 5.1 %collective-permute-start.2 = (bf16[2,16,1024]{2,1,0:T(8,128)(2,1)S(1)}, bf16[2,16,1024]{2,1,0:T(8,128)(2,1)S(1)}, u32[]{:S(2)}, u32[]{:S(2)}) collective-permute-start(bf16[2,16,1024]{2,1,0:T(8,128)(2,1)S(1)} %get-tuple-element.50), channel_id=1, source_target_pairs={{0,3},{1,2},{2,1},{3,0},{4,7},{5,6},{6,5},{7,4},{8,11},{9,10},{10,... | collective-permute-start | bytes 196616 | tf_op jit(solution)/shard_map/ppermute | solution.py:219
  6.2 0.0 collective-permute-start.1
  6.2 0.6 %collective-permute-start = (bf16[2,16,1024]{2,1,0:T(8,128)(2,1)S(1)}, bf16[2,16,1024]{2,1,0:T(8,128)(2,1)S(1)}, u32[]{:S(2)}, u32[]{:S(2)}) collective-permute-start(bf16[2,16,1024]{2,1,0:T(8,128)(2,1)S(1)} %get-tuple-element.50), channel_id=1, source_target_pairs={{0,1},{1,0},{2,3},{3,2},{4,5},{5,4},{6,7},{7,6},{8,9},{9,8},{10,11... | collective-permute-start | bytes 196616 | tf_op jit(solution)/shard_map/ppermute | solution.py:219
  6.8 3.7 %collective-permute-start.6 = (bf16[2,16,1024]{2,1,0:T(8,128)(2,1)S(1)}, bf16[2,16,1024]{2,1,0:T(8,128)(2,1)S(1)}, u32[]{:S(2)}, u32[]{:S(2)}) collective-permute-start(bf16[2,16,1024]{2,1,0:T(8,128)(2,1)S(1)} %get-tuple-element.49), channel_id=1, source_target_pairs={{0,3},{1,2},{2,1},{3,0},{4,7},{5,6},{6,5},{7,4},{8,11},{9,10},{10,... | collective-permute-start | bytes 196616 | tf_op jit(solution)/shard_map/ppermute | solution.py:219
  10.6 0.0 collective-permute-start.5
  10.6 0.0 collective-permute-done.2
  10.6 0.8 %collective-permute-start.4 = (bf16[2,16,1024]{2,1,0:T(8,128)(2,1)S(1)}, bf16[2,16,1024]{2,1,0:T(8,128)(2,1)S(1)}, u32[]{:S(2)}, u32[]{:S(2)}) collective-permute-start(bf16[2,16,1024]{2,1,0:T(8,128)(2,1)S(1)} %get-tuple-element.49), channel_id=1, source_target_pairs={{0,1},{1,0},{2,3},{3,2},{4,5},{5,4},{6,7},{7,6},{8,9},{9,8},{10,11... | collective-permute-start | bytes 196616 | tf_op jit(solution)/shard_map/ppermute | solution.py:219
  11.4 3.4 %collective-permute-done.1 = bf16[2,16,1024]{2,1,0:T(8,128)(2,1)S(1)} collective-permute-done((bf16[2,16,1024]{2,1,0:T(8,128)(2,1)S(1)}, bf16[2,16,1024]{2,1,0:T(8,128)(2,1)S(1)}, u32[]{:S(2)}, u32[]{:S(2)}) %collective-permute-start.1) | collective-permute-done | bytes 65568 | tf_op jit(solution)/shard_map/ppermute | solution.py:219
  14.8 0.0 collective-permute-done
  14.8 0.1 collective-permute-start.3
  14.9 0.0 collective-permute-done.6
  14.9 2.5 %collective-permute-done.5 = bf16[2,16,1024]{2,1,0:T(8,128)(2,1)S(1)} collective-permute-done((bf16[2,16,1024]{2,1,0:T(8,128)(2,1)S(1)}, bf16[2,16,1024]{2,1,0:T(8,128)(2,1)S(1)}, u32[]{:S(2)}, u32[]{:S(2)}) %collective-permute-start.5) | collective-permute-done | bytes 65568 | tf_op jit(solution)/shard_map/ppermute | solution.py:219
  17.4 0.0 collective-permute-done.4
  17.5 0.1 collective-permute-start.7
  17.6 0.7 %concatenate.9.device_ref.info_ref = s32[12]{0:T(128)S(1)} concatenate(s32[1]{0:T(128)} %bitcast, s32[1]{0:T(128)} %bitcast.1, s32[1]{0:T(128)} %bitcast.2, s32[1]{0:T(128)} %bitcast.3, s32[8]{0:T(128)} %param.11), dimensions={0} | concatenate | bytes 96 | tf_op jit(solution)/shard_map/concatenate | solution.py:215
  18.3 0.7 %pad_maximum_fusion.2.kernels_ref = f32[3,8,31]{2,1,0:T(8,128)S(1)} fusion(f32[1,8,31]{2,1,0:T(8,128)} %bitcast.9, f32[1,8,31]{2,1,0:T(8,128)} %bitcast.10, f32[1,8,31]{2,1,0:T(8,128)} %bitcast.11), kind=kLoop, calls=%fused_computation.4 | loop fusion | flops 1488 | bytes 5952 | tf_op jit(solution)/shard_map/stack | solution.py:243
  19.0 1.9 %shard_map.64 = (bf16[512,512]{1,0:T(8,128)(2,1)S(1)}, bf16[512,512]{1,0:T(8,128)(2,1)S(1)}, bf16[8,512,256]{2,1,0:T(8,128)(2,1)S(1)}, bf16[8,512,256]{2,1,0:T(8,128)(2,1)S(1)}) custom-call(s32[12]{0:T(128)S(1)} %concatenate.9.device_ref.info_ref, f32[3,8,31]{2,1,0:T(8,128)S(1)} %pad_maximum_fusion.2.kernels_ref), custom_call_target="tpu_custom_call" | custom-call | flops 100000000 | bytes 5242880 | tf_op jit(solution)/shard_map/pallas_call | solution.py:238
  20.9 0.4 collective-permute-done.3.refs_0_
  21.3 0.0 collective-permute-done.7.refs_3_
  21.3 0.0 copy-done.1
  21.3 0.0 copy-start
  21.3 4.0 %shard_map.65 = (f32[8,16,1024]{2,1,0:T(8,128)S(1)}, bf16[8,16,1024]{2,1,0:T(8,128)(2,1)S(1)}, f32[4,16,1024]{2,1,0:T(8,128)S(1)}, f32[4,16,1024]{2,1,0:T(8,128)...) custom-call(s32[12]{0:T(128)S(1)} %concatenate.9.device_ref.info_ref, ...), custom_call_target="tpu_custom_call" | custom-call | flops 2000000000 | bytes 10485760 | tf_op jit(solution)/shard_map/pallas_call | solution.py:246
  25.3 0.9 %collective-permute-start.8 = (bf16[8,16,1024]{2,1,0:T(8,128)(2,1)S(1)}, bf16[8,16,1024]{2,1,0:T(8,128)(2,1)S(1)}, u32[]{:S(2)}, u32[]{:S(2)}) collective-permute-start(bf16[8,16,1024]{2,1,0:T(8,128)(2,1)S(1)} %get-tuple-element.34), channel_id=1, source_target_pairs={{0,4},{4,0},{8,12},{12,8},{16,20},{20,16},{24,28},{28,24},{1,5},{5... | collective-permute-start | bytes 786440 | tf_op jit(solution)/shard_map/ppermute | solution.py:229
  26.2 0.0 collective-permute-start.12
  26.2 2.0 %collective-permute-start.13 = (bf16[4,16,1024]{2,1,0:T(8,128)(2,1)S(1)}, bf16[4,16,1024]{2,1,0:T(8,128)(2,1)S(1)}, u32[]{:S(2)}, u32[]{:S(2)}) collective-permute-start(bf16[4,16,1024]{2,1,0:T(8,128)(2,1)S(1)} %get-tuple-element.46), channel_id=1, source_target_pairs={{4,8},{8,4},{12,16},{16,12},{20,24},{24,20},{0,1},{28,29},{5,9},{9... | collective-permute-start | bytes 393224 | tf_op jit(solution)/shard_map/ppermute | solution.py:226
  28.2 0.0 collective-permute-done.8.other_ref
  28.2 0.1 shard_map.66
  28.3 1.5 %collective-permute-start.10 = (bf16[2,16,1024]{2,1,0:T(8,128)(2,1)S(1)}, bf16[2,16,1024]{2,1,0:T(8,128)(2,1)S(1)}, u32[]{:S(2)}, u32[]{:S(2)}) collective-permute-start(bf16[2,16,1024]{2,1,0:T(8,128)(2,1)S(1)} %get-tuple-element.37), channel_id=1, source_target_pairs={{0,2},{1,3},{2,0},{3,1},{4,6},{5,7},{6,4},{7,5},{8,10},{9,11},{10,... | collective-permute-start | bytes 196616 | tf_op jit(solution)/shard_map/ppermute | solution.py:219
  29.8 1.5 %collective-permute-start.11 = (bf16[2,16,1024]{2,1,0:T(8,128)(2,1)S(1)}, bf16[2,16,1024]{2,1,0:T(8,128)(2,1)S(1)}, u32[]{:S(2)}, u32[]{:S(2)}) collective-permute-start(bf16[2,16,1024]{2,1,0:T(8,128)(2,1)S(1)} %get-tuple-element.38), channel_id=1, source_target_pairs={{0,3},{1,2},{2,1},{3,0},{4,7},{5,6},{6,5},{7,4},{8,11},{9,10},{10,... | collective-permute-start | bytes 196616 | tf_op jit(solution)/shard_map/ppermute | solution.py:219
  31.3 0.5 %collective-permute-start.9 = (bf16[2,16,1024]{2,1,0:T(8,128)(2,1)S(1)}, bf16[2,16,1024]{2,1,0:T(8,128)(2,1)S(1)}, u32[]{:S(2)}, u32[]{:S(2)}) collective-permute-start(bf16[2,16,1024]{2,1,0:T(8,128)(2,1)S(1)} %get-tuple-element.36), channel_id=1, source_target_pairs={{0,1},{1,0},{2,3},{3,2},{4,5},{5,4},{6,7},{7,6},{8,9},{9,8},{10,11... | collective-permute-start | bytes 196616 | tf_op jit(solution)/shard_map/ppermute | solution.py:219
  31.8 0.0 collective-permute-done.12.other_ref
  31.9 2.4 %collective-permute-start.15 = (bf16[2,16,1024]{2,1,0:T(8,128)(2,1)S(1)}, bf16[2,16,1024]{2,1,0:T(8,128)(2,1)S(1)}, u32[]{:S(2)}, u32[]{:S(2)}) collective-permute-start(bf16[2,16,1024]{2,1,0:T(8,128)(2,1)S(1)} %get-tuple-element.43), channel_id=1, source_target_pairs={{0,2},{1,3},{2,0},{3,1},{4,6},{5,7},{6,4},{7,5},{8,10},{9,11},{10,... | collective-permute-start | bytes 196616 | tf_op jit(solution)/shard_map/ppermute | solution.py:219
  34.3 0.6 %collective-permute-done.10.refs_2_ = bf16[2,16,1024]{2,1,0:T(8,128)(2,1)S(1)} collective-permute-done((bf16[2,16,1024]{2,1,0:T(8,128)(2,1)S(1)}, bf16[2,16,1024]{2,1,0:T(8,128)(2,1)S(1)}, u32[]{:S(2)}, u32[]{:S(2)}) %collective-permute-start.10) | collective-permute-done | bytes 65568 | tf_op jit(solution)/shard_map/ppermute | solution.py:219
  35.0 6.1 %collective-permute-start.16 = (bf16[2,16,1024]{2,1,0:T(8,128)(2,1)S(1)}, bf16[2,16,1024]{2,1,0:T(8,128)(2,1)S(1)}, u32[]{:S(2)}, u32[]{:S(2)}) collective-permute-start(bf16[2,16,1024]{2,1,0:T(8,128)(2,1)S(1)} %get-tuple-element.44), channel_id=1, source_target_pairs={{0,3},{1,2},{2,1},{3,0},{4,7},{5,6},{6,5},{7,4},{8,11},{9,10},{10,... | collective-permute-start | bytes 196616 | tf_op jit(solution)/shard_map/ppermute | solution.py:219
  41.0 0.0 collective-permute-done.11.refs_3_
  41.0 0.0 collective-permute-done.13.other_ref
  41.1 0.1 collective-permute-start.14
  41.1 0.1 collective-permute-done.15.refs_6_
  41.3 2.0 %collective-permute-done.16.refs_7_ = bf16[2,16,1024]{2,1,0:T(8,128)(2,1)S(1)} collective-permute-done((bf16[2,16,1024]{2,1,0:T(8,128)(2,1)S(1)}, bf16[2,16,1024]{2,1,0:T(8,128)(2,1)S(1)}, u32[]{:S(2)}, u32[]{:S(2)}) %collective-permute-start.16) | collective-permute-done | bytes 65568 | tf_op jit(solution)/shard_map/ppermute | solution.py:219
  43.3 0.0 collective-permute-done.9.refs_1_
  43.3 2.1 %collective-permute-done.14.refs_5_ = bf16[2,16,1024]{2,1,0:T(8,128)(2,1)S(1)} collective-permute-done((bf16[2,16,1024]{2,1,0:T(8,128)(2,1)S(1)}, bf16[2,16,1024]{2,1,0:T(8,128)(2,1)S(1)}, u32[]{:S(2)}, u32[]{:S(2)}) %collective-permute-start.14) | collective-permute-done | bytes 65568 | tf_op jit(solution)/shard_map/ppermute | solution.py:219
  45.4 0.0 copy-done
  45.4 0.8 %shard_map.69 = f32[2,32,1024]{2,1,0:T(8,128)} custom-call(f32[2,32,1024]{2,1,0:T(8,128)S(1)} %copy-done, f32[32,128]{1,0:T(8,128)S(1)} %get-tuple-element.31.scale_ref, s32[16,128]{1,0:T(8,128)S(1)} %get-tuple-element.32.odd_ref, f32[2,16,1024]{2,1,0:T(8,128)S(1)} %get-tuple-element.35.refs_0_, bf16[2,16,1024]{2,1,0:T(8,128)(2,1)S(1)} %collective-permute-done.9.refs_1_, ...), custom_call_target="tpu_custom_call" | custom-call | flops 1000000 | bytes 1048576 | tf_op jit(solution)/shard_map/pallas_call | solution.py:275
  (5 shorter events, 0.2 us)
Async XLA Ops:
  0.0 21.3 %copy-start.1 = (bf16[8,2,32,1024]{3,2,1,0:T(8,128)(2,1)S(1)}, bf16[8,2,32,1024]{3,2,1,0:T(8,128)(2,1)}, u32[]{:S(2)}) copy-start(bf16[8,2,32,1024]{3,2,1,0:T(8,128)(2,1)} %param.7) | copy-start | bytes 3145732
  1.1 9.5 %collective-permute-start.2 = (bf16[2,16,1024]{2,1,0:T(8,128)(2,1)S(1)}, bf16[2,16,1024]{2,1,0:T(8,128)(2,1)S(1)}, u32[]{:S(2)}, u32[]{:S(2)}) collective-permute-start(bf16[2,16,1024]{2,1,0:T(8,128)(2,1)S(1)} %get-tuple-element.50), channel_id=1, source_target_pairs={{0,3},{1,2},{2,1},{3,0},{4,7},{5,6},{6,5},{7,4},{8,11},{9,10},{10,... | collective-permute-start | bytes 196616 | tf_op jit(solution)/shard_map/ppermute | solution.py:219
  6.2 8.6 %collective-permute-start.1 = (bf16[2,16,1024]{2,1,0:T(8,128)(2,1)S(1)}, bf16[2,16,1024]{2,1,0:T(8,128)(2,1)S(1)}, u32[]{:S(2)}, u32[]{:S(2)}) collective-permute-start(bf16[2,16,1024]{2,1,0:T(8,128)(2,1)S(1)} %get-tuple-element.50), channel_id=1, source_target_pairs={{0,2},{1,3},{2,0},{3,1},{4,6},{5,7},{6,4},{7,5},{8,10},{9,11},{10,... | collective-permute-start | bytes 196616 | tf_op jit(solution)/shard_map/ppermute | solution.py:219
  6.2 8.6 %collective-permute-start = (bf16[2,16,1024]{2,1,0:T(8,128)(2,1)S(1)}, bf16[2,16,1024]{2,1,0:T(8,128)(2,1)S(1)}, u32[]{:S(2)}, u32[]{:S(2)}) collective-permute-start(bf16[2,16,1024]{2,1,0:T(8,128)(2,1)S(1)} %get-tuple-element.50), channel_id=1, source_target_pairs={{0,1},{1,0},{2,3},{3,2},{4,5},{5,4},{6,7},{7,6},{8,9},{9,8},{10,11... | collective-permute-start | bytes 196616 | tf_op jit(solution)/shard_map/ppermute | solution.py:219
  6.8 8.1 %collective-permute-start.6 = (bf16[2,16,1024]{2,1,0:T(8,128)(2,1)S(1)}, bf16[2,16,1024]{2,1,0:T(8,128)(2,1)S(1)}, u32[]{:S(2)}, u32[]{:S(2)}) collective-permute-start(bf16[2,16,1024]{2,1,0:T(8,128)(2,1)S(1)} %get-tuple-element.49), channel_id=1, source_target_pairs={{0,3},{1,2},{2,1},{3,0},{4,7},{5,6},{6,5},{7,4},{8,11},{9,10},{10,... | collective-permute-start | bytes 196616 | tf_op jit(solution)/shard_map/ppermute | solution.py:219
  10.6 6.8 %collective-permute-start.5 = (bf16[2,16,1024]{2,1,0:T(8,128)(2,1)S(1)}, bf16[2,16,1024]{2,1,0:T(8,128)(2,1)S(1)}, u32[]{:S(2)}, u32[]{:S(2)}) collective-permute-start(bf16[2,16,1024]{2,1,0:T(8,128)(2,1)S(1)} %get-tuple-element.49), channel_id=1, source_target_pairs={{0,2},{1,3},{2,0},{3,1},{4,6},{5,7},{6,4},{7,5},{8,10},{9,11},{10,... | collective-permute-start | bytes 196616 | tf_op jit(solution)/shard_map/ppermute | solution.py:219
  10.6 6.8 %collective-permute-start.4 = (bf16[2,16,1024]{2,1,0:T(8,128)(2,1)S(1)}, bf16[2,16,1024]{2,1,0:T(8,128)(2,1)S(1)}, u32[]{:S(2)}, u32[]{:S(2)}) collective-permute-start(bf16[2,16,1024]{2,1,0:T(8,128)(2,1)S(1)} %get-tuple-element.49), channel_id=1, source_target_pairs={{0,1},{1,0},{2,3},{3,2},{4,5},{5,4},{6,7},{7,6},{8,9},{9,8},{10,11... | collective-permute-start | bytes 196616 | tf_op jit(solution)/shard_map/ppermute | solution.py:219
  14.8 6.4 %collective-permute-start.3 = (bf16[8,16,1024]{2,1,0:T(8,128)(2,1)S(1)}, bf16[8,16,1024]{2,1,0:T(8,128)(2,1)S(1)}, u32[]{:S(2)}, u32[]{:S(2)}) collective-permute-start(bf16[8,16,1024]{2,1,0:T(8,128)(2,1)S(1)} %pad_maximum_fusion.refs_1_), channel_id=1, source_target_pairs={{4,8},{8,4},{12,16},{16,12},{20,24},{24,20},{0,1},{28,29},{5,9},{9... | collective-permute-start | bytes 786440 | tf_op jit(solution)/shard_map/ppermute | solution.py:226
  17.5 3.8 %collective-permute-start.7 = (bf16[8,16,1024]{2,1,0:T(8,128)(2,1)S(1)}, bf16[8,16,1024]{2,1,0:T(8,128)(2,1)S(1)}, u32[]{:S(2)}, u32[]{:S(2)}) collective-permute-start(bf16[8,16,1024]{2,1,0:T(8,128)(2,1)S(1)} %pad_maximum_fusion.1.refs_2_), channel_id=1, source_target_pairs={{0,4},{4,0},{8,12},{12,8},{16,20},{20,16},{24,28},{28,24},{1,5},{5... | collective-permute-start | bytes 786440 | tf_op jit(solution)/shard_map/ppermute | solution.py:229
  21.3 24.1 %copy-start = (f32[2,32,1024]{2,1,0:T(8,128)S(1)}, f32[2,32,1024]{2,1,0:T(8,128)}, u32[]{:S(2)}) copy-start(f32[2,32,1024]{2,1,0:T(8,128)} %estimate_ref.1) | copy-start | bytes 786436
  25.3 2.9 %collective-permute-start.8 = (bf16[8,16,1024]{2,1,0:T(8,128)(2,1)S(1)}, bf16[8,16,1024]{2,1,0:T(8,128)(2,1)S(1)}, u32[]{:S(2)}, u32[]{:S(2)}) collective-permute-start(bf16[8,16,1024]{2,1,0:T(8,128)(2,1)S(1)} %get-tuple-element.34), channel_id=1, source_target_pairs={{0,4},{4,0},{8,12},{12,8},{16,20},{20,16},{24,28},{28,24},{1,5},{5... | collective-permute-start | bytes 786440 | tf_op jit(solution)/shard_map/ppermute | solution.py:229
  26.2 5.7 %collective-permute-start.12 = (bf16[4,16,1024]{2,1,0:T(8,128)(2,1)S(1)}, bf16[4,16,1024]{2,1,0:T(8,128)(2,1)S(1)}, u32[]{:S(2)}, u32[]{:S(2)}) collective-permute-start(bf16[4,16,1024]{2,1,0:T(8,128)(2,1)S(1)} %get-tuple-element.42), channel_id=1, source_target_pairs={{4,8},{8,4},{12,16},{16,12},{20,24},{24,20},{0,1},{28,29},{5,9},{9... | collective-permute-start | bytes 393224 | tf_op jit(solution)/shard_map/ppermute | solution.py:226
  26.2 14.9 %collective-permute-start.13 = (bf16[4,16,1024]{2,1,0:T(8,128)(2,1)S(1)}, bf16[4,16,1024]{2,1,0:T(8,128)(2,1)S(1)}, u32[]{:S(2)}, u32[]{:S(2)}) collective-permute-start(bf16[4,16,1024]{2,1,0:T(8,128)(2,1)S(1)} %get-tuple-element.46), channel_id=1, source_target_pairs={{4,8},{8,4},{12,16},{16,12},{20,24},{24,20},{0,1},{28,29},{5,9},{9... | collective-permute-start | bytes 393224 | tf_op jit(solution)/shard_map/ppermute | solution.py:226
  28.3 6.7 %collective-permute-start.10 = (bf16[2,16,1024]{2,1,0:T(8,128)(2,1)S(1)}, bf16[2,16,1024]{2,1,0:T(8,128)(2,1)S(1)}, u32[]{:S(2)}, u32[]{:S(2)}) collective-permute-start(bf16[2,16,1024]{2,1,0:T(8,128)(2,1)S(1)} %get-tuple-element.37), channel_id=1, source_target_pairs={{0,2},{1,3},{2,0},{3,1},{4,6},{5,7},{6,4},{7,5},{8,10},{9,11},{10,... | collective-permute-start | bytes 196616 | tf_op jit(solution)/shard_map/ppermute | solution.py:219
  29.8 11.2 %collective-permute-start.11 = (bf16[2,16,1024]{2,1,0:T(8,128)(2,1)S(1)}, bf16[2,16,1024]{2,1,0:T(8,128)(2,1)S(1)}, u32[]{:S(2)}, u32[]{:S(2)}) collective-permute-start(bf16[2,16,1024]{2,1,0:T(8,128)(2,1)S(1)} %get-tuple-element.38), channel_id=1, source_target_pairs={{0,3},{1,2},{2,1},{3,0},{4,7},{5,6},{6,5},{7,4},{8,11},{9,10},{10,... | collective-permute-start | bytes 196616 | tf_op jit(solution)/shard_map/ppermute | solution.py:219
  31.3 11.9 %collective-permute-start.9 = (bf16[2,16,1024]{2,1,0:T(8,128)(2,1)S(1)}, bf16[2,16,1024]{2,1,0:T(8,128)(2,1)S(1)}, u32[]{:S(2)}, u32[]{:S(2)}) collective-permute-start(bf16[2,16,1024]{2,1,0:T(8,128)(2,1)S(1)} %get-tuple-element.36), channel_id=1, source_target_pairs={{0,1},{1,0},{2,3},{3,2},{4,5},{5,4},{6,7},{7,6},{8,9},{9,8},{10,11... | collective-permute-start | bytes 196616 | tf_op jit(solution)/shard_map/ppermute | solution.py:219
  31.9 9.4 %collective-permute-start.15 = (bf16[2,16,1024]{2,1,0:T(8,128)(2,1)S(1)}, bf16[2,16,1024]{2,1,0:T(8,128)(2,1)S(1)}, u32[]{:S(2)}, u32[]{:S(2)}) collective-permute-start(bf16[2,16,1024]{2,1,0:T(8,128)(2,1)S(1)} %get-tuple-element.43), channel_id=1, source_target_pairs={{0,2},{1,3},{2,0},{3,1},{4,6},{5,7},{6,4},{7,5},{8,10},{9,11},{10,... | collective-permute-start | bytes 196616 | tf_op jit(solution)/shard_map/ppermute | solution.py:219
  35.0 8.3 %collective-permute-start.16 = (bf16[2,16,1024]{2,1,0:T(8,128)(2,1)S(1)}, bf16[2,16,1024]{2,1,0:T(8,128)(2,1)S(1)}, u32[]{:S(2)}, u32[]{:S(2)}) collective-permute-start(bf16[2,16,1024]{2,1,0:T(8,128)(2,1)S(1)} %get-tuple-element.44), channel_id=1, source_target_pairs={{0,3},{1,2},{2,1},{3,0},{4,7},{5,6},{6,5},{7,4},{8,11},{9,10},{10,... | collective-permute-start | bytes 196616 | tf_op jit(solution)/shard_map/ppermute | solution.py:219
  41.1 4.3 %collective-permute-start.14 = (bf16[2,16,1024]{2,1,0:T(8,128)(2,1)S(1)}, bf16[2,16,1024]{2,1,0:T(8,128)(2,1)S(1)}, u32[]{:S(2)}, u32[]{:S(2)}) collective-permute-start(bf16[2,16,1024]{2,1,0:T(8,128)(2,1)S(1)} %get-tuple-element.48), channel_id=1, source_target_pairs={{0,1},{1,0},{2,3},{3,2},{4,5},{5,4},{6,7},{7,6},{8,9},{9,8},{10,11... | collective-permute-start | bytes 196616 | tf_op jit(solution)/shard_map/ppermute | solution.py:219
where the time goes:
time: 46.4 us; the launch traced here: 46.2 us
  starting transfers between devices  25.5 us (55%)
  waiting for transfers between devices  11.1 us (24%)
  Pallas kernels  6.88 us (15%)
  other arithmetic  1.86 us (4%)
  local copies, waits for them, and re-layouts  0.74 us (2%)
    ppermute x12, starting transfers between devices, across(): return lax.ppermute(array, 'depth', [(i, i ^ step) for i in range(depth)])  22.4 us
    ppermute x12, waiting for transfers between devices, across(): return lax.ppermute(array, 'depth', [(i, i ^ step) for i in range(depth)])  10.8 us
    pallas_call x1, Pallas kernels, shards(): call(functools.partial(main_kernel, planes, view_rows), (shape(halves, F3...  4.01 us
    ppermute x3, starting transfers between devices, beside(): return lax.ppermute(array, ('tile', 'depth'), pairs)  2.1 us
    pallas_call x1, Pallas kernels, shards(): call(functools.partial(matrices_kernel, planes, strip), (shape((rows, spa...  1.88 us
    convert_element_type x1, other arithmetic, shards(): own = estimate.astype(BF16)  1.05 us
    ppermute x2, starting transfers between devices, within(): return lax.ppermute(array, 'tile', [(i, i ^ 1) for i in range(tiles)])  0.95 us
  transfers between devices with their start and end apart: 17, of which 7 were waited for; matrix products, arithmetic and copies ran while one was open for 3% of the time, Pallas kernels for 4%

commit v1 on v0

--- a/solution.py
+++ b/solution.py
@@ -130,7 +130,9 @@
         for n, first in enumerate(starts):
             part = blurred[n * group : (n + 1) * group]
             seen = views_ref[rows, first : first + WIDE].astype(F32)
-            correction = jnp.where(inside, seen / part - 1.0, 0.0)
+            inverse = pl.reciprocal(part, approx=True)
+            inverse = inverse * (2.0 - part * inverse)
+            correction = jnp.where(inside, seen * inverse - 1.0, 0.0)
             back_ref[rows, LANES + first : LANES + first + WIDE] = correction.astype(BF16)
         backward = jnp.dot(windows(back_ref, rows), tb_ref[view], preferred_element_type=F32)
         for n, first in enumerate(starts):
@@ -218,11 +220,14 @@
     def across(array, step):
         return lax.ppermute(array, "depth", [(i, i ^ step) for i in range(depth)])
 
-    def beside(array):
+    def beside(array, along_depth):
         pairs = []
         for d in range(depth):
-            pairs += [(i * depth + d, (i - 1 + 2 * (i % 2)) * depth + d) for i in range(1, tiles - 1)]
-            pairs += [(i * depth + d, i * depth + (d ^ 1)) for i in (0, tiles - 1)]
+            for i in range(tiles):
+                j, e = (i - 1 + 2 * (i % 2)) % tiles, d
+                if along_depth and i in (0, tiles - 1):
+                    j, e = i, d ^ 1
+                pairs.append((i * depth + d, j * depth + e))
         return lax.ppermute(array, ("tile", "depth"), pairs)
 
     def within(array):
@@ -231,8 +236,10 @@
     own = estimate.astype(BF16)
     early, late = own[:, :HALO], own[:, HALO:]
     outer_own, inner_own = jnp.where(odd == 1, late, early), jnp.where(odd == 1, early, late)
-    outer = jnp.concatenate([outer_own] + [across(outer_own, step) for step in range(1, depth)], axis=0)
-    other_chip = beside(outer)
+    outer = [outer_own] + [across(outer_own, step) for step in range(1, depth)]
+    inner_own, _ = lax.optimization_barrier((inner_own, outer[-1]))
+    outer = jnp.concatenate(outer, axis=0)
+    other_chip = beside(outer, True)
     inner = jnp.concatenate([inner_own] + [across(inner_own, step) for step in range(1, depth)], axis=0)
     other_core = within(inner)
     w, wt, tf, tb = call(
@@ -268,10 +275,10 @@
         )(core, other)
         return totals, [across(total, step) if step else total for step, total in zip(steps, totals)]
 
-    far_edge = beside(far_edge)
+    far_edge = beside(far_edge, False)
     totals, sums = joined(core, within(to_core), 0)
     totals, far = joined(far, far_edge, depth // 2, totals)
-    sums += joined(near, beside(near_edge), 0, [totals, sums[2:]])[1] + far
+    sums += joined(near, beside(near_edge, False), 0, [totals, sums[2:]])[1] + far
     return call(
         update_kernel,
         shape(estimate.shape, F32),

time: 46.4 us -> 45.5 us (0.981)
  waiting for transfers between devices: 11.1 us -> 8.66 us
  starting transfers between devices: 25.5 us -> 27 us
    ppermute x12, waiting for transfers between devices: 10.8 us -> 8.65 us  [across(): return lax.ppermute(array, 'depth', [(i, i ^ step) for i in range(depth)])]
    ppermute x3, starting transfers between devices: 2.1 us -> 4.17 us  [beside(): return lax.ppermute(array, ('tile', 'depth'), pairs)]
  transfers between devices with their start and end apart: 17 -> 17, of which waited for: 7 -> 7; matrix products, arithmetic and copies ran while one was open for 3% -> 3% of each run, Pallas kernels for 4% -> 5%
where the time goes in v1:
time: 45.5 us; the launch traced here: 45.3 us
  starting transfers between devices  27 us (59%)
  waiting for transfers between devices  8.66 us (19%)
  Pallas kernels  6.9 us (15%)
  other arithmetic  1.83 us (4%)
  local copies, waits for them, and re-layouts  0.77 us (2%)
    ppermute x12, starting transfers between devices, across(): return lax.ppermute(array, 'depth', [(i, i ^ step) for i in range(depth)])  22.2 us
    ppermute x12, waiting for transfers between devices, across(): return lax.ppermute(array, 'depth', [(i, i ^ step) for i in range(depth)])  8.65 us
    ppermute x3, starting transfers between devices, beside(): return lax.ppermute(array, ('tile', 'depth'), pairs)  4.17 us
    pallas_call x1, Pallas kernels, shards(): call(functools.partial(main_kernel, planes, view_rows), (shape(halves, F3...  4.03 us
    pallas_call x1, Pallas kernels, shards(): call(functools.partial(matrices_kernel, planes, strip), (shape((rows, spa...  1.88 us
    convert_element_type x1, other arithmetic, shards(): own = estimate.astype(BF16)  1.05 us
  transfers between devices with their start and end apart: 17, of which 7 were waited for; matrix products, arithmetic and copies ran while one was open for 3% of the time, Pallas kernels for 5%

profile of v1, /device:TPU:0, one launch (start us, length us, event | category | flops | bytes accessed | tf_op | source)
XLA Modules:
  0.0 45.3 jit_solution(7707219137478059618)
XLA Ops:
  0.0 0.0 copy-start.1
  0.0 1.1 %convert_element_type.4 = bf16[2,32,1024]{2,1,0:T(8,128)(2,1)S(1)} convert(f32[2,32,1024]{2,1,0:T(8,128)} %estimate_ref.1) | non-fusion elementwise | flops 65536 | bytes 393216 | tf_op jit(solution)/shard_map/convert_element_type | solution.py:236
  1.1 5.1 %collective-permute-start.2 = (bf16[2,16,1024]{2,1,0:T(8,128)(2,1)S(1)}, bf16[2,16,1024]{2,1,0:T(8,128)(2,1)S(1)}, u32[]{:S(2)}, u32[]{:S(2)}) collective-permute-start(bf16[2,16,1024]{2,1,0:T(8,128)(2,1)S(1)} %get-tuple-element.52), channel_id=1, source_target_pairs={{0,3},{1,2},{2,1},{3,0},{4,7},{5,6},{6,5},{7,4},{8,11},{9,10},{10,... | collective-permute-start | bytes 196616 | tf_op jit(solution)/shard_map/ppermute | solution.py:221
  6.2 0.0 collective-permute-start.1
  6.2 0.6 %collective-permute-start = (bf16[2,16,1024]{2,1,0:T(8,128)(2,1)S(1)}, bf16[2,16,1024]{2,1,0:T(8,128)(2,1)S(1)}, u32[]{:S(2)}, u32[]{:S(2)}) collective-permute-start(bf16[2,16,1024]{2,1,0:T(8,128)(2,1)S(1)} %get-tuple-element.52), channel_id=1, source_target_pairs={{0,1},{1,0},{2,3},{3,2},{4,5},{5,4},{6,7},{7,6},{8,9},{9,8},{10,11... | collective-permute-start | bytes 196616 | tf_op jit(solution)/shard_map/ppermute | solution.py:221
  6.8 1.9 %collective-permute-done.2 = bf16[2,16,1024]{2,1,0:T(8,128)(2,1)S(1)} collective-permute-done((bf16[2,16,1024]{2,1,0:T(8,128)(2,1)S(1)}, bf16[2,16,1024]{2,1,0:T(8,128)(2,1)S(1)}, u32[]{:S(2)}, u32[]{:S(2)}) %collective-permute-start.2) | collective-permute-done | bytes 65568 | tf_op jit(solution)/shard_map/ppermute | solution.py:221
  8.8 4.2 %collective-permute-start.6 = (bf16[2,16,1024]{2,1,0:T(8,128)(2,1)S(1)}, bf16[2,16,1024]{2,1,0:T(8,128)(2,1)S(1)}, u32[]{:S(2)}, u32[]{:S(2)}) collective-permute-start(bf16[2,16,1024]{2,1,0:T(8,128)(2,1)S(1)} %get-tuple-element.28), channel_id=1, source_target_pairs={{0,3},{1,2},{2,1},{3,0},{4,7},{5,6},{6,5},{7,4},{8,11},{9,10},{10,... | collective-permute-start | bytes 196616 | tf_op jit(solution)/shard_map/ppermute | solution.py:221
  13.0 0.0 collective-permute-start.5
  13.0 0.6 %collective-permute-start.4 = (bf16[2,16,1024]{2,1,0:T(8,128)(2,1)S(1)}, bf16[2,16,1024]{2,1,0:T(8,128)(2,1)S(1)}, u32[]{:S(2)}, u32[]{:S(2)}) collective-permute-start(bf16[2,16,1024]{2,1,0:T(8,128)(2,1)S(1)} %get-tuple-element.28), channel_id=1, source_target_pairs={{0,1},{1,0},{2,3},{3,2},{4,5},{5,4},{6,7},{7,6},{8,9},{9,8},{10,11... | collective-permute-start | bytes 196616 | tf_op jit(solution)/shard_map/ppermute | solution.py:221
  13.5 0.0 collective-permute-done.1
  13.5 0.0 collective-permute-done
  13.6 1.5 %collective-permute-start.3 = (bf16[8,16,1024]{2,1,0:T(8,128)(2,1)S(1)}, bf16[8,16,1024]{2,1,0:T(8,128)(2,1)S(1)}, u32[]{:S(2)}, u32[]{:S(2)}) collective-permute-start(bf16[8,16,1024]{2,1,0:T(8,128)(2,1)S(1)} %pad_maximum_fusion.refs_1_), channel_id=1, source_target_pairs={{0,1},{4,8},{8,4},{12,16},{16,12},{20,24},{24,20},{28,29},{1,0},{5... | collective-permute-start | bytes 786440 | tf_op jit(solution)/shard_map/ppermute | solution.py:231
  15.1 2.1 %collective-permute-done.4 = bf16[2,16,1024]{2,1,0:T(8,128)(2,1)S(1)} collective-permute-done((bf16[2,16,1024]{2,1,0:T(8,128)(2,1)S(1)}, bf16[2,16,1024]{2,1,0:T(8,128)(2,1)S(1)}, u32[]{:S(2)}, u32[]{:S(2)}) %collective-permute-start.4) | collective-permute-done | bytes 65568 | tf_op jit(solution)/shard_map/ppermute | solution.py:221
  17.3 1.1 %collective-permute-done.5 = bf16[2,16,1024]{2,1,0:T(8,128)(2,1)S(1)} collective-permute-done((bf16[2,16,1024]{2,1,0:T(8,128)(2,1)S(1)}, bf16[2,16,1024]{2,1,0:T(8,128)(2,1)S(1)}, u32[]{:S(2)}, u32[]{:S(2)}) %collective-permute-start.5) | collective-permute-done | bytes 65568 | tf_op jit(solution)/shard_map/ppermute | solution.py:221
  18.4 0.0 collective-permute-done.6
  18.4 0.1 collective-permute-start.7
  18.5 0.7 %concatenate.9.device_ref.info_ref = s32[12]{0:T(128)S(1)} concatenate(s32[1]{0:T(128)} %bitcast, s32[1]{0:T(128)} %bitcast.1, s32[1]{0:T(128)} %bitcast.2, s32[1]{0:T(128)} %bitcast.3, s32[8]{0:T(128)} %param.11), dimensions={0} | concatenate | bytes 96 | tf_op jit(solution)/shard_map/concatenate | solution.py:217
  19.3 0.7 %pad_maximum_fusion.1.kernels_ref = f32[3,8,31]{2,1,0:T(8,128)S(1)} fusion(f32[1,8,31]{2,1,0:T(8,128)} %bitcast.9, f32[1,8,31]{2,1,0:T(8,128)} %bitcast.10, f32[1,8,31]{2,1,0:T(8,128)} %bitcast.11), kind=kLoop, calls=%fused_computation.3 | loop fusion | flops 1488 | bytes 5952 | tf_op jit(solution)/shard_map/stack | solution.py:250
  20.0 1.9 %shard_map.64 = (bf16[512,512]{1,0:T(8,128)(2,1)S(1)}, bf16[512,512]{1,0:T(8,128)(2,1)S(1)}, bf16[8,512,256]{2,1,0:T(8,128)(2,1)S(1)}, bf16[8,512,256]{2,1,0:T(8,128)(2,1)S(1)}) custom-call(s32[12]{0:T(128)S(1)} %concatenate.9.device_ref.info_ref, f32[3,8,31]{2,1,0:T(8,128)S(1)} %pad_maximum_fusion.1.kernels_ref), custom_call_target="tpu_custom_call" | custom-call | flops 100000000 | bytes 5242880 | tf_op jit(solution)/shard_map/pallas_call | solution.py:245
  21.9 0.0 collective-permute-done.3.refs_0_
  21.9 0.0 collective-permute-done.7.refs_3_
  21.9 0.0 copy-done.1
  21.9 0.0 copy-start
  21.9 4.0 %shard_map.65 = (f32[8,16,1024]{2,1,0:T(8,128)S(1)}, bf16[8,16,1024]{2,1,0:T(8,128)(2,1)S(1)}, f32[4,16,1024]{2,1,0:T(8,128)S(1)}, f32[4,16,1024]{2,1,0:T(8,128)...) custom-call(s32[12]{0:T(128)S(1)} %concatenate.9.device_ref.info_ref, ...), custom_call_target="tpu_custom_call" | custom-call | flops 2000000000 | bytes 10485760 | tf_op jit(solution)/shard_map/pallas_call | solution.py:253
  25.9 0.5 %collective-permute-start.8 = (bf16[8,16,1024]{2,1,0:T(8,128)(2,1)S(1)}, bf16[8,16,1024]{2,1,0:T(8,128)(2,1)S(1)}, u32[]{:S(2)}, u32[]{:S(2)}) collective-permute-start(bf16[8,16,1024]{2,1,0:T(8,128)(2,1)S(1)} %get-tuple-element.36), channel_id=1, source_target_pairs={{0,4},{4,0},{8,12},{12,8},{16,20},{20,16},{24,28},{28,24},{1,5},{5... | collective-permute-start | bytes 786440 | tf_op jit(solution)/shard_map/ppermute | solution.py:234
  26.5 2.5 %collective-permute-start.12 = (bf16[4,16,1024]{2,1,0:T(8,128)(2,1)S(1)}, bf16[4,16,1024]{2,1,0:T(8,128)(2,1)S(1)}, u32[]{:S(2)}, u32[]{:S(2)}) collective-permute-start(bf16[4,16,1024]{2,1,0:T(8,128)(2,1)S(1)} %get-tuple-element.44), channel_id=1, source_target_pairs={{0,28},{4,8},{8,4},{12,16},{16,12},{20,24},{24,20},{28,0},{1,29},{... | collective-permute-start | bytes 393224 | tf_op jit(solution)/shard_map/ppermute | solution.py:231
  29.0 0.1 collective-permute-start.13
  29.1 0.0 collective-permute-done.8.other_ref
  29.1 0.1 shard_map.66
  29.2 2.2 %collective-permute-start.10 = (bf16[2,16,1024]{2,1,0:T(8,128)(2,1)S(1)}, bf16[2,16,1024]{2,1,0:T(8,128)(2,1)S(1)}, u32[]{:S(2)}, u32[]{:S(2)}) collective-permute-start(bf16[2,16,1024]{2,1,0:T(8,128)(2,1)S(1)} %get-tuple-element.39), channel_id=1, source_target_pairs={{0,2},{1,3},{2,0},{3,1},{4,6},{5,7},{6,4},{7,5},{8,10},{9,11},{10,... | collective-permute-start | bytes 196616 | tf_op jit(solution)/shard_map/ppermute | solution.py:221
  31.4 2.2 %collective-permute-start.11 = (bf16[2,16,1024]{2,1,0:T(8,128)(2,1)S(1)}, bf16[2,16,1024]{2,1,0:T(8,128)(2,1)S(1)}, u32[]{:S(2)}, u32[]{:S(2)}) collective-permute-start(bf16[2,16,1024]{2,1,0:T(8,128)(2,1)S(1)} %get-tuple-element.40), channel_id=1, source_target_pairs={{0,3},{1,2},{2,1},{3,0},{4,7},{5,6},{6,5},{7,4},{8,11},{9,10},{10,... | collective-permute-start | bytes 196616 | tf_op jit(solution)/shard_map/ppermute | solution.py:221
  33.6 0.0 collective-permute-start.9
  33.6 0.0 collective-permute-done.12.other_ref
  33.7 2.3 %collective-permute-start.15 = (bf16[2,16,1024]{2,1,0:T(8,128)(2,1)S(1)}, bf16[2,16,1024]{2,1,0:T(8,128)(2,1)S(1)}, u32[]{:S(2)}, u32[]{:S(2)}) collective-permute-start(bf16[2,16,1024]{2,1,0:T(8,128)(2,1)S(1)} %get-tuple-element.45), channel_id=1, source_target_pairs={{0,2},{1,3},{2,0},{3,1},{4,6},{5,7},{6,4},{7,5},{8,10},{9,11},{10,... | collective-permute-start | bytes 196616 | tf_op jit(solution)/shard_map/ppermute | solution.py:221
  35.9 0.2 collective-permute-done.10.refs_2_
  36.2 3.9 %collective-permute-start.16 = (bf16[2,16,1024]{2,1,0:T(8,128)(2,1)S(1)}, bf16[2,16,1024]{2,1,0:T(8,128)(2,1)S(1)}, u32[]{:S(2)}, u32[]{:S(2)}) collective-permute-start(bf16[2,16,1024]{2,1,0:T(8,128)(2,1)S(1)} %get-tuple-element.46), channel_id=1, source_target_pairs={{0,3},{1,2},{2,1},{3,0},{4,7},{5,6},{6,5},{7,4},{8,11},{9,10},{10,... | collective-permute-start | bytes 196616 | tf_op jit(solution)/shard_map/ppermute | solution.py:221
  40.0 0.0 collective-permute-done.11.refs_3_
  40.1 0.0 collective-permute-done.13.other_ref
  40.1 1.1 %collective-permute-start.14 = (bf16[2,16,1024]{2,1,0:T(8,128)(2,1)S(1)}, bf16[2,16,1024]{2,1,0:T(8,128)(2,1)S(1)}, u32[]{:S(2)}, u32[]{:S(2)}) collective-permute-start(bf16[2,16,1024]{2,1,0:T(8,128)(2,1)S(1)} %get-tuple-element.50), channel_id=1, source_target_pairs={{0,1},{1,0},{2,3},{3,2},{4,5},{5,4},{6,7},{7,6},{8,9},{9,8},{10,11... | collective-permute-start | bytes 196616 | tf_op jit(solution)/shard_map/ppermute | solution.py:221
  41.2 1.1 %collective-permute-done.15.refs_6_ = bf16[2,16,1024]{2,1,0:T(8,128)(2,1)S(1)} collective-permute-done((bf16[2,16,1024]{2,1,0:T(8,128)(2,1)S(1)}, bf16[2,16,1024]{2,1,0:T(8,128)(2,1)S(1)}, u32[]{:S(2)}, u32[]{:S(2)}) %collective-permute-start.15) | collective-permute-done | bytes 65568 | tf_op jit(solution)/shard_map/ppermute | solution.py:221
  42.3 0.5 %collective-permute-done.16.refs_7_ = bf16[2,16,1024]{2,1,0:T(8,128)(2,1)S(1)} collective-permute-done((bf16[2,16,1024]{2,1,0:T(8,128)(2,1)S(1)}, bf16[2,16,1024]{2,1,0:T(8,128)(2,1)S(1)}, u32[]{:S(2)}, u32[]{:S(2)}) %collective-permute-start.16) | collective-permute-done | bytes 65568 | tf_op jit(solution)/shard_map/ppermute | solution.py:221
  42.8 0.0 collective-permute-done.9.refs_1_
  42.8 1.6 %collective-permute-done.14.refs_5_ = bf16[2,16,1024]{2,1,0:T(8,128)(2,1)S(1)} collective-permute-done((bf16[2,16,1024]{2,1,0:T(8,128)(2,1)S(1)}, bf16[2,16,1024]{2,1,0:T(8,128)(2,1)S(1)}, u32[]{:S(2)}, u32[]{:S(2)}) %collective-permute-start.14) | collective-permute-done | bytes 65568 | tf_op jit(solution)/shard_map/ppermute | solution.py:221
  44.4 0.0 copy-done
  44.4 0.8 %shard_map.69 = f32[2,32,1024]{2,1,0:T(8,128)} custom-call(f32[2,32,1024]{2,1,0:T(8,128)S(1)} %copy-done, f32[32,128]{1,0:T(8,128)S(1)} %get-tuple-element.33.scale_ref, s32[16,128]{1,0:T(8,128)S(1)} %get-tuple-element.34.odd_ref, f32[2,16,1024]{2,1,0:T(8,128)S(1)} %get-tuple-element.37.refs_0_, bf16[2,16,1024]{2,1,0:T(8,128)(2,1)S(1)} %collective-permute-done.9.refs_1_, ...), custom_call_target="tpu_custom_call" | custom-call | flops 1000000 | bytes 1048576 | tf_op jit(solution)/shard_map/pallas_call | solution.py:282
  (8 shorter events, 0.2 us)
Async XLA Ops:
  0.0 21.9 %copy-start.1 = (bf16[8,2,32,1024]{3,2,1,0:T(8,128)(2,1)S(1)}, bf16[8,2,32,1024]{3,2,1,0:T(8,128)(2,1)}, u32[]{:S(2)}) copy-start(bf16[8,2,32,1024]{3,2,1,0:T(8,128)(2,1)} %param.7) | copy-start | bytes 3145732
  1.1 7.7 %collective-permute-start.2 = (bf16[2,16,1024]{2,1,0:T(8,128)(2,1)S(1)}, bf16[2,16,1024]{2,1,0:T(8,128)(2,1)S(1)}, u32[]{:S(2)}, u32[]{:S(2)}) collective-permute-start(bf16[2,16,1024]{2,1,0:T(8,128)(2,1)S(1)} %get-tuple-element.52), channel_id=1, source_target_pairs={{0,3},{1,2},{2,1},{3,0},{4,7},{5,6},{6,5},{7,4},{8,11},{9,10},{10,... | collective-permute-start | bytes 196616 | tf_op jit(solution)/shard_map/ppermute | solution.py:221
  6.2 7.4 %collective-permute-start.1 = (bf16[2,16,1024]{2,1,0:T(8,128)(2,1)S(1)}, bf16[2,16,1024]{2,1,0:T(8,128)(2,1)S(1)}, u32[]{:S(2)}, u32[]{:S(2)}) collective-permute-start(bf16[2,16,1024]{2,1,0:T(8,128)(2,1)S(1)} %get-tuple-element.52), channel_id=1, source_target_pairs={{0,2},{1,3},{2,0},{3,1},{4,6},{5,7},{6,4},{7,5},{8,10},{9,11},{10,... | collective-permute-start | bytes 196616 | tf_op jit(solution)/shard_map/ppermute | solution.py:221
  6.2 7.4 %collective-permute-start = (bf16[2,16,1024]{2,1,0:T(8,128)(2,1)S(1)}, bf16[2,16,1024]{2,1,0:T(8,128)(2,1)S(1)}, u32[]{:S(2)}, u32[]{:S(2)}) collective-permute-start(bf16[2,16,1024]{2,1,0:T(8,128)(2,1)S(1)} %get-tuple-element.52), channel_id=1, source_target_pairs={{0,1},{1,0},{2,3},{3,2},{4,5},{5,4},{6,7},{7,6},{8,9},{9,8},{10,11... | collective-permute-start | bytes 196616 | tf_op jit(solution)/shard_map/ppermute | solution.py:221
  8.8 9.6 %collective-permute-start.6 = (bf16[2,16,1024]{2,1,0:T(8,128)(2,1)S(1)}, bf16[2,16,1024]{2,1,0:T(8,128)(2,1)S(1)}, u32[]{:S(2)}, u32[]{:S(2)}) collective-permute-start(bf16[2,16,1024]{2,1,0:T(8,128)(2,1)S(1)} %get-tuple-element.28), channel_id=1, source_target_pairs={{0,3},{1,2},{2,1},{3,0},{4,7},{5,6},{6,5},{7,4},{8,11},{9,10},{10,... | collective-permute-start | bytes 196616 | tf_op jit(solution)/shard_map/ppermute | solution.py:221
  13.0 5.4 %collective-permute-start.5 = (bf16[2,16,1024]{2,1,0:T(8,128)(2,1)S(1)}, bf16[2,16,1024]{2,1,0:T(8,128)(2,1)S(1)}, u32[]{:S(2)}, u32[]{:S(2)}) collective-permute-start(bf16[2,16,1024]{2,1,0:T(8,128)(2,1)S(1)} %get-tuple-element.28), channel_id=1, source_target_pairs={{0,2},{1,3},{2,0},{3,1},{4,6},{5,7},{6,4},{7,5},{8,10},{9,11},{10,... | collective-permute-start | bytes 196616 | tf_op jit(solution)/shard_map/ppermute | solution.py:221
  13.0 4.3 %collective-permute-start.4 = (bf16[2,16,1024]{2,1,0:T(8,128)(2,1)S(1)}, bf16[2,16,1024]{2,1,0:T(8,128)(2,1)S(1)}, u32[]{:S(2)}, u32[]{:S(2)}) collective-permute-start(bf16[2,16,1024]{2,1,0:T(8,128)(2,1)S(1)} %get-tuple-element.28), channel_id=1, source_target_pairs={{0,1},{1,0},{2,3},{3,2},{4,5},{5,4},{6,7},{7,6},{8,9},{9,8},{10,11... | collective-permute-start | bytes 196616 | tf_op jit(solution)/shard_map/ppermute | solution.py:221
  13.6 8.3 %collective-permute-start.3 = (bf16[8,16,1024]{2,1,0:T(8,128)(2,1)S(1)}, bf16[8,16,1024]{2,1,0:T(8,128)(2,1)S(1)}, u32[]{:S(2)}, u32[]{:S(2)}) collective-permute-start(bf16[8,16,1024]{2,1,0:T(8,128)(2,1)S(1)} %pad_maximum_fusion.refs_1_), channel_id=1, source_target_pairs={{0,1},{4,8},{8,4},{12,16},{16,12},{20,24},{24,20},{28,29},{1,0},{5... | collective-permute-start | bytes 786440 | tf_op jit(solution)/shard_map/ppermute | solution.py:231
  18.4 3.5 %collective-permute-start.7 = (bf16[8,16,1024]{2,1,0:T(8,128)(2,1)S(1)}, bf16[8,16,1024]{2,1,0:T(8,128)(2,1)S(1)}, u32[]{:S(2)}, u32[]{:S(2)}) collective-permute-start(bf16[8,16,1024]{2,1,0:T(8,128)(2,1)S(1)} %constant_dynamic-update-slice_fusion.refs_2_), channel_id=1, source_target_pairs={{0,4},{4,0},{8,12},{12,8},{16,20},{20,16},{24,28},{28,24},{1,5},{5... | collective-permute-start | bytes 786440 | tf_op jit(solution)/shard_map/ppermute | solution.py:234
  21.9 22.5 %copy-start = (f32[2,32,1024]{2,1,0:T(8,128)S(1)}, f32[2,32,1024]{2,1,0:T(8,128)}, u32[]{:S(2)}) copy-start(f32[2,32,1024]{2,1,0:T(8,128)} %estimate_ref.1) | copy-start | bytes 786436
  25.9 3.2 %collective-permute-start.8 = (bf16[8,16,1024]{2,1,0:T(8,128)(2,1)S(1)}, bf16[8,16,1024]{2,1,0:T(8,128)(2,1)S(1)}, u32[]{:S(2)}, u32[]{:S(2)}) collective-permute-start(bf16[8,16,1024]{2,1,0:T(8,128)(2,1)S(1)} %get-tuple-element.36), channel_id=1, source_target_pairs={{0,4},{4,0},{8,12},{12,8},{16,20},{20,16},{24,28},{28,24},{1,5},{5... | collective-permute-start | bytes 786440 | tf_op jit(solution)/shard_map/ppermute | solution.py:234
  26.5 7.2 %collective-permute-start.12 = (bf16[4,16,1024]{2,1,0:T(8,128)(2,1)S(1)}, bf16[4,16,1024]{2,1,0:T(8,128)(2,1)S(1)}, u32[]{:S(2)}, u32[]{:S(2)}) collective-permute-start(bf16[4,16,1024]{2,1,0:T(8,128)(2,1)S(1)} %get-tuple-element.44), channel_id=1, source_target_pairs={{0,28},{4,8},{8,4},{12,16},{16,12},{20,24},{24,20},{28,0},{1,29},{... | collective-permute-start | bytes 393224 | tf_op jit(solution)/shard_map/ppermute | solution.py:231
  29.0 11.1 %collective-permute-start.13 = (bf16[4,16,1024]{2,1,0:T(8,128)(2,1)S(1)}, bf16[4,16,1024]{2,1,0:T(8,128)(2,1)S(1)}, u32[]{:S(2)}, u32[]{:S(2)}) collective-permute-start(bf16[4,16,1024]{2,1,0:T(8,128)(2,1)S(1)} %get-tuple-element.48), channel_id=1, source_target_pairs={{0,28},{4,8},{8,4},{12,16},{16,12},{20,24},{24,20},{28,0},{1,29},{... | collective-permute-start | bytes 393224 | tf_op jit(solution)/shard_map/ppermute | solution.py:231
  29.2 7.0 %collective-permute-start.10 = (bf16[2,16,1024]{2,1,0:T(8,128)(2,1)S(1)}, bf16[2,16,1024]{2,1,0:T(8,128)(2,1)S(1)}, u32[]{:S(2)}, u32[]{:S(2)}) collective-permute-start(bf16[2,16,1024]{2,1,0:T(8,128)(2,1)S(1)} %get-tuple-element.39), channel_id=1, source_target_pairs={{0,2},{1,3},{2,0},{3,1},{4,6},{5,7},{6,4},{7,5},{8,10},{9,11},{10,... | collective-permute-start | bytes 196616 | tf_op jit(solution)/shard_map/ppermute | solution.py:221
  31.4 8.6 %collective-permute-start.11 = (bf16[2,16,1024]{2,1,0:T(8,128)(2,1)S(1)}, bf16[2,16,1024]{2,1,0:T(8,128)(2,1)S(1)}, u32[]{:S(2)}, u32[]{:S(2)}) collective-permute-start(bf16[2,16,1024]{2,1,0:T(8,128)(2,1)S(1)} %get-tuple-element.40), channel_id=1, source_target_pairs={{0,3},{1,2},{2,1},{3,0},{4,7},{5,6},{6,5},{7,4},{8,11},{9,10},{10,... | collective-permute-start | bytes 196616 | tf_op jit(solution)/shard_map/ppermute | solution.py:221
  33.6 9.2 %collective-permute-start.9 = (bf16[2,16,1024]{2,1,0:T(8,128)(2,1)S(1)}, bf16[2,16,1024]{2,1,0:T(8,128)(2,1)S(1)}, u32[]{:S(2)}, u32[]{:S(2)}) collective-permute-start(bf16[2,16,1024]{2,1,0:T(8,128)(2,1)S(1)} %get-tuple-element.38), channel_id=1, source_target_pairs={{0,1},{1,0},{2,3},{3,2},{4,5},{5,4},{6,7},{7,6},{8,9},{9,8},{10,11... | collective-permute-start | bytes 196616 | tf_op jit(solution)/shard_map/ppermute | solution.py:221
  33.7 8.6 %collective-permute-start.15 = (bf16[2,16,1024]{2,1,0:T(8,128)(2,1)S(1)}, bf16[2,16,1024]{2,1,0:T(8,128)(2,1)S(1)}, u32[]{:S(2)}, u32[]{:S(2)}) collective-permute-start(bf16[2,16,1024]{2,1,0:T(8,128)(2,1)S(1)} %get-tuple-element.45), channel_id=1, source_target_pairs={{0,2},{1,3},{2,0},{3,1},{4,6},{5,7},{6,4},{7,5},{8,10},{9,11},{10,... | collective-permute-start | bytes 196616 | tf_op jit(solution)/shard_map/ppermute | solution.py:221
  36.2 6.7 %collective-permute-start.16 = (bf16[2,16,1024]{2,1,0:T(8,128)(2,1)S(1)}, bf16[2,16,1024]{2,1,0:T(8,128)(2,1)S(1)}, u32[]{:S(2)}, u32[]{:S(2)}) collective-permute-start(bf16[2,16,1024]{2,1,0:T(8,128)(2,1)S(1)} %get-tuple-element.46), channel_id=1, source_target_pairs={{0,3},{1,2},{2,1},{3,0},{4,7},{5,6},{6,5},{7,4},{8,11},{9,10},{10,... | collective-permute-start | bytes 196616 | tf_op jit(solution)/shard_map/ppermute | solution.py:221
  40.1 4.3 %collective-permute-start.14 = (bf16[2,16,1024]{2,1,0:T(8,128)(2,1)S(1)}, bf16[2,16,1024]{2,1,0:T(8,128)(2,1)S(1)}, u32[]{:S(2)}, u32[]{:S(2)}) collective-permute-start(bf16[2,16,1024]{2,1,0:T(8,128)(2,1)S(1)} %get-tuple-element.50), channel_id=1, source_target_pairs={{0,1},{1,0},{2,3},{3,2},{4,5},{5,4},{6,7},{7,6},{8,9},{9,8},{10,11... | collective-permute-start | bytes 196616 | tf_op jit(solution)/shard_map/ppermute | solution.py:221

commit v2 on v1

--- a/solution.py
+++ b/solution.py
@@ -240,14 +240,17 @@
     inner_own, _ = lax.optimization_barrier((inner_own, outer[-1]))
     outer = jnp.concatenate(outer, axis=0)
     other_chip = beside(outer, True)
-    inner = jnp.concatenate([inner_own] + [across(inner_own, step) for step in range(1, depth)], axis=0)
-    other_core = within(inner)
+    kernels, _ = lax.optimization_barrier((jnp.stack([kernel_x, kernel_y, kernel_z]), outer))
     w, wt, tf, tb = call(
         functools.partial(matrices_kernel, planes, strip),
         (shape((rows, span), BF16), shape((span, rows), BF16))
         + (shape((count, WIDE + 2 * LANES, WIDE), BF16),) * 2,
         1, 1, flops=10**8, moved=5 * 2**20,
-    )(info, jnp.stack([kernel_x, kernel_y, kernel_z]))
+    )(info, kernels)
+    inner = [inner_own] + [across(inner_own, step) for step in range(1, depth)]
+    inner, _ = lax.optimization_barrier((inner, w))
+    inner = jnp.concatenate(inner, axis=0)
+    other_core = within(inner)
     halves = (depth * planes, HALO, columns)
     quarter = (depth * planes // 2, HALO, columns)
     core, to_core, near, far, near_edge, far_edge, scale, odd_rows = call(
@@ -277,7 +280,7 @@
 
     far_edge = beside(far_edge, False)
     totals, sums = joined(core, within(to_core), 0)
-    totals, far = joined(far, far_edge, depth // 2, totals)
+    totals, far = joined(far, far_edge, depth // 2, [totals, sums[1]])
     sums += joined(near, beside(near_edge, False), 0, [totals, sums[2:]])[1] + far
     return call(
         update_kernel,

time: 45.5 us -> 46.3 us (1.018)
  waiting for transfers between devices: 8.66 us -> 9.77 us
  starting transfers between devices: 27 us -> 26.3 us
    ppermute x3, waiting for transfers between devices: 0.01 us -> 2.31 us  [beside(): return lax.ppermute(array, ('tile', 'depth'), pairs)]
    ppermute x12, waiting for transfers between devices: 8.65 us -> 7.46 us  [across(): return lax.ppermute(array, 'depth', [(i, i ^ step) for i in range(depth)])]
    ppermute x12, starting transfers between devices: 22.2 us -> 21.5 us  [across(): return lax.ppermute(array, 'depth', [(i, i ^ step) for i in range(depth)])]
  transfers between devices with their start and end apart: 17 -> 17, of which waited for: 7 -> 7; matrix products, arithmetic and copies ran while one was open for 3% -> 3% of each run, Pallas kernels for 5% -> 4%
where the time goes in v2:
time: 46.3 us; the launch traced here: 45.7 us
  starting transfers between devices  26.3 us (57%)
  waiting for transfers between devices  9.77 us (21%)
  Pallas kernels  6.92 us (15%)
  other arithmetic  1.83 us (4%)
  local copies, waits for them, and re-layouts  0.77 us (2%)
    ppermute x12, starting transfers between devices, across(): return lax.ppermute(array, 'depth', [(i, i ^ step) for i in range(depth)])  21.5 us
    ppermute x12, waiting for transfers between devices, across(): return lax.ppermute(array, 'depth', [(i, i ^ step) for i in range(depth)])  7.46 us
    ppermute x3, starting transfers between devices, beside(): return lax.ppermute(array, ('tile', 'depth'), pairs)  4.24 us
    pallas_call x1, Pallas kernels, shards(): call(functools.partial(main_kernel, planes, view_rows), (shape(halves, F3...  4.04 us
    ppermute x3, waiting for transfers between devices, beside(): return lax.ppermute(array, ('tile', 'depth'), pairs)  2.31 us
    pallas_call x1, Pallas kernels, shards(): call(functools.partial(matrices_kernel, planes, strip), (shape((rows, spa...  1.88 us
    convert_element_type x1, other arithmetic, shards(): own = estimate.astype(BF16)  1.05 us
  transfers between devices with their start and end apart: 17, of which 7 were waited for; matrix products, arithmetic and copies ran while one was open for 3% of the time, Pallas kernels for 4%

profile of v2, /device:TPU:0, one launch (start us, length us, event | category | flops | bytes accessed | tf_op | source)
XLA Modules:
  0.0 45.7 jit_solution(18006253185349992049)
XLA Ops:
  0.0 0.0 copy-start.1
  0.0 1.1 %convert_element_type.4 = bf16[2,32,1024]{2,1,0:T(8,128)(2,1)S(1)} convert(f32[2,32,1024]{2,1,0:T(8,128)} %estimate_ref.1) | non-fusion elementwise | flops 65536 | bytes 393216 | tf_op jit(solution)/shard_map/convert_element_type | solution.py:236
  1.1 5.1 %collective-permute-start.2 = (bf16[2,16,1024]{2,1,0:T(8,128)(2,1)S(1)}, bf16[2,16,1024]{2,1,0:T(8,128)(2,1)S(1)}, u32[]{:S(2)}, u32[]{:S(2)}) collective-permute-start(bf16[2,16,1024]{2,1,0:T(8,128)(2,1)S(1)} %get-tuple-element.62), channel_id=1, source_target_pairs={{0,3},{1,2},{2,1},{3,0},{4,7},{5,6},{6,5},{7,4},{8,11},{9,10},{10,... | collective-permute-start | bytes 196616 | tf_op jit(solution)/shard_map/ppermute | solution.py:221
  6.2 0.0 collective-permute-start.1
  6.2 0.6 %collective-permute-start = (bf16[2,16,1024]{2,1,0:T(8,128)(2,1)S(1)}, bf16[2,16,1024]{2,1,0:T(8,128)(2,1)S(1)}, u32[]{:S(2)}, u32[]{:S(2)}) collective-permute-start(bf16[2,16,1024]{2,1,0:T(8,128)(2,1)S(1)} %get-tuple-element.62), channel_id=1, source_target_pairs={{0,1},{1,0},{2,3},{3,2},{4,5},{5,4},{6,7},{7,6},{8,9},{9,8},{10,11... | collective-permute-start | bytes 196616 | tf_op jit(solution)/shard_map/ppermute | solution.py:221
  6.8 0.7 %concatenate.9.device_ref.info_ref = s32[12]{0:T(128)S(1)} concatenate(s32[1]{0:T(128)} %bitcast, s32[1]{0:T(128)} %bitcast.1, s32[1]{0:T(128)} %bitcast.2, s32[1]{0:T(128)} %bitcast.3, s32[8]{0:T(128)} %param.11), dimensions={0} | concatenate | bytes 96 | tf_op jit(solution)/shard_map/concatenate | solution.py:217
  7.6 0.7 %pad_maximum_fusion.1.kernels_ref = f32[3,8,31]{2,1,0:T(8,128)S(1)} fusion(f32[1,8,31]{2,1,0:T(8,128)} %bitcast.9, f32[1,8,31]{2,1,0:T(8,128)} %bitcast.10, f32[1,8,31]{2,1,0:T(8,128)} %bitcast.11), kind=kLoop, calls=%fused_computation.3 | loop fusion | flops 1488 | bytes 5952 | tf_op jit(solution)/shard_map/stack | solution.py:243
  8.3 0.5 %collective-permute-done.2 = bf16[2,16,1024]{2,1,0:T(8,128)(2,1)S(1)} collective-permute-done((bf16[2,16,1024]{2,1,0:T(8,128)(2,1)S(1)}, bf16[2,16,1024]{2,1,0:T(8,128)(2,1)S(1)}, u32[]{:S(2)}, u32[]{:S(2)}) %collective-permute-start.2) | collective-permute-done | bytes 65568 | tf_op jit(solution)/shard_map/ppermute | solution.py:221
  8.8 4.2 %collective-permute-start.6 = (bf16[2,16,1024]{2,1,0:T(8,128)(2,1)S(1)}, bf16[2,16,1024]{2,1,0:T(8,128)(2,1)S(1)}, u32[]{:S(2)}, u32[]{:S(2)}) collective-permute-start(bf16[2,16,1024]{2,1,0:T(8,128)(2,1)S(1)} %get-tuple-element.36), channel_id=1, source_target_pairs={{0,3},{1,2},{2,1},{3,0},{4,7},{5,6},{6,5},{7,4},{8,11},{9,10},{10,... | collective-permute-start | bytes 196616 | tf_op jit(solution)/shard_map/ppermute | solution.py:221
  13.0 0.0 collective-permute-start.5
  13.0 0.6 %collective-permute-start.4 = (bf16[2,16,1024]{2,1,0:T(8,128)(2,1)S(1)}, bf16[2,16,1024]{2,1,0:T(8,128)(2,1)S(1)}, u32[]{:S(2)}, u32[]{:S(2)}) collective-permute-start(bf16[2,16,1024]{2,1,0:T(8,128)(2,1)S(1)} %get-tuple-element.36), channel_id=1, source_target_pairs={{0,1},{1,0},{2,3},{3,2},{4,5},{5,4},{6,7},{7,6},{8,9},{9,8},{10,11... | collective-permute-start | bytes 196616 | tf_op jit(solution)/shard_map/ppermute | solution.py:221
  13.5 0.0 collective-permute-done.1
  13.5 0.0 collective-permute-done
  13.6 1.5 %collective-permute-start.3 = (bf16[8,16,1024]{2,1,0:T(8,128)(2,1)S(1)}, bf16[8,16,1024]{2,1,0:T(8,128)(2,1)S(1)}, u32[]{:S(2)}, u32[]{:S(2)}) collective-permute-start(bf16[8,16,1024]{2,1,0:T(8,128)(2,1)S(1)} %pad_maximum_fusion.refs_1_), channel_id=1, source_target_pairs={{0,1},{4,8},{8,4},{12,16},{16,12},{20,24},{24,20},{28,29},{1,0},{5... | collective-permute-start | bytes 786440 | tf_op jit(solution)/shard_map/ppermute | solution.py:231
  15.1 1.9 %shard_map.64 = (bf16[512,512]{1,0:T(8,128)(2,1)S(1)}, bf16[512,512]{1,0:T(8,128)(2,1)S(1)}, bf16[8,512,256]{2,1,0:T(8,128)(2,1)S(1)}, bf16[8,512,256]{2,1,0:T(8,128)(2,1)S(1)}) custom-call(s32[12]{0:T(128)S(1)} %concatenate.9.device_ref.info_ref, f32[3,8,31]{2,1,0:T(8,128)S(1)} %pad_maximum_fusion.1.kernels_ref), custom_call_target="tpu_custom_call" | custom-call | flops 100000000 | bytes 5242880 | tf_op jit(solution)/shard_map/pallas_call | solution.py:244
  17.0 0.0 collective-permute-done.6
  17.0 1.3 %collective-permute-done.5 = bf16[2,16,1024]{2,1,0:T(8,128)(2,1)S(1)} collective-permute-done((bf16[2,16,1024]{2,1,0:T(8,128)(2,1)S(1)}, bf16[2,16,1024]{2,1,0:T(8,128)(2,1)S(1)}, u32[]{:S(2)}, u32[]{:S(2)}) %collective-permute-start.5) | collective-permute-done | bytes 65568 | tf_op jit(solution)/shard_map/ppermute | solution.py:221
  18.3 0.0 collective-permute-done.4
  18.4 0.1 collective-permute-start.7
  18.5 2.3 %collective-permute-done.3.refs_0_ = bf16[8,16,1024]{2,1,0:T(8,128)(2,1)S(1)} collective-permute-done((bf16[8,16,1024]{2,1,0:T(8,128)(2,1)S(1)}, bf16[8,16,1024]{2,1,0:T(8,128)(2,1)S(1)}, u32[]{:S(2)}, u32[]{:S(2)}) %collective-permute-start.3) | collective-permute-done | bytes 262176 | tf_op jit(solution)/shard_map/ppermute | solution.py:231
  20.8 0.0 collective-permute-done.7.refs_3_
  20.8 0.0 copy-done.1
  20.8 0.0 copy-start
  20.8 4.0 %shard_map.65 = (f32[8,16,1024]{2,1,0:T(8,128)S(1)}, bf16[8,16,1024]{2,1,0:T(8,128)(2,1)S(1)}, f32[4,16,1024]{2,1,0:T(8,128)S(1)}, f32[4,16,1024]{2,1,0:T(8,128)...) custom-call(s32[12]{0:T(128)S(1)} %concatenate.9.device_ref.info_ref, ...), custom_call_target="tpu_custom_call" | custom-call | flops 2000000000 | bytes 10485760 | tf_op jit(solution)/shard_map/pallas_call | solution.py:256
  24.8 0.5 %collective-permute-start.8 = (bf16[8,16,1024]{2,1,0:T(8,128)(2,1)S(1)}, bf16[8,16,1024]{2,1,0:T(8,128)(2,1)S(1)}, u32[]{:S(2)}, u32[]{:S(2)}) collective-permute-start(bf16[8,16,1024]{2,1,0:T(8,128)(2,1)S(1)} %get-tuple-element.46), channel_id=1, source_target_pairs={{0,4},{4,0},{8,12},{12,8},{16,20},{20,16},{24,28},{28,24},{1,5},{5... | collective-permute-start | bytes 786440 | tf_op jit(solution)/shard_map/ppermute | solution.py:234
  25.3 2.7 %collective-permute-start.12 = (bf16[4,16,1024]{2,1,0:T(8,128)(2,1)S(1)}, bf16[4,16,1024]{2,1,0:T(8,128)(2,1)S(1)}, u32[]{:S(2)}, u32[]{:S(2)}) collective-permute-start(bf16[4,16,1024]{2,1,0:T(8,128)(2,1)S(1)} %get-tuple-element.54), channel_id=1, source_target_pairs={{0,28},{4,8},{8,4},{12,16},{16,12},{20,24},{24,20},{28,0},{1,29},{... | collective-permute-start | bytes 393224 | tf_op jit(solution)/shard_map/ppermute | solution.py:231
  28.0 0.0 collective-permute-start.13
  28.0 0.0 collective-permute-done.8.other_ref
  28.0 0.1 shard_map.66
  28.1 1.5 %collective-permute-start.9 = (bf16[2,16,1024]{2,1,0:T(8,128)(2,1)S(1)}, bf16[2,16,1024]{2,1,0:T(8,128)(2,1)S(1)}, u32[]{:S(2)}, u32[]{:S(2)}) collective-permute-start(bf16[2,16,1024]{2,1,0:T(8,128)(2,1)S(1)} %get-tuple-element.48), channel_id=1, source_target_pairs={{0,1},{1,0},{2,3},{3,2},{4,5},{5,4},{6,7},{7,6},{8,9},{9,8},{10,11... | collective-permute-start | bytes 196616 | tf_op jit(solution)/shard_map/ppermute | solution.py:221
  29.7 2.9 %collective-permute-start.10 = (bf16[2,16,1024]{2,1,0:T(8,128)(2,1)S(1)}, bf16[2,16,1024]{2,1,0:T(8,128)(2,1)S(1)}, u32[]{:S(2)}, u32[]{:S(2)}) collective-permute-start(bf16[2,16,1024]{2,1,0:T(8,128)(2,1)S(1)} %get-tuple-element.49), channel_id=1, source_target_pairs={{0,2},{1,3},{2,0},{3,1},{4,6},{5,7},{6,4},{7,5},{8,10},{9,11},{10,... | collective-permute-start | bytes 196616 | tf_op jit(solution)/shard_map/ppermute | solution.py:221
  32.6 0.0 collective-permute-start.11
  32.6 0.4 collective-permute-done.9.refs_1_
  33.0 0.0 collective-permute-done.12.other_ref
  33.0 1.9 %collective-permute-start.15 = (bf16[2,16,1024]{2,1,0:T(8,128)(2,1)S(1)}, bf16[2,16,1024]{2,1,0:T(8,128)(2,1)S(1)}, u32[]{:S(2)}, u32[]{:S(2)}) collective-permute-start(bf16[2,16,1024]{2,1,0:T(8,128)(2,1)S(1)} %get-tuple-element.55), channel_id=1, source_target_pairs={{0,2},{1,3},{2,0},{3,1},{4,6},{5,7},{6,4},{7,5},{8,10},{9,11},{10,... | collective-permute-start | bytes 196616 | tf_op jit(solution)/shard_map/ppermute | solution.py:221
  34.9 1.7 %collective-permute-start.16 = (bf16[2,16,1024]{2,1,0:T(8,128)(2,1)S(1)}, bf16[2,16,1024]{2,1,0:T(8,128)(2,1)S(1)}, u32[]{:S(2)}, u32[]{:S(2)}) collective-permute-start(bf16[2,16,1024]{2,1,0:T(8,128)(2,1)S(1)} %get-tuple-element.56), channel_id=1, source_target_pairs={{0,3},{1,2},{2,1},{3,0},{4,7},{5,6},{6,5},{7,4},{8,11},{9,10},{10,... | collective-permute-start | bytes 196616 | tf_op jit(solution)/shard_map/ppermute | solution.py:221
  36.6 3.0 %collective-permute-done.10.refs_2_ = bf16[2,16,1024]{2,1,0:T(8,128)(2,1)S(1)} collective-permute-done((bf16[2,16,1024]{2,1,0:T(8,128)(2,1)S(1)}, bf16[2,16,1024]{2,1,0:T(8,128)(2,1)S(1)}, u32[]{:S(2)}, u32[]{:S(2)}) %collective-permute-start.10) | collective-permute-done | bytes 65568 | tf_op jit(solution)/shard_map/ppermute | solution.py:221
  39.7 0.0 collective-permute-done.11.refs_3_
  39.7 0.0 collective-permute-done.13.other_ref
  39.7 2.9 %collective-permute-start.14 = (bf16[2,16,1024]{2,1,0:T(8,128)(2,1)S(1)}, bf16[2,16,1024]{2,1,0:T(8,128)(2,1)S(1)}, u32[]{:S(2)}, u32[]{:S(2)}) collective-permute-start(bf16[2,16,1024]{2,1,0:T(8,128)(2,1)S(1)} %get-tuple-element.60), channel_id=1, source_target_pairs={{0,1},{1,0},{2,3},{3,2},{4,5},{5,4},{6,7},{7,6},{8,9},{9,8},{10,11... | collective-permute-start | bytes 196616 | tf_op jit(solution)/shard_map/ppermute | solution.py:221
  42.6 0.2 collective-permute-done.15.refs_6_
  42.8 0.0 collective-permute-done.16.refs_7_
  42.8 2.0 %collective-permute-done.14.refs_5_ = bf16[2,16,1024]{2,1,0:T(8,128)(2,1)S(1)} collective-permute-done((bf16[2,16,1024]{2,1,0:T(8,128)(2,1)S(1)}, bf16[2,16,1024]{2,1,0:T(8,128)(2,1)S(1)}, u32[]{:S(2)}, u32[]{:S(2)}) %collective-permute-start.14) | collective-permute-done | bytes 65568 | tf_op jit(solution)/shard_map/ppermute | solution.py:221
  44.8 0.0 copy-done
  44.8 0.8 %shard_map.69 = f32[2,32,1024]{2,1,0:T(8,128)} custom-call(f32[2,32,1024]{2,1,0:T(8,128)S(1)} %copy-done, f32[32,128]{1,0:T(8,128)S(1)} %get-tuple-element.43.scale_ref, s32[16,128]{1,0:T(8,128)S(1)} %get-tuple-element.44.odd_ref, f32[2,16,1024]{2,1,0:T(8,128)S(1)} %get-tuple-element.47.refs_0_, bf16[2,16,1024]{2,1,0:T(8,128)(2,1)S(1)} %collective-permute-done.9.refs_1_, ...), custom_call_target="tpu_custom_call" | custom-call | flops 1000000 | bytes 1048576 | tf_op jit(solution)/shard_map/pallas_call | solution.py:285
  (8 shorter events, 0.2 us)
Async XLA Ops:
  0.0 20.8 %copy-start.1 = (bf16[8,2,32,1024]{3,2,1,0:T(8,128)(2,1)S(1)}, bf16[8,2,32,1024]{3,2,1,0:T(8,128)(2,1)}, u32[]{:S(2)}) copy-start(bf16[8,2,32,1024]{3,2,1,0:T(8,128)(2,1)} %param.7) | copy-start | bytes 3145732
  1.1 7.7 %collective-permute-start.2 = (bf16[2,16,1024]{2,1,0:T(8,128)(2,1)S(1)}, bf16[2,16,1024]{2,1,0:T(8,128)(2,1)S(1)}, u32[]{:S(2)}, u32[]{:S(2)}) collective-permute-start(bf16[2,16,1024]{2,1,0:T(8,128)(2,1)S(1)} %get-tuple-element.62), channel_id=1, source_target_pairs={{0,3},{1,2},{2,1},{3,0},{4,7},{5,6},{6,5},{7,4},{8,11},{9,10},{10,... | collective-permute-start | bytes 196616 | tf_op jit(solution)/shard_map/ppermute | solution.py:221
  6.2 7.4 %collective-permute-start.1 = (bf16[2,16,1024]{2,1,0:T(8,128)(2,1)S(1)}, bf16[2,16,1024]{2,1,0:T(8,128)(2,1)S(1)}, u32[]{:S(2)}, u32[]{:S(2)}) collective-permute-start(bf16[2,16,1024]{2,1,0:T(8,128)(2,1)S(1)} %get-tuple-element.62), channel_id=1, source_target_pairs={{0,2},{1,3},{2,0},{3,1},{4,6},{5,7},{6,4},{7,5},{8,10},{9,11},{10,... | collective-permute-start | bytes 196616 | tf_op jit(solution)/shard_map/ppermute | solution.py:221
  6.2 7.4 %collective-permute-start = (bf16[2,16,1024]{2,1,0:T(8,128)(2,1)S(1)}, bf16[2,16,1024]{2,1,0:T(8,128)(2,1)S(1)}, u32[]{:S(2)}, u32[]{:S(2)}) collective-permute-start(bf16[2,16,1024]{2,1,0:T(8,128)(2,1)S(1)} %get-tuple-element.62), channel_id=1, source_target_pairs={{0,1},{1,0},{2,3},{3,2},{4,5},{5,4},{6,7},{7,6},{8,9},{9,8},{10,11... | collective-permute-start | bytes 196616 | tf_op jit(solution)/shard_map/ppermute | solution.py:221
  8.8 8.2 %collective-permute-start.6 = (bf16[2,16,1024]{2,1,0:T(8,128)(2,1)S(1)}, bf16[2,16,1024]{2,1,0:T(8,128)(2,1)S(1)}, u32[]{:S(2)}, u32[]{:S(2)}) collective-permute-start(bf16[2,16,1024]{2,1,0:T(8,128)(2,1)S(1)} %get-tuple-element.36), channel_id=1, source_target_pairs={{0,3},{1,2},{2,1},{3,0},{4,7},{5,6},{6,5},{7,4},{8,11},{9,10},{10,... | collective-permute-start | bytes 196616 | tf_op jit(solution)/shard_map/ppermute | solution.py:221
  13.0 5.3 %collective-permute-start.5 = (bf16[2,16,1024]{2,1,0:T(8,128)(2,1)S(1)}, bf16[2,16,1024]{2,1,0:T(8,128)(2,1)S(1)}, u32[]{:S(2)}, u32[]{:S(2)}) collective-permute-start(bf16[2,16,1024]{2,1,0:T(8,128)(2,1)S(1)} %get-tuple-element.36), channel_id=1, source_target_pairs={{0,2},{1,3},{2,0},{3,1},{4,6},{5,7},{6,4},{7,5},{8,10},{9,11},{10,... | collective-permute-start | bytes 196616 | tf_op jit(solution)/shard_map/ppermute | solution.py:221
  13.0 5.3 %collective-permute-start.4 = (bf16[2,16,1024]{2,1,0:T(8,128)(2,1)S(1)}, bf16[2,16,1024]{2,1,0:T(8,128)(2,1)S(1)}, u32[]{:S(2)}, u32[]{:S(2)}) collective-permute-start(bf16[2,16,1024]{2,1,0:T(8,128)(2,1)S(1)} %get-tuple-element.36), channel_id=1, source_target_pairs={{0,1},{1,0},{2,3},{3,2},{4,5},{5,4},{6,7},{7,6},{8,9},{9,8},{10,11... | collective-permute-start | bytes 196616 | tf_op jit(solution)/shard_map/ppermute | solution.py:221
  13.6 7.2 %collective-permute-start.3 = (bf16[8,16,1024]{2,1,0:T(8,128)(2,1)S(1)}, bf16[8,16,1024]{2,1,0:T(8,128)(2,1)S(1)}, u32[]{:S(2)}, u32[]{:S(2)}) collective-permute-start(bf16[8,16,1024]{2,1,0:T(8,128)(2,1)S(1)} %pad_maximum_fusion.refs_1_), channel_id=1, source_target_pairs={{0,1},{4,8},{8,4},{12,16},{16,12},{20,24},{24,20},{28,29},{1,0},{5... | collective-permute-start | bytes 786440 | tf_op jit(solution)/shard_map/ppermute | solution.py:231
  18.4 2.4 %collective-permute-start.7 = (bf16[8,16,1024]{2,1,0:T(8,128)(2,1)S(1)}, bf16[8,16,1024]{2,1,0:T(8,128)(2,1)S(1)}, u32[]{:S(2)}, u32[]{:S(2)}) collective-permute-start(bf16[8,16,1024]{2,1,0:T(8,128)(2,1)S(1)} %constant_dynamic-update-slice_fusion.refs_2_), channel_id=1, source_target_pairs={{0,4},{4,0},{8,12},{12,8},{16,20},{20,16},{24,28},{28,24},{1,5},{5... | collective-permute-start | bytes 786440 | tf_op jit(solution)/shard_map/ppermute | solution.py:234
  20.8 24.1 %copy-start = (f32[2,32,1024]{2,1,0:T(8,128)S(1)}, f32[2,32,1024]{2,1,0:T(8,128)}, u32[]{:S(2)}) copy-start(f32[2,32,1024]{2,1,0:T(8,128)} %estimate_ref.1) | copy-start | bytes 786436
  24.8 3.2 %collective-permute-start.8 = (bf16[8,16,1024]{2,1,0:T(8,128)(2,1)S(1)}, bf16[8,16,1024]{2,1,0:T(8,128)(2,1)S(1)}, u32[]{:S(2)}, u32[]{:S(2)}) collective-permute-start(bf16[8,16,1024]{2,1,0:T(8,128)(2,1)S(1)} %get-tuple-element.46), channel_id=1, source_target_pairs={{0,4},{4,0},{8,12},{12,8},{16,20},{20,16},{24,28},{28,24},{1,5},{5... | collective-permute-start | bytes 786440 | tf_op jit(solution)/shard_map/ppermute | solution.py:234
  25.3 7.7 %collective-permute-start.12 = (bf16[4,16,1024]{2,1,0:T(8,128)(2,1)S(1)}, bf16[4,16,1024]{2,1,0:T(8,128)(2,1)S(1)}, u32[]{:S(2)}, u32[]{:S(2)}) collective-permute-start(bf16[4,16,1024]{2,1,0:T(8,128)(2,1)S(1)} %get-tuple-element.54), channel_id=1, source_target_pairs={{0,28},{4,8},{8,4},{12,16},{16,12},{20,24},{24,20},{28,0},{1,29},{... | collective-permute-start | bytes 393224 | tf_op jit(solution)/shard_map/ppermute | solution.py:231
  28.0 11.7 %collective-permute-start.13 = (bf16[4,16,1024]{2,1,0:T(8,128)(2,1)S(1)}, bf16[4,16,1024]{2,1,0:T(8,128)(2,1)S(1)}, u32[]{:S(2)}, u32[]{:S(2)}) collective-permute-start(bf16[4,16,1024]{2,1,0:T(8,128)(2,1)S(1)} %get-tuple-element.58), channel_id=1, source_target_pairs={{0,28},{4,8},{8,4},{12,16},{16,12},{20,24},{24,20},{28,0},{1,29},{... | collective-permute-start | bytes 393224 | tf_op jit(solution)/shard_map/ppermute | solution.py:231
  28.1 4.9 %collective-permute-start.9 = (bf16[2,16,1024]{2,1,0:T(8,128)(2,1)S(1)}, bf16[2,16,1024]{2,1,0:T(8,128)(2,1)S(1)}, u32[]{:S(2)}, u32[]{:S(2)}) collective-permute-start(bf16[2,16,1024]{2,1,0:T(8,128)(2,1)S(1)} %get-tuple-element.48), channel_id=1, source_target_pairs={{0,1},{1,0},{2,3},{3,2},{4,5},{5,4},{6,7},{7,6},{8,9},{9,8},{10,11... | collective-permute-start | bytes 196616 | tf_op jit(solution)/shard_map/ppermute | solution.py:221
  29.7 10.0 %collective-permute-start.10 = (bf16[2,16,1024]{2,1,0:T(8,128)(2,1)S(1)}, bf16[2,16,1024]{2,1,0:T(8,128)(2,1)S(1)}, u32[]{:S(2)}, u32[]{:S(2)}) collective-permute-start(bf16[2,16,1024]{2,1,0:T(8,128)(2,1)S(1)} %get-tuple-element.49), channel_id=1, source_target_pairs={{0,2},{1,3},{2,0},{3,1},{4,6},{5,7},{6,4},{7,5},{8,10},{9,11},{10,... | collective-permute-start | bytes 196616 | tf_op jit(solution)/shard_map/ppermute | solution.py:221
  32.6 7.1 %collective-permute-start.11 = (bf16[2,16,1024]{2,1,0:T(8,128)(2,1)S(1)}, bf16[2,16,1024]{2,1,0:T(8,128)(2,1)S(1)}, u32[]{:S(2)}, u32[]{:S(2)}) collective-permute-start(bf16[2,16,1024]{2,1,0:T(8,128)(2,1)S(1)} %get-tuple-element.50), channel_id=1, source_target_pairs={{0,3},{1,2},{2,1},{3,0},{4,7},{5,6},{6,5},{7,4},{8,11},{9,10},{10,... | collective-permute-start | bytes 196616 | tf_op jit(solution)/shard_map/ppermute | solution.py:221
  33.0 9.8 %collective-permute-start.15 = (bf16[2,16,1024]{2,1,0:T(8,128)(2,1)S(1)}, bf16[2,16,1024]{2,1,0:T(8,128)(2,1)S(1)}, u32[]{:S(2)}, u32[]{:S(2)}) collective-permute-start(bf16[2,16,1024]{2,1,0:T(8,128)(2,1)S(1)} %get-tuple-element.55), channel_id=1, source_target_pairs={{0,2},{1,3},{2,0},{3,1},{4,6},{5,7},{6,4},{7,5},{8,10},{9,11},{10,... | collective-permute-start | bytes 196616 | tf_op jit(solution)/shard_map/ppermute | solution.py:221
  34.9 7.9 %collective-permute-start.16 = (bf16[2,16,1024]{2,1,0:T(8,128)(2,1)S(1)}, bf16[2,16,1024]{2,1,0:T(8,128)(2,1)S(1)}, u32[]{:S(2)}, u32[]{:S(2)}) collective-permute-start(bf16[2,16,1024]{2,1,0:T(8,128)(2,1)S(1)} %get-tuple-element.56), channel_id=1, source_target_pairs={{0,3},{1,2},{2,1},{3,0},{4,7},{5,6},{6,5},{7,4},{8,11},{9,10},{10,... | collective-permute-start | bytes 196616 | tf_op jit(solution)/shard_map/ppermute | solution.py:221
  39.7 5.1 %collective-permute-start.14 = (bf16[2,16,1024]{2,1,0:T(8,128)(2,1)S(1)}, bf16[2,16,1024]{2,1,0:T(8,128)(2,1)S(1)}, u32[]{:S(2)}, u32[]{:S(2)}) collective-permute-start(bf16[2,16,1024]{2,1,0:T(8,128)(2,1)S(1)} %get-tuple-element.60), channel_id=1, source_target_pairs={{0,1},{1,0},{2,3},{3,2},{4,5},{5,4},{6,7},{7,6},{8,9},{9,8},{10,11... | collective-permute-start | bytes 196616 | tf_op jit(solution)/shard_map/ppermute | solution.py:221

commit v3 on v2

--- a/solution.py
+++ b/solution.py
@@ -281,7 +281,7 @@
     far_edge = beside(far_edge, False)
     totals, sums = joined(core, within(to_core), 0)
     totals, far = joined(far, far_edge, depth // 2, [totals, sums[1]])
-    sums += joined(near, beside(near_edge, False), 0, [totals, sums[2:]])[1] + far
+    sums += joined(near, beside(near_edge, False), 0, [totals, sums[2]])[1] + far
     return call(
         update_kernel,
         shape(estimate.shape, F32),

time: 46.3 us -> 44.8 us (0.968)
  starting transfers between devices: 26.3 us -> 23.6 us
  waiting for transfers between devices: 9.77 us -> 11.2 us
    ppermute x12, starting transfers between devices: 21.5 us -> 18.8 us  [across(): return lax.ppermute(array, 'depth', [(i, i ^ step) for i in range(depth)])]
    ppermute x12, waiting for transfers between devices: 7.46 us -> 8.9 us  [across(): return lax.ppermute(array, 'depth', [(i, i ^ step) for i in range(depth)])]
  transfers between devices with their start and end apart: 17 -> 17, of which waited for: 7 -> 7; matrix products, arithmetic and copies ran while one was open for 3% -> 3% of each run, Pallas kernels for 4% -> 5%
where the time goes in v3:
time: 44.8 us; the launch traced here: 44.4 us
  starting transfers between devices  23.6 us (53%)
  waiting for transfers between devices  11.2 us (25%)
  Pallas kernels  6.92 us (15%)
  other arithmetic  1.83 us (4%)
  local copies, waits for them, and re-layouts  0.77 us (2%)
    ppermute x12, starting transfers between devices, across(): return lax.ppermute(array, 'depth', [(i, i ^ step) for i in range(depth)])  18.8 us
    ppermute x12, waiting for transfers between devices, across(): return lax.ppermute(array, 'depth', [(i, i ^ step) for i in range(depth)])  8.9 us
    ppermute x3, starting transfers between devices, beside(): return lax.ppermute(array, ('tile', 'depth'), pairs)  4.24 us
    pallas_call x1, Pallas kernels, shards(): call(functools.partial(main_kernel, planes, view_rows), (shape(halves, F3...  4.04 us
    ppermute x3, waiting for transfers between devices, beside(): return lax.ppermute(array, ('tile', 'depth'), pairs)  2.31 us
    pallas_call x1, Pallas kernels, shards(): call(functools.partial(matrices_kernel, planes, strip), (shape((rows, spa...  1.88 us
    convert_element_type x1, other arithmetic, shards(): own = estimate.astype(BF16)  1.05 us
  transfers between devices with their start and end apart: 17, of which 7 were waited for; matrix products, arithmetic and copies ran while one was open for 3% of the time, Pallas kernels for 5%

profile of v3, /device:TPU:0, one launch (start us, length us, event | category | flops | bytes accessed | tf_op | source)
XLA Modules:
  0.0 44.4 jit_solution(3647220136242864090)
XLA Ops:
  0.0 0.0 copy-start.1
  0.0 1.1 %convert_element_type.4 = bf16[2,32,1024]{2,1,0:T(8,128)(2,1)S(1)} convert(f32[2,32,1024]{2,1,0:T(8,128)} %estimate_ref.1) | non-fusion elementwise | flops 65536 | bytes 393216 | tf_op jit(solution)/shard_map/convert_element_type | solution.py:236
  1.1 5.1 %collective-permute-start.2 = (bf16[2,16,1024]{2,1,0:T(8,128)(2,1)S(1)}, bf16[2,16,1024]{2,1,0:T(8,128)(2,1)S(1)}, u32[]{:S(2)}, u32[]{:S(2)}) collective-permute-start(bf16[2,16,1024]{2,1,0:T(8,128)(2,1)S(1)} %get-tuple-element.62), channel_id=1, source_target_pairs={{0,3},{1,2},{2,1},{3,0},{4,7},{5,6},{6,5},{7,4},{8,11},{9,10},{10,... | collective-permute-start | bytes 196616 | tf_op jit(solution)/shard_map/ppermute | solution.py:221
  6.2 0.0 collective-permute-start.1
  6.2 0.6 %collective-permute-start = (bf16[2,16,1024]{2,1,0:T(8,128)(2,1)S(1)}, bf16[2,16,1024]{2,1,0:T(8,128)(2,1)S(1)}, u32[]{:S(2)}, u32[]{:S(2)}) collective-permute-start(bf16[2,16,1024]{2,1,0:T(8,128)(2,1)S(1)} %get-tuple-element.62), channel_id=1, source_target_pairs={{0,1},{1,0},{2,3},{3,2},{4,5},{5,4},{6,7},{7,6},{8,9},{9,8},{10,11... | collective-permute-start | bytes 196616 | tf_op jit(solution)/shard_map/ppermute | solution.py:221
  6.8 0.7 %concatenate.9.device_ref.info_ref = s32[12]{0:T(128)S(1)} concatenate(s32[1]{0:T(128)} %bitcast, s32[1]{0:T(128)} %bitcast.1, s32[1]{0:T(128)} %bitcast.2, s32[1]{0:T(128)} %bitcast.3, s32[8]{0:T(128)} %param.11), dimensions={0} | concatenate | bytes 96 | tf_op jit(solution)/shard_map/concatenate | solution.py:217
  7.6 0.7 %pad_maximum_fusion.1.kernels_ref = f32[3,8,31]{2,1,0:T(8,128)S(1)} fusion(f32[1,8,31]{2,1,0:T(8,128)} %bitcast.9, f32[1,8,31]{2,1,0:T(8,128)} %bitcast.10, f32[1,8,31]{2,1,0:T(8,128)} %bitcast.11), kind=kLoop, calls=%fused_computation.3 | loop fusion | flops 1488 | bytes 5952 | tf_op jit(solution)/shard_map/stack | solution.py:243
  8.3 0.5 %collective-permute-done.2 = bf16[2,16,1024]{2,1,0:T(8,128)(2,1)S(1)} collective-permute-done((bf16[2,16,1024]{2,1,0:T(8,128)(2,1)S(1)}, bf16[2,16,1024]{2,1,0:T(8,128)(2,1)S(1)}, u32[]{:S(2)}, u32[]{:S(2)}) %collective-permute-start.2) | collective-permute-done | bytes 65568 | tf_op jit(solution)/shard_map/ppermute | solution.py:221
  8.8 4.2 %collective-permute-start.6 = (bf16[2,16,1024]{2,1,0:T(8,128)(2,1)S(1)}, bf16[2,16,1024]{2,1,0:T(8,128)(2,1)S(1)}, u32[]{:S(2)}, u32[]{:S(2)}) collective-permute-start(bf16[2,16,1024]{2,1,0:T(8,128)(2,1)S(1)} %get-tuple-element.36), channel_id=1, source_target_pairs={{0,3},{1,2},{2,1},{3,0},{4,7},{5,6},{6,5},{7,4},{8,11},{9,10},{10,... | collective-permute-start | bytes 196616 | tf_op jit(solution)/shard_map/ppermute | solution.py:221
  13.0 0.0 collective-permute-start.5
  13.0 0.6 %collective-permute-start.4 = (bf16[2,16,1024]{2,1,0:T(8,128)(2,1)S(1)}, bf16[2,16,1024]{2,1,0:T(8,128)(2,1)S(1)}, u32[]{:S(2)}, u32[]{:S(2)}) collective-permute-start(bf16[2,16,1024]{2,1,0:T(8,128)(2,1)S(1)} %get-tuple-element.36), channel_id=1, source_target_pairs={{0,1},{1,0},{2,3},{3,2},{4,5},{5,4},{6,7},{7,6},{8,9},{9,8},{10,11... | collective-permute-start | bytes 196616 | tf_op jit(solution)/shard_map/ppermute | solution.py:221
  13.5 0.0 collective-permute-done.1
  13.5 0.0 collective-permute-done
  13.6 1.5 %collective-permute-start.3 = (bf16[8,16,1024]{2,1,0:T(8,128)(2,1)S(1)}, bf16[8,16,1024]{2,1,0:T(8,128)(2,1)S(1)}, u32[]{:S(2)}, u32[]{:S(2)}) collective-permute-start(bf16[8,16,1024]{2,1,0:T(8,128)(2,1)S(1)} %pad_maximum_fusion.refs_1_), channel_id=1, source_target_pairs={{0,1},{4,8},{8,4},{12,16},{16,12},{20,24},{24,20},{28,29},{1,0},{5... | collective-permute-start | bytes 786440 | tf_op jit(solution)/shard_map/ppermute | solution.py:231
  15.1 1.9 %shard_map.64 = (bf16[512,512]{1,0:T(8,128)(2,1)S(1)}, bf16[512,512]{1,0:T(8,128)(2,1)S(1)}, bf16[8,512,256]{2,1,0:T(8,128)(2,1)S(1)}, bf16[8,512,256]{2,1,0:T(8,128)(2,1)S(1)}) custom-call(s32[12]{0:T(128)S(1)} %concatenate.9.device_ref.info_ref, f32[3,8,31]{2,1,0:T(8,128)S(1)} %pad_maximum_fusion.1.kernels_ref), custom_call_target="tpu_custom_call" | custom-call | flops 100000000 | bytes 5242880 | tf_op jit(solution)/shard_map/pallas_call | solution.py:244
  17.0 0.0 collective-permute-done.6
  17.0 1.3 %collective-permute-done.5 = bf16[2,16,1024]{2,1,0:T(8,128)(2,1)S(1)} collective-permute-done((bf16[2,16,1024]{2,1,0:T(8,128)(2,1)S(1)}, bf16[2,16,1024]{2,1,0:T(8,128)(2,1)S(1)}, u32[]{:S(2)}, u32[]{:S(2)}) %collective-permute-start.5) | collective-permute-done | bytes 65568 | tf_op jit(solution)/shard_map/ppermute | solution.py:221
  18.3 0.0 collective-permute-done.4
  18.4 0.1 collective-permute-start.7
  18.5 2.3 %collective-permute-done.3.refs_0_ = bf16[8,16,1024]{2,1,0:T(8,128)(2,1)S(1)} collective-permute-done((bf16[8,16,1024]{2,1,0:T(8,128)(2,1)S(1)}, bf16[8,16,1024]{2,1,0:T(8,128)(2,1)S(1)}, u32[]{:S(2)}, u32[]{:S(2)}) %collective-permute-start.3) | collective-permute-done | bytes 262176 | tf_op jit(solution)/shard_map/ppermute | solution.py:231
  20.8 0.0 collective-permute-done.7.refs_3_
  20.8 0.0 copy-done.1
  20.8 0.0 copy-start
  20.8 4.0 %shard_map.65 = (f32[8,16,1024]{2,1,0:T(8,128)S(1)}, bf16[8,16,1024]{2,1,0:T(8,128)(2,1)S(1)}, f32[4,16,1024]{2,1,0:T(8,128)S(1)}, f32[4,16,1024]{2,1,0:T(8,128)...) custom-call(s32[12]{0:T(128)S(1)} %concatenate.9.device_ref.info_ref, ...), custom_call_target="tpu_custom_call" | custom-call | flops 2000000000 | bytes 10485760 | tf_op jit(solution)/shard_map/pallas_call | solution.py:256
  24.8 0.5 %collective-permute-start.8 = (bf16[8,16,1024]{2,1,0:T(8,128)(2,1)S(1)}, bf16[8,16,1024]{2,1,0:T(8,128)(2,1)S(1)}, u32[]{:S(2)}, u32[]{:S(2)}) collective-permute-start(bf16[8,16,1024]{2,1,0:T(8,128)(2,1)S(1)} %get-tuple-element.46), channel_id=1, source_target_pairs={{0,4},{4,0},{8,12},{12,8},{16,20},{20,16},{24,28},{28,24},{1,5},{5... | collective-permute-start | bytes 786440 | tf_op jit(solution)/shard_map/ppermute | solution.py:234
  25.3 2.7 %collective-permute-start.12 = (bf16[4,16,1024]{2,1,0:T(8,128)(2,1)S(1)}, bf16[4,16,1024]{2,1,0:T(8,128)(2,1)S(1)}, u32[]{:S(2)}, u32[]{:S(2)}) collective-permute-start(bf16[4,16,1024]{2,1,0:T(8,128)(2,1)S(1)} %get-tuple-element.54), channel_id=1, source_target_pairs={{0,28},{4,8},{8,4},{12,16},{16,12},{20,24},{24,20},{28,0},{1,29},{... | collective-permute-start | bytes 393224 | tf_op jit(solution)/shard_map/ppermute | solution.py:231
  28.0 0.0 collective-permute-start.13
  28.0 0.0 collective-permute-done.8.other_ref
  28.0 0.1 shard_map.66
  28.1 1.5 %collective-permute-start.9 = (bf16[2,16,1024]{2,1,0:T(8,128)(2,1)S(1)}, bf16[2,16,1024]{2,1,0:T(8,128)(2,1)S(1)}, u32[]{:S(2)}, u32[]{:S(2)}) collective-permute-start(bf16[2,16,1024]{2,1,0:T(8,128)(2,1)S(1)} %get-tuple-element.48), channel_id=1, source_target_pairs={{0,1},{1,0},{2,3},{3,2},{4,5},{5,4},{6,7},{7,6},{8,9},{9,8},{10,11... | collective-permute-start | bytes 196616 | tf_op jit(solution)/shard_map/ppermute | solution.py:221
  29.7 2.9 %collective-permute-start.10 = (bf16[2,16,1024]{2,1,0:T(8,128)(2,1)S(1)}, bf16[2,16,1024]{2,1,0:T(8,128)(2,1)S(1)}, u32[]{:S(2)}, u32[]{:S(2)}) collective-permute-start(bf16[2,16,1024]{2,1,0:T(8,128)(2,1)S(1)} %get-tuple-element.49), channel_id=1, source_target_pairs={{0,2},{1,3},{2,0},{3,1},{4,6},{5,7},{6,4},{7,5},{8,10},{9,11},{10,... | collective-permute-start | bytes 196616 | tf_op jit(solution)/shard_map/ppermute | solution.py:221
  32.6 0.0 collective-permute-start.11
  32.6 0.4 collective-permute-done.9.refs_1_
  33.0 0.0 collective-permute-done.12.other_ref
  33.0 1.9 %collective-permute-start.15 = (bf16[2,16,1024]{2,1,0:T(8,128)(2,1)S(1)}, bf16[2,16,1024]{2,1,0:T(8,128)(2,1)S(1)}, u32[]{:S(2)}, u32[]{:S(2)}) collective-permute-start(bf16[2,16,1024]{2,1,0:T(8,128)(2,1)S(1)} %get-tuple-element.55), channel_id=1, source_target_pairs={{0,2},{1,3},{2,0},{3,1},{4,6},{5,7},{6,4},{7,5},{8,10},{9,11},{10,... | collective-permute-start | bytes 196616 | tf_op jit(solution)/shard_map/ppermute | solution.py:221
  34.9 1.7 %collective-permute-start.16 = (bf16[2,16,1024]{2,1,0:T(8,128)(2,1)S(1)}, bf16[2,16,1024]{2,1,0:T(8,128)(2,1)S(1)}, u32[]{:S(2)}, u32[]{:S(2)}) collective-permute-start(bf16[2,16,1024]{2,1,0:T(8,128)(2,1)S(1)} %get-tuple-element.56), channel_id=1, source_target_pairs={{0,3},{1,2},{2,1},{3,0},{4,7},{5,6},{6,5},{7,4},{8,11},{9,10},{10,... | collective-permute-start | bytes 196616 | tf_op jit(solution)/shard_map/ppermute | solution.py:221
  36.6 2.6 %collective-permute-done.10.refs_2_ = bf16[2,16,1024]{2,1,0:T(8,128)(2,1)S(1)} collective-permute-done((bf16[2,16,1024]{2,1,0:T(8,128)(2,1)S(1)}, bf16[2,16,1024]{2,1,0:T(8,128)(2,1)S(1)}, u32[]{:S(2)}, u32[]{:S(2)}) %collective-permute-start.10) | collective-permute-done | bytes 65568 | tf_op jit(solution)/shard_map/ppermute | solution.py:221
  39.2 0.0 collective-permute-done.13.other_ref
  39.2 0.2 collective-permute-start.14
  39.4 0.0 collective-permute-done.11.refs_3_
  39.4 3.4 %collective-permute-done.15.refs_6_ = bf16[2,16,1024]{2,1,0:T(8,128)(2,1)S(1)} collective-permute-done((bf16[2,16,1024]{2,1,0:T(8,128)(2,1)S(1)}, bf16[2,16,1024]{2,1,0:T(8,128)(2,1)S(1)}, u32[]{:S(2)}, u32[]{:S(2)}) %collective-permute-start.15) | collective-permute-done | bytes 65568 | tf_op jit(solution)/shard_map/ppermute | solution.py:221
  42.8 0.0 collective-permute-done.16.refs_7_
  42.8 0.7 %collective-permute-done.14.refs_5_ = bf16[2,16,1024]{2,1,0:T(8,128)(2,1)S(1)} collective-permute-done((bf16[2,16,1024]{2,1,0:T(8,128)(2,1)S(1)}, bf16[2,16,1024]{2,1,0:T(8,128)(2,1)S(1)}, u32[]{:S(2)}, u32[]{:S(2)}) %collective-permute-start.14) | collective-permute-done | bytes 65568 | tf_op jit(solution)/shard_map/ppermute | solution.py:221
  43.6 0.0 copy-done
  43.6 0.8 %shard_map.69 = f32[2,32,1024]{2,1,0:T(8,128)} custom-call(f32[2,32,1024]{2,1,0:T(8,128)S(1)} %copy-done, f32[32,128]{1,0:T(8,128)S(1)} %get-tuple-element.43.scale_ref, s32[16,128]{1,0:T(8,128)S(1)} %get-tuple-element.44.odd_ref, f32[2,16,1024]{2,1,0:T(8,128)S(1)} %get-tuple-element.47.refs_0_, bf16[2,16,1024]{2,1,0:T(8,128)(2,1)S(1)} %collective-permute-done.9.refs_1_, ...), custom_call_target="tpu_custom_call" | custom-call | flops 1000000 | bytes 1048576 | tf_op jit(solution)/shard_map/pallas_call | solution.py:285
  (8 shorter events, 0.2 us)
Async XLA Ops:
  0.0 20.8 %copy-start.1 = (bf16[8,2,32,1024]{3,2,1,0:T(8,128)(2,1)S(1)}, bf16[8,2,32,1024]{3,2,1,0:T(8,128)(2,1)}, u32[]{:S(2)}) copy-start(bf16[8,2,32,1024]{3,2,1,0:T(8,128)(2,1)} %param.7) | copy-start | bytes 3145732
  1.1 7.7 %collective-permute-start.2 = (bf16[2,16,1024]{2,1,0:T(8,128)(2,1)S(1)}, bf16[2,16,1024]{2,1,0:T(8,128)(2,1)S(1)}, u32[]{:S(2)}, u32[]{:S(2)}) collective-permute-start(bf16[2,16,1024]{2,1,0:T(8,128)(2,1)S(1)} %get-tuple-element.62), channel_id=1, source_target_pairs={{0,3},{1,2},{2,1},{3,0},{4,7},{5,6},{6,5},{7,4},{8,11},{9,10},{10,... | collective-permute-start | bytes 196616 | tf_op jit(solution)/shard_map/ppermute | solution.py:221
  6.2 7.4 %collective-permute-start.1 = (bf16[2,16,1024]{2,1,0:T(8,128)(2,1)S(1)}, bf16[2,16,1024]{2,1,0:T(8,128)(2,1)S(1)}, u32[]{:S(2)}, u32[]{:S(2)}) collective-permute-start(bf16[2,16,1024]{2,1,0:T(8,128)(2,1)S(1)} %get-tuple-element.62), channel_id=1, source_target_pairs={{0,2},{1,3},{2,0},{3,1},{4,6},{5,7},{6,4},{7,5},{8,10},{9,11},{10,... | collective-permute-start | bytes 196616 | tf_op jit(solution)/shard_map/ppermute | solution.py:221
  6.2 7.4 %collective-permute-start = (bf16[2,16,1024]{2,1,0:T(8,128)(2,1)S(1)}, bf16[2,16,1024]{2,1,0:T(8,128)(2,1)S(1)}, u32[]{:S(2)}, u32[]{:S(2)}) collective-permute-start(bf16[2,16,1024]{2,1,0:T(8,128)(2,1)S(1)} %get-tuple-element.62), channel_id=1, source_target_pairs={{0,1},{1,0},{2,3},{3,2},{4,5},{5,4},{6,7},{7,6},{8,9},{9,8},{10,11... | collective-permute-start | bytes 196616 | tf_op jit(solution)/shard_map/ppermute | solution.py:221
  8.8 8.2 %collective-permute-start.6 = (bf16[2,16,1024]{2,1,0:T(8,128)(2,1)S(1)}, bf16[2,16,1024]{2,1,0:T(8,128)(2,1)S(1)}, u32[]{:S(2)}, u32[]{:S(2)}) collective-permute-start(bf16[2,16,1024]{2,1,0:T(8,128)(2,1)S(1)} %get-tuple-element.36), channel_id=1, source_target_pairs={{0,3},{1,2},{2,1},{3,0},{4,7},{5,6},{6,5},{7,4},{8,11},{9,10},{10,... | collective-permute-start | bytes 196616 | tf_op jit(solution)/shard_map/ppermute | solution.py:221
  13.0 5.3 %collective-permute-start.5 = (bf16[2,16,1024]{2,1,0:T(8,128)(2,1)S(1)}, bf16[2,16,1024]{2,1,0:T(8,128)(2,1)S(1)}, u32[]{:S(2)}, u32[]{:S(2)}) collective-permute-start(bf16[2,16,1024]{2,1,0:T(8,128)(2,1)S(1)} %get-tuple-element.36), channel_id=1, source_target_pairs={{0,2},{1,3},{2,0},{3,1},{4,6},{5,7},{6,4},{7,5},{8,10},{9,11},{10,... | collective-permute-start | bytes 196616 | tf_op jit(solution)/shard_map/ppermute | solution.py:221
  13.0 5.3 %collective-permute-start.4 = (bf16[2,16,1024]{2,1,0:T(8,128)(2,1)S(1)}, bf16[2,16,1024]{2,1,0:T(8,128)(2,1)S(1)}, u32[]{:S(2)}, u32[]{:S(2)}) collective-permute-start(bf16[2,16,1024]{2,1,0:T(8,128)(2,1)S(1)} %get-tuple-element.36), channel_id=1, source_target_pairs={{0,1},{1,0},{2,3},{3,2},{4,5},{5,4},{6,7},{7,6},{8,9},{9,8},{10,11... | collective-permute-start | bytes 196616 | tf_op jit(solution)/shard_map/ppermute | solution.py:221
  13.6 7.2 %collective-permute-start.3 = (bf16[8,16,1024]{2,1,0:T(8,128)(2,1)S(1)}, bf16[8,16,1024]{2,1,0:T(8,128)(2,1)S(1)}, u32[]{:S(2)}, u32[]{:S(2)}) collective-permute-start(bf16[8,16,1024]{2,1,0:T(8,128)(2,1)S(1)} %pad_maximum_fusion.refs_1_), channel_id=1, source_target_pairs={{0,1},{4,8},{8,4},{12,16},{16,12},{20,24},{24,20},{28,29},{1,0},{5... | collective-permute-start | bytes 786440 | tf_op jit(solution)/shard_map/ppermute | solution.py:231
  18.4 2.4 %collective-permute-start.7 = (bf16[8,16,1024]{2,1,0:T(8,128)(2,1)S(1)}, bf16[8,16,1024]{2,1,0:T(8,128)(2,1)S(1)}, u32[]{:S(2)}, u32[]{:S(2)}) collective-permute-start(bf16[8,16,1024]{2,1,0:T(8,128)(2,1)S(1)} %constant_dynamic-update-slice_fusion.refs_2_), channel_id=1, source_target_pairs={{0,4},{4,0},{8,12},{12,8},{16,20},{20,16},{24,28},{28,24},{1,5},{5... | collective-permute-start | bytes 786440 | tf_op jit(solution)/shard_map/ppermute | solution.py:234
  20.8 22.8 %copy-start = (f32[2,32,1024]{2,1,0:T(8,128)S(1)}, f32[2,32,1024]{2,1,0:T(8,128)}, u32[]{:S(2)}) copy-start(f32[2,32,1024]{2,1,0:T(8,128)} %estimate_ref.1) | copy-start | bytes 786436
  24.8 3.2 %collective-permute-start.8 = (bf16[8,16,1024]{2,1,0:T(8,128)(2,1)S(1)}, bf16[8,16,1024]{2,1,0:T(8,128)(2,1)S(1)}, u32[]{:S(2)}, u32[]{:S(2)}) collective-permute-start(bf16[8,16,1024]{2,1,0:T(8,128)(2,1)S(1)} %get-tuple-element.46), channel_id=1, source_target_pairs={{0,4},{4,0},{8,12},{12,8},{16,20},{20,16},{24,28},{28,24},{1,5},{5... | collective-permute-start | bytes 786440 | tf_op jit(solution)/shard_map/ppermute | solution.py:234
  25.3 7.7 %collective-permute-start.12 = (bf16[4,16,1024]{2,1,0:T(8,128)(2,1)S(1)}, bf16[4,16,1024]{2,1,0:T(8,128)(2,1)S(1)}, u32[]{:S(2)}, u32[]{:S(2)}) collective-permute-start(bf16[4,16,1024]{2,1,0:T(8,128)(2,1)S(1)} %get-tuple-element.54), channel_id=1, source_target_pairs={{0,28},{4,8},{8,4},{12,16},{16,12},{20,24},{24,20},{28,0},{1,29},{... | collective-permute-start | bytes 393224 | tf_op jit(solution)/shard_map/ppermute | solution.py:231
  28.0 11.2 %collective-permute-start.13 = (bf16[4,16,1024]{2,1,0:T(8,128)(2,1)S(1)}, bf16[4,16,1024]{2,1,0:T(8,128)(2,1)S(1)}, u32[]{:S(2)}, u32[]{:S(2)}) collective-permute-start(bf16[4,16,1024]{2,1,0:T(8,128)(2,1)S(1)} %get-tuple-element.58), channel_id=1, source_target_pairs={{0,28},{4,8},{8,4},{12,16},{16,12},{20,24},{24,20},{28,0},{1,29},{... | collective-permute-start | bytes 393224 | tf_op jit(solution)/shard_map/ppermute | solution.py:231
  28.1 4.9 %collective-permute-start.9 = (bf16[2,16,1024]{2,1,0:T(8,128)(2,1)S(1)}, bf16[2,16,1024]{2,1,0:T(8,128)(2,1)S(1)}, u32[]{:S(2)}, u32[]{:S(2)}) collective-permute-start(bf16[2,16,1024]{2,1,0:T(8,128)(2,1)S(1)} %get-tuple-element.48), channel_id=1, source_target_pairs={{0,1},{1,0},{2,3},{3,2},{4,5},{5,4},{6,7},{7,6},{8,9},{9,8},{10,11... | collective-permute-start | bytes 196616 | tf_op jit(solution)/shard_map/ppermute | solution.py:221
  29.7 9.5 %collective-permute-start.10 = (bf16[2,16,1024]{2,1,0:T(8,128)(2,1)S(1)}, bf16[2,16,1024]{2,1,0:T(8,128)(2,1)S(1)}, u32[]{:S(2)}, u32[]{:S(2)}) collective-permute-start(bf16[2,16,1024]{2,1,0:T(8,128)(2,1)S(1)} %get-tuple-element.49), channel_id=1, source_target_pairs={{0,2},{1,3},{2,0},{3,1},{4,6},{5,7},{6,4},{7,5},{8,10},{9,11},{10,... | collective-permute-start | bytes 196616 | tf_op jit(solution)/shard_map/ppermute | solution.py:221
  32.6 6.9 %collective-permute-start.11 = (bf16[2,16,1024]{2,1,0:T(8,128)(2,1)S(1)}, bf16[2,16,1024]{2,1,0:T(8,128)(2,1)S(1)}, u32[]{:S(2)}, u32[]{:S(2)}) collective-permute-start(bf16[2,16,1024]{2,1,0:T(8,128)(2,1)S(1)} %get-tuple-element.50), channel_id=1, source_target_pairs={{0,3},{1,2},{2,1},{3,0},{4,7},{5,6},{6,5},{7,4},{8,11},{9,10},{10,... | collective-permute-start | bytes 196616 | tf_op jit(solution)/shard_map/ppermute | solution.py:221
  33.0 9.8 %collective-permute-start.15 = (bf16[2,16,1024]{2,1,0:T(8,128)(2,1)S(1)}, bf16[2,16,1024]{2,1,0:T(8,128)(2,1)S(1)}, u32[]{:S(2)}, u32[]{:S(2)}) collective-permute-start(bf16[2,16,1024]{2,1,0:T(8,128)(2,1)S(1)} %get-tuple-element.55), channel_id=1, source_target_pairs={{0,2},{1,3},{2,0},{3,1},{4,6},{5,7},{6,4},{7,5},{8,10},{9,11},{10,... | collective-permute-start | bytes 196616 | tf_op jit(solution)/shard_map/ppermute | solution.py:221
  34.9 7.9 %collective-permute-start.16 = (bf16[2,16,1024]{2,1,0:T(8,128)(2,1)S(1)}, bf16[2,16,1024]{2,1,0:T(8,128)(2,1)S(1)}, u32[]{:S(2)}, u32[]{:S(2)}) collective-permute-start(bf16[2,16,1024]{2,1,0:T(8,128)(2,1)S(1)} %get-tuple-element.56), channel_id=1, source_target_pairs={{0,3},{1,2},{2,1},{3,0},{4,7},{5,6},{6,5},{7,4},{8,11},{9,10},{10,... | collective-permute-start | bytes 196616 | tf_op jit(solution)/shard_map/ppermute | solution.py:221
  39.2 4.3 %collective-permute-start.14 = (bf16[2,16,1024]{2,1,0:T(8,128)(2,1)S(1)}, bf16[2,16,1024]{2,1,0:T(8,128)(2,1)S(1)}, u32[]{:S(2)}, u32[]{:S(2)}) collective-permute-start(bf16[2,16,1024]{2,1,0:T(8,128)(2,1)S(1)} %get-tuple-element.60), channel_id=1, source_target_pairs={{0,1},{1,0},{2,3},{3,2},{4,5},{5,4},{6,7},{7,6},{8,9},{9,8},{10,11... | collective-permute-start | bytes 196616 | tf_op jit(solution)/shard_map/ppermute | solution.py:221

commit v4 on v3

--- a/solution.py
+++ b/solution.py
@@ -237,18 +237,21 @@
     early, late = own[:, :HALO], own[:, HALO:]
     outer_own, inner_own = jnp.where(odd == 1, late, early), jnp.where(odd == 1, early, late)
     outer = [outer_own] + [across(outer_own, step) for step in range(1, depth)]
-    inner_own, _ = lax.optimization_barrier((inner_own, outer[-1]))
+    kernels = jnp.stack([kernel_x, kernel_y, kernel_z])
+    outer, *_ = lax.optimization_barrier((outer, kernels, info))
+    first, _ = lax.optimization_barrier((inner_own, outer[-1]))
     outer = jnp.concatenate(outer, axis=0)
     other_chip = beside(outer, True)
-    kernels, _ = lax.optimization_barrier((jnp.stack([kernel_x, kernel_y, kernel_z]), outer))
+    second, _ = lax.optimization_barrier((first, outer))
+    inner = [inner_own] + [across(second if step < depth - 1 else first, step) for step in range(1, depth)]
+    kernels, _ = lax.optimization_barrier((kernels, outer))
     w, wt, tf, tb = call(
         functools.partial(matrices_kernel, planes, strip),
         (shape((rows, span), BF16), shape((span, rows), BF16))
         + (shape((count, WIDE + 2 * LANES, WIDE), BF16),) * 2,
         1, 1, flops=10**8, moved=5 * 2**20,
     )(info, kernels)
-    inner = [inner_own] + [across(inner_own, step) for step in range(1, depth)]
-    inner, _ = lax.optimization_barrier((inner, w))
+    inner, _ = lax.optimization_barrier((inner, (w, other_chip)))
     inner = jnp.concatenate(inner, axis=0)
     other_core = within(inner)
     halves = (depth * planes, HALO, columns)

time: 44.8 us -> 47.7 us (1.065)
  waiting for transfers between devices: 11.2 us -> 16.2 us
  starting transfers between devices: 23.6 us -> 21.7 us
    ppermute x12, waiting for transfers between devices: 8.9 us -> 14.7 us  [across(): return lax.ppermute(array, 'depth', [(i, i ^ step) for i in range(depth)])]
    ppermute x3, waiting for transfers between devices: 2.31 us -> 0.01 us  [beside(): return lax.ppermute(array, ('tile', 'depth'), pairs)]
    ppermute x2, waiting for transfers between devices: 0.01 us -> 1.42 us  [within(): return lax.ppermute(array, 'tile', [(i, i ^ 1) for i in range(tiles)])]
    ppermute x12, starting transfers between devices: 18.8 us -> 17.6 us  [across(): return lax.ppermute(array, 'depth', [(i, i ^ step) for i in range(depth)])]
  transfers between devices with their start and end apart: 17 -> 17, of which waited for: 7 -> 9; matrix products, arithmetic and copies ran while one was open for 3% -> 3% of each run, Pallas kernels for 5% -> 4%
where the time goes in v4:
time: 47.7 us; the launch traced here: 47.5 us
  starting transfers between devices  21.7 us (45%)
  waiting for transfers between devices  16.2 us (34%)
  Pallas kernels  6.91 us (14%)
  other arithmetic  1.79 us (4%)
  local copies, waits for them, and re-layouts  0.79 us (2%)
    ppermute x12, starting transfers between devices, across(): return lax.ppermute(array, 'depth', [(i, i ^ step) for i in range(depth)])  17.6 us
    ppermute x12, waiting for transfers between devices, across(): return lax.ppermute(array, 'depth', [(i, i ^ step) for i in range(depth)])  14.7 us
    pallas_call x1, Pallas kernels, shards(): call(functools.partial(main_kernel, planes, view_rows), (shape(halves, F3...  4.03 us
    ppermute x3, starting transfers between devices, beside(): return lax.ppermute(array, ('tile', 'depth'), pairs)  3.78 us
    pallas_call x1, Pallas kernels, shards(): call(functools.partial(matrices_kernel, planes, strip), (shape((rows, spa...  1.88 us
    ppermute x2, waiting for transfers between devices, within(): return lax.ppermute(array, 'tile', [(i, i ^ 1) for i in range(tiles)])  1.42 us
    convert_element_type x1, other arithmetic, shards(): own = estimate.astype(BF16)  1.05 us
  transfers between devices with their start and end apart: 17, of which 9 were waited for; matrix products, arithmetic and copies ran while one was open for 3% of the time, Pallas kernels for 4%

profile of v4, /device:TPU:0, one launch (start us, length us, event | category | flops | bytes accessed | tf_op | source)
XLA Modules:
  0.0 47.5 jit_solution(13324729612142482199)
XLA Ops:
  0.0 0.0 copy-start.1
  0.0 1.1 %convert_element_type.4 = bf16[2,32,1024]{2,1,0:T(8,128)(2,1)S(1)} convert(f32[2,32,1024]{2,1,0:T(8,128)} %estimate_ref.1) | non-fusion elementwise | flops 65536 | bytes 393216 | tf_op jit(solution)/shard_map/convert_element_type | solution.py:236
  1.1 5.1 %collective-permute-start.2 = (bf16[2,16,1024]{2,1,0:T(8,128)(2,1)S(1)}, bf16[2,16,1024]{2,1,0:T(8,128)(2,1)S(1)}, u32[]{:S(2)}, u32[]{:S(2)}) collective-permute-start(bf16[2,16,1024]{2,1,0:T(8,128)(2,1)S(1)} %get-tuple-element.38), channel_id=1, source_target_pairs={{0,3},{1,2},{2,1},{3,0},{4,7},{5,6},{6,5},{7,4},{8,11},{9,10},{10,... | collective-permute-start | bytes 196616 | tf_op jit(solution)/shard_map/ppermute | solution.py:221
  6.2 0.0 collective-permute-start.1
  6.2 0.6 %collective-permute-start = (bf16[2,16,1024]{2,1,0:T(8,128)(2,1)S(1)}, bf16[2,16,1024]{2,1,0:T(8,128)(2,1)S(1)}, u32[]{:S(2)}, u32[]{:S(2)}) collective-permute-start(bf16[2,16,1024]{2,1,0:T(8,128)(2,1)S(1)} %get-tuple-element.38), channel_id=1, source_target_pairs={{0,1},{1,0},{2,3},{3,2},{4,5},{5,4},{6,7},{7,6},{8,9},{9,8},{10,11... | collective-permute-start | bytes 196616 | tf_op jit(solution)/shard_map/ppermute | solution.py:221
  6.8 0.7 %concatenate.9.device_ref.info_ref = s32[12]{0:T(128)S(1)} concatenate(s32[1]{0:T(128)} %bitcast, s32[1]{0:T(128)} %bitcast.1, s32[1]{0:T(128)} %bitcast.2, s32[1]{0:T(128)} %bitcast.3, s32[8]{0:T(128)} %param.11), dimensions={0} | concatenate | bytes 96 | tf_op jit(solution)/shard_map/concatenate | solution.py:217
  7.6 0.7 %pad_maximum_fusion.kernels_ref = f32[3,8,31]{2,1,0:T(8,128)S(1)} fusion(f32[1,8,31]{2,1,0:T(8,128)} %bitcast.9, f32[1,8,31]{2,1,0:T(8,128)} %bitcast.10, f32[1,8,31]{2,1,0:T(8,128)} %bitcast.11), kind=kLoop, calls=%fused_computation.10 | loop fusion | flops 1488 | bytes 5952 | tf_op jit(solution)/shard_map/stack | solution.py:240
  8.3 0.5 %collective-permute-done.2 = bf16[2,16,1024]{2,1,0:T(8,128)(2,1)S(1)} collective-permute-done((bf16[2,16,1024]{2,1,0:T(8,128)(2,1)S(1)}, bf16[2,16,1024]{2,1,0:T(8,128)(2,1)S(1)}, u32[]{:S(2)}, u32[]{:S(2)}) %collective-permute-start.2) | collective-permute-done | bytes 65568 | tf_op jit(solution)/shard_map/ppermute | solution.py:221
  8.8 3.0 %collective-permute-done.1 = bf16[2,16,1024]{2,1,0:T(8,128)(2,1)S(1)} collective-permute-done((bf16[2,16,1024]{2,1,0:T(8,128)(2,1)S(1)}, bf16[2,16,1024]{2,1,0:T(8,128)(2,1)S(1)}, u32[]{:S(2)}, u32[]{:S(2)}) %collective-permute-start.1) | collective-permute-done | bytes 65568 | tf_op jit(solution)/shard_map/ppermute | solution.py:221
  11.8 0.0 collective-permute-done
  11.9 1.1 %collective-permute-start.3 = (bf16[8,16,1024]{2,1,0:T(8,128)(2,1)S(1)}, bf16[8,16,1024]{2,1,0:T(8,128)(2,1)S(1)}, u32[]{:S(2)}, u32[]{:S(2)}) collective-permute-start(bf16[8,16,1024]{2,1,0:T(8,128)(2,1)S(1)} %constant_dynamic-update-slice_fusion.refs_1_), channel_id=1, source_target_pairs={{0,1},{4,8},{8,4},{12,16},{16,12},{20,24},{24,20},{28,29},{1,0},{5... | collective-permute-start | bytes 786440 | tf_op jit(solution)/shard_map/ppermute | solution.py:231
  13.0 2.0 %collective-permute-start.6 = (bf16[2,16,1024]{2,1,0:T(8,128)(2,1)S(1)}, bf16[2,16,1024]{2,1,0:T(8,128)(2,1)S(1)}, u32[]{:S(2)}, u32[]{:S(2)}) collective-permute-start(bf16[2,16,1024]{2,1,0:T(8,128)(2,1)S(1)} %get-tuple-element.46), channel_id=1, source_target_pairs={{0,3},{1,2},{2,1},{3,0},{4,7},{5,6},{6,5},{7,4},{8,11},{9,10},{10,... | collective-permute-start | bytes 196616 | tf_op jit(solution)/shard_map/ppermute | solution.py:221
  15.0 0.5 collective-permute-start.5
  15.4 2.0 %collective-permute-start.4 = (bf16[2,16,1024]{2,1,0:T(8,128)(2,1)S(1)}, bf16[2,16,1024]{2,1,0:T(8,128)(2,1)S(1)}, u32[]{:S(2)}, u32[]{:S(2)}) collective-permute-start(bf16[2,16,1024]{2,1,0:T(8,128)(2,1)S(1)} %get-tuple-element.46), channel_id=1, source_target_pairs={{0,1},{1,0},{2,3},{3,2},{4,5},{5,4},{6,7},{7,6},{8,9},{9,8},{10,11... | collective-permute-start | bytes 196616 | tf_op jit(solution)/shard_map/ppermute | solution.py:221
  17.4 1.9 %shard_map.64 = (bf16[512,512]{1,0:T(8,128)(2,1)S(1)}, bf16[512,512]{1,0:T(8,128)(2,1)S(1)}, bf16[8,512,256]{2,1,0:T(8,128)(2,1)S(1)}, bf16[8,512,256]{2,1,0:T(8,128)(2,1)S(1)}) custom-call(s32[12]{0:T(128)S(1)} %concatenate.9.device_ref.info_ref, f32[3,8,31]{2,1,0:T(8,128)S(1)} %pad_maximum_fusion.kernels_ref), custom_call_target="tpu_custom_call" | custom-call | flops 100000000 | bytes 5242880 | tf_op jit(solution)/shard_map/pallas_call | solution.py:248
  19.3 2.8 %collective-permute-done.6 = bf16[2,16,1024]{2,1,0:T(8,128)(2,1)S(1)} collective-permute-done((bf16[2,16,1024]{2,1,0:T(8,128)(2,1)S(1)}, bf16[2,16,1024]{2,1,0:T(8,128)(2,1)S(1)}, u32[]{:S(2)}, u32[]{:S(2)}) %collective-permute-start.6) | collective-permute-done | bytes 65568 | tf_op jit(solution)/shard_map/ppermute | solution.py:221
  22.1 0.8 %collective-permute-done.5 = bf16[2,16,1024]{2,1,0:T(8,128)(2,1)S(1)} collective-permute-done((bf16[2,16,1024]{2,1,0:T(8,128)(2,1)S(1)}, bf16[2,16,1024]{2,1,0:T(8,128)(2,1)S(1)}, u32[]{:S(2)}, u32[]{:S(2)}) %collective-permute-start.5) | collective-permute-done | bytes 65568 | tf_op jit(solution)/shard_map/ppermute | solution.py:221
  22.9 0.0 collective-permute-done.4
  22.9 0.0 collective-permute-done.3.refs_0_
  23.0 0.2 collective-permute-start.7
  23.1 1.4 %collective-permute-done.7.refs_3_ = bf16[8,16,1024]{2,1,0:T(8,128)(2,1)S(1)} collective-permute-done((bf16[8,16,1024]{2,1,0:T(8,128)(2,1)S(1)}, bf16[8,16,1024]{2,1,0:T(8,128)(2,1)S(1)}, u32[]{:S(2)}, u32[]{:S(2)}) %collective-permute-start.7) | collective-permute-done | bytes 262176 | tf_op jit(solution)/shard_map/ppermute | solution.py:234
  24.6 0.0 copy-done.1
  24.6 0.0 copy-start
  24.6 4.0 %shard_map.65 = (f32[8,16,1024]{2,1,0:T(8,128)S(1)}, bf16[8,16,1024]{2,1,0:T(8,128)(2,1)S(1)}, f32[4,16,1024]{2,1,0:T(8,128)S(1)}, f32[4,16,1024]{2,1,0:T(8,128)...) custom-call(s32[12]{0:T(128)S(1)} %concatenate.9.device_ref.info_ref, ...), custom_call_target="tpu_custom_call" | custom-call | flops 2000000000 | bytes 10485760 | tf_op jit(solution)/shard_map/pallas_call | solution.py:259
  28.6 0.2 collective-permute-start.8
  28.8 0.8 %collective-permute-start.12 = (bf16[4,16,1024]{2,1,0:T(8,128)(2,1)S(1)}, bf16[4,16,1024]{2,1,0:T(8,128)(2,1)S(1)}, u32[]{:S(2)}, u32[]{:S(2)}) collective-permute-start(bf16[4,16,1024]{2,1,0:T(8,128)(2,1)S(1)} %get-tuple-element.64), channel_id=1, source_target_pairs={{0,28},{4,8},{8,4},{12,16},{16,12},{20,24},{24,20},{28,0},{1,29},{... | collective-permute-start | bytes 393224 | tf_op jit(solution)/shard_map/ppermute | solution.py:231
  29.5 1.9 %collective-permute-start.13 = (bf16[4,16,1024]{2,1,0:T(8,128)(2,1)S(1)}, bf16[4,16,1024]{2,1,0:T(8,128)(2,1)S(1)}, u32[]{:S(2)}, u32[]{:S(2)}) collective-permute-start(bf16[4,16,1024]{2,1,0:T(8,128)(2,1)S(1)} %get-tuple-element.68), channel_id=1, source_target_pairs={{0,28},{4,8},{8,4},{12,16},{16,12},{20,24},{24,20},{28,0},{1,29},{... | collective-permute-start | bytes 393224 | tf_op jit(solution)/shard_map/ppermute | solution.py:231
  31.4 0.0 collective-permute-done.8.other_ref
  31.4 0.1 shard_map.66
  31.5 0.8 %collective-permute-start.9 = (bf16[2,16,1024]{2,1,0:T(8,128)(2,1)S(1)}, bf16[2,16,1024]{2,1,0:T(8,128)(2,1)S(1)}, u32[]{:S(2)}, u32[]{:S(2)}) collective-permute-start(bf16[2,16,1024]{2,1,0:T(8,128)(2,1)S(1)} %get-tuple-element.58), channel_id=1, source_target_pairs={{0,1},{1,0},{2,3},{3,2},{4,5},{5,4},{6,7},{7,6},{8,9},{9,8},{10,11... | collective-permute-start | bytes 196616 | tf_op jit(solution)/shard_map/ppermute | solution.py:221
  32.3 2.2 %collective-permute-start.10 = (bf16[2,16,1024]{2,1,0:T(8,128)(2,1)S(1)}, bf16[2,16,1024]{2,1,0:T(8,128)(2,1)S(1)}, u32[]{:S(2)}, u32[]{:S(2)}) collective-permute-start(bf16[2,16,1024]{2,1,0:T(8,128)(2,1)S(1)} %get-tuple-element.59), channel_id=1, source_target_pairs={{0,2},{1,3},{2,0},{3,1},{4,6},{5,7},{6,4},{7,5},{8,10},{9,11},{10,... | collective-permute-start | bytes 196616 | tf_op jit(solution)/shard_map/ppermute | solution.py:221
  34.5 1.5 %collective-permute-start.11 = (bf16[2,16,1024]{2,1,0:T(8,128)(2,1)S(1)}, bf16[2,16,1024]{2,1,0:T(8,128)(2,1)S(1)}, u32[]{:S(2)}, u32[]{:S(2)}) collective-permute-start(bf16[2,16,1024]{2,1,0:T(8,128)(2,1)S(1)} %get-tuple-element.60), channel_id=1, source_target_pairs={{0,3},{1,2},{2,1},{3,0},{4,7},{5,6},{6,5},{7,4},{8,11},{9,10},{10,... | collective-permute-start | bytes 196616 | tf_op jit(solution)/shard_map/ppermute | solution.py:221
  36.0 0.5 collective-permute-done.9.refs_1_
  36.4 0.0 collective-permute-done.12.other_ref
  36.5 1.4 %collective-permute-start.15 = (bf16[2,16,1024]{2,1,0:T(8,128)(2,1)S(1)}, bf16[2,16,1024]{2,1,0:T(8,128)(2,1)S(1)}, u32[]{:S(2)}, u32[]{:S(2)}) collective-permute-start(bf16[2,16,1024]{2,1,0:T(8,128)(2,1)S(1)} %get-tuple-element.65), channel_id=1, source_target_pairs={{0,2},{1,3},{2,0},{3,1},{4,6},{5,7},{6,4},{7,5},{8,10},{9,11},{10,... | collective-permute-start | bytes 196616 | tf_op jit(solution)/shard_map/ppermute | solution.py:221
  37.8 1.6 %collective-permute-start.16 = (bf16[2,16,1024]{2,1,0:T(8,128)(2,1)S(1)}, bf16[2,16,1024]{2,1,0:T(8,128)(2,1)S(1)}, u32[]{:S(2)}, u32[]{:S(2)}) collective-permute-start(bf16[2,16,1024]{2,1,0:T(8,128)(2,1)S(1)} %get-tuple-element.66), channel_id=1, source_target_pairs={{0,3},{1,2},{2,1},{3,0},{4,7},{5,6},{6,5},{7,4},{8,11},{9,10},{10,... | collective-permute-start | bytes 196616 | tf_op jit(solution)/shard_map/ppermute | solution.py:221
  39.4 2.9 %collective-permute-done.10.refs_2_ = bf16[2,16,1024]{2,1,0:T(8,128)(2,1)S(1)} collective-permute-done((bf16[2,16,1024]{2,1,0:T(8,128)(2,1)S(1)}, bf16[2,16,1024]{2,1,0:T(8,128)(2,1)S(1)}, u32[]{:S(2)}, u32[]{:S(2)}) %collective-permute-start.10) | collective-permute-done | bytes 65568 | tf_op jit(solution)/shard_map/ppermute | solution.py:221
  42.3 0.0 collective-permute-done.13.other_ref
  42.3 0.1 collective-permute-start.14
  42.4 0.0 collective-permute-done.11.refs_3_
  42.4 3.2 %collective-permute-done.15.refs_6_ = bf16[2,16,1024]{2,1,0:T(8,128)(2,1)S(1)} collective-permute-done((bf16[2,16,1024]{2,1,0:T(8,128)(2,1)S(1)}, bf16[2,16,1024]{2,1,0:T(8,128)(2,1)S(1)}, u32[]{:S(2)}, u32[]{:S(2)}) %collective-permute-start.15) | collective-permute-done | bytes 65568 | tf_op jit(solution)/shard_map/ppermute | solution.py:221
  45.6 0.0 collective-permute-done.16.refs_7_
  45.6 1.0 %collective-permute-done.14.refs_5_ = bf16[2,16,1024]{2,1,0:T(8,128)(2,1)S(1)} collective-permute-done((bf16[2,16,1024]{2,1,0:T(8,128)(2,1)S(1)}, bf16[2,16,1024]{2,1,0:T(8,128)(2,1)S(1)}, u32[]{:S(2)}, u32[]{:S(2)}) %collective-permute-start.14) | collective-permute-done | bytes 65568 | tf_op jit(solution)/shard_map/ppermute | solution.py:221
  46.7 0.0 copy-done
  46.7 0.8 %shard_map.69 = f32[2,32,1024]{2,1,0:T(8,128)} custom-call(f32[2,32,1024]{2,1,0:T(8,128)S(1)} %copy-done, f32[32,128]{1,0:T(8,128)S(1)} %get-tuple-element.53.scale_ref, s32[16,128]{1,0:T(8,128)S(1)} %get-tuple-element.54.odd_ref, f32[2,16,1024]{2,1,0:T(8,128)S(1)} %get-tuple-element.57.refs_0_, bf16[2,16,1024]{2,1,0:T(8,128)(2,1)S(1)} %collective-permute-done.9.refs_1_, ...), custom_call_target="tpu_custom_call" | custom-call | flops 1000000 | bytes 1048576 | tf_op jit(solution)/shard_map/pallas_call | solution.py:288
  (11 shorter events, 0.1 us)
Async XLA Ops:
  0.0 24.6 %copy-start.1 = (bf16[8,2,32,1024]{3,2,1,0:T(8,128)(2,1)S(1)}, bf16[8,2,32,1024]{3,2,1,0:T(8,128)(2,1)}, u32[]{:S(2)}) copy-start(bf16[8,2,32,1024]{3,2,1,0:T(8,128)(2,1)} %param.7) | copy-start | bytes 3145732
  1.1 7.7 %collective-permute-start.2 = (bf16[2,16,1024]{2,1,0:T(8,128)(2,1)S(1)}, bf16[2,16,1024]{2,1,0:T(8,128)(2,1)S(1)}, u32[]{:S(2)}, u32[]{:S(2)}) collective-permute-start(bf16[2,16,1024]{2,1,0:T(8,128)(2,1)S(1)} %get-tuple-element.38), channel_id=1, source_target_pairs={{0,3},{1,2},{2,1},{3,0},{4,7},{5,6},{6,5},{7,4},{8,11},{9,10},{10,... | collective-permute-start | bytes 196616 | tf_op jit(solution)/shard_map/ppermute | solution.py:221
  6.2 5.6 %collective-permute-start.1 = (bf16[2,16,1024]{2,1,0:T(8,128)(2,1)S(1)}, bf16[2,16,1024]{2,1,0:T(8,128)(2,1)S(1)}, u32[]{:S(2)}, u32[]{:S(2)}) collective-permute-start(bf16[2,16,1024]{2,1,0:T(8,128)(2,1)S(1)} %get-tuple-element.38), channel_id=1, source_target_pairs={{0,2},{1,3},{2,0},{3,1},{4,6},{5,7},{6,4},{7,5},{8,10},{9,11},{10,... | collective-permute-start | bytes 196616 | tf_op jit(solution)/shard_map/ppermute | solution.py:221
  6.2 5.6 %collective-permute-start = (bf16[2,16,1024]{2,1,0:T(8,128)(2,1)S(1)}, bf16[2,16,1024]{2,1,0:T(8,128)(2,1)S(1)}, u32[]{:S(2)}, u32[]{:S(2)}) collective-permute-start(bf16[2,16,1024]{2,1,0:T(8,128)(2,1)S(1)} %get-tuple-element.38), channel_id=1, source_target_pairs={{0,1},{1,0},{2,3},{3,2},{4,5},{5,4},{6,7},{7,6},{8,9},{9,8},{10,11... | collective-permute-start | bytes 196616 | tf_op jit(solution)/shard_map/ppermute | solution.py:221
  11.9 11.0 %collective-permute-start.3 = (bf16[8,16,1024]{2,1,0:T(8,128)(2,1)S(1)}, bf16[8,16,1024]{2,1,0:T(8,128)(2,1)S(1)}, u32[]{:S(2)}, u32[]{:S(2)}) collective-permute-start(bf16[8,16,1024]{2,1,0:T(8,128)(2,1)S(1)} %constant_dynamic-update-slice_fusion.refs_1_), channel_id=1, source_target_pairs={{0,1},{4,8},{8,4},{12,16},{16,12},{20,24},{24,20},{28,29},{1,0},{5... | collective-permute-start | bytes 786440 | tf_op jit(solution)/shard_map/ppermute | solution.py:231
  13.0 9.1 %collective-permute-start.6 = (bf16[2,16,1024]{2,1,0:T(8,128)(2,1)S(1)}, bf16[2,16,1024]{2,1,0:T(8,128)(2,1)S(1)}, u32[]{:S(2)}, u32[]{:S(2)}) collective-permute-start(bf16[2,16,1024]{2,1,0:T(8,128)(2,1)S(1)} %get-tuple-element.46), channel_id=1, source_target_pairs={{0,3},{1,2},{2,1},{3,0},{4,7},{5,6},{6,5},{7,4},{8,11},{9,10},{10,... | collective-permute-start | bytes 196616 | tf_op jit(solution)/shard_map/ppermute | solution.py:221
  15.0 7.9 %collective-permute-start.5 = (bf16[2,16,1024]{2,1,0:T(8,128)(2,1)S(1)}, bf16[2,16,1024]{2,1,0:T(8,128)(2,1)S(1)}, u32[]{:S(2)}, u32[]{:S(2)}) collective-permute-start(bf16[2,16,1024]{2,1,0:T(8,128)(2,1)S(1)} %get-tuple-element.46), channel_id=1, source_target_pairs={{0,2},{1,3},{2,0},{3,1},{4,6},{5,7},{6,4},{7,5},{8,10},{9,11},{10,... | collective-permute-start | bytes 196616 | tf_op jit(solution)/shard_map/ppermute | solution.py:221
  15.4 7.5 %collective-permute-start.4 = (bf16[2,16,1024]{2,1,0:T(8,128)(2,1)S(1)}, bf16[2,16,1024]{2,1,0:T(8,128)(2,1)S(1)}, u32[]{:S(2)}, u32[]{:S(2)}) collective-permute-start(bf16[2,16,1024]{2,1,0:T(8,128)(2,1)S(1)} %get-tuple-element.46), channel_id=1, source_target_pairs={{0,1},{1,0},{2,3},{3,2},{4,5},{5,4},{6,7},{7,6},{8,9},{9,8},{10,11... | collective-permute-start | bytes 196616 | tf_op jit(solution)/shard_map/ppermute | solution.py:221
  23.0 1.6 %collective-permute-start.7 = (bf16[8,16,1024]{2,1,0:T(8,128)(2,1)S(1)}, bf16[8,16,1024]{2,1,0:T(8,128)(2,1)S(1)}, u32[]{:S(2)}, u32[]{:S(2)}) collective-permute-start(bf16[8,16,1024]{2,1,0:T(8,128)(2,1)S(1)} %constant_dynamic-update-slice_fusion.4.refs_2_), channel_id=1, source_target_pairs={{0,4},{4,0},{8,12},{12,8},{16,20},{20,16},{24,28},{28,24},{1,5},{5... | collective-permute-start | bytes 786440 | tf_op jit(solution)/shard_map/ppermute | solution.py:234
  24.6 22.1 %copy-start = (f32[2,32,1024]{2,1,0:T(8,128)S(1)}, f32[2,32,1024]{2,1,0:T(8,128)}, u32[]{:S(2)}) copy-start(f32[2,32,1024]{2,1,0:T(8,128)} %estimate_ref.1) | copy-start | bytes 786436
  28.6 2.8 %collective-permute-start.8 = (bf16[8,16,1024]{2,1,0:T(8,128)(2,1)S(1)}, bf16[8,16,1024]{2,1,0:T(8,128)(2,1)S(1)}, u32[]{:S(2)}, u32[]{:S(2)}) collective-permute-start(bf16[8,16,1024]{2,1,0:T(8,128)(2,1)S(1)} %get-tuple-element.56), channel_id=1, source_target_pairs={{0,4},{4,0},{8,12},{12,8},{16,20},{20,16},{24,28},{28,24},{1,5},{5... | collective-permute-start | bytes 786440 | tf_op jit(solution)/shard_map/ppermute | solution.py:234
  28.8 7.7 %collective-permute-start.12 = (bf16[4,16,1024]{2,1,0:T(8,128)(2,1)S(1)}, bf16[4,16,1024]{2,1,0:T(8,128)(2,1)S(1)}, u32[]{:S(2)}, u32[]{:S(2)}) collective-permute-start(bf16[4,16,1024]{2,1,0:T(8,128)(2,1)S(1)} %get-tuple-element.64), channel_id=1, source_target_pairs={{0,28},{4,8},{8,4},{12,16},{16,12},{20,24},{24,20},{28,0},{1,29},{... | collective-permute-start | bytes 393224 | tf_op jit(solution)/shard_map/ppermute | solution.py:231
  29.5 12.7 %collective-permute-start.13 = (bf16[4,16,1024]{2,1,0:T(8,128)(2,1)S(1)}, bf16[4,16,1024]{2,1,0:T(8,128)(2,1)S(1)}, u32[]{:S(2)}, u32[]{:S(2)}) collective-permute-start(bf16[4,16,1024]{2,1,0:T(8,128)(2,1)S(1)} %get-tuple-element.68), channel_id=1, source_target_pairs={{0,28},{4,8},{8,4},{12,16},{16,12},{20,24},{24,20},{28,0},{1,29},{... | collective-permute-start | bytes 393224 | tf_op jit(solution)/shard_map/ppermute | solution.py:231
  31.5 4.9 %collective-permute-start.9 = (bf16[2,16,1024]{2,1,0:T(8,128)(2,1)S(1)}, bf16[2,16,1024]{2,1,0:T(8,128)(2,1)S(1)}, u32[]{:S(2)}, u32[]{:S(2)}) collective-permute-start(bf16[2,16,1024]{2,1,0:T(8,128)(2,1)S(1)} %get-tuple-element.58), channel_id=1, source_target_pairs={{0,1},{1,0},{2,3},{3,2},{4,5},{5,4},{6,7},{7,6},{8,9},{9,8},{10,11... | collective-permute-start | bytes 196616 | tf_op jit(solution)/shard_map/ppermute | solution.py:221
  32.3 10.0 %collective-permute-start.10 = (bf16[2,16,1024]{2,1,0:T(8,128)(2,1)S(1)}, bf16[2,16,1024]{2,1,0:T(8,128)(2,1)S(1)}, u32[]{:S(2)}, u32[]{:S(2)}) collective-permute-start(bf16[2,16,1024]{2,1,0:T(8,128)(2,1)S(1)} %get-tuple-element.59), channel_id=1, source_target_pairs={{0,2},{1,3},{2,0},{3,1},{4,6},{5,7},{6,4},{7,5},{8,10},{9,11},{10,... | collective-permute-start | bytes 196616 | tf_op jit(solution)/shard_map/ppermute | solution.py:221
  34.5 7.9 %collective-permute-start.11 = (bf16[2,16,1024]{2,1,0:T(8,128)(2,1)S(1)}, bf16[2,16,1024]{2,1,0:T(8,128)(2,1)S(1)}, u32[]{:S(2)}, u32[]{:S(2)}) collective-permute-start(bf16[2,16,1024]{2,1,0:T(8,128)(2,1)S(1)} %get-tuple-element.60), channel_id=1, source_target_pairs={{0,3},{1,2},{2,1},{3,0},{4,7},{5,6},{6,5},{7,4},{8,11},{9,10},{10,... | collective-permute-start | bytes 196616 | tf_op jit(solution)/shard_map/ppermute | solution.py:221
  36.5 9.1 %collective-permute-start.15 = (bf16[2,16,1024]{2,1,0:T(8,128)(2,1)S(1)}, bf16[2,16,1024]{2,1,0:T(8,128)(2,1)S(1)}, u32[]{:S(2)}, u32[]{:S(2)}) collective-permute-start(bf16[2,16,1024]{2,1,0:T(8,128)(2,1)S(1)} %get-tuple-element.65), channel_id=1, source_target_pairs={{0,2},{1,3},{2,0},{3,1},{4,6},{5,7},{6,4},{7,5},{8,10},{9,11},{10,... | collective-permute-start | bytes 196616 | tf_op jit(solution)/shard_map/ppermute | solution.py:221
  37.8 7.8 %collective-permute-start.16 = (bf16[2,16,1024]{2,1,0:T(8,128)(2,1)S(1)}, bf16[2,16,1024]{2,1,0:T(8,128)(2,1)S(1)}, u32[]{:S(2)}, u32[]{:S(2)}) collective-permute-start(bf16[2,16,1024]{2,1,0:T(8,128)(2,1)S(1)} %get-tuple-element.66), channel_id=1, source_target_pairs={{0,3},{1,2},{2,1},{3,0},{4,7},{5,6},{6,5},{7,4},{8,11},{9,10},{10,... | collective-permute-start | bytes 196616 | tf_op jit(solution)/shard_map/ppermute | solution.py:221
  42.3 4.3 %collective-permute-start.14 = (bf16[2,16,1024]{2,1,0:T(8,128)(2,1)S(1)}, bf16[2,16,1024]{2,1,0:T(8,128)(2,1)S(1)}, u32[]{:S(2)}, u32[]{:S(2)}) collective-permute-start(bf16[2,16,1024]{2,1,0:T(8,128)(2,1)S(1)} %get-tuple-element.70), channel_id=1, source_target_pairs={{0,1},{1,0},{2,3},{3,2},{4,5},{5,4},{6,7},{7,6},{8,9},{9,8},{10,11... | collective-permute-start | bytes 196616 | tf_op jit(solution)/shard_map/ppermute | solution.py:221

commit v5 on v3

--- a/solution.py
+++ b/solution.py
@@ -134,6 +134,8 @@
             inverse = inverse * (2.0 - part * inverse)
             correction = jnp.where(inside, seen * inverse - 1.0, 0.0)
             back_ref[rows, LANES + first : LANES + first + WIDE] = correction.astype(BF16)
+    for view in range(views):
+        rows = slice(view * group, (view + 1) * group)
         backward = jnp.dot(windows(back_ref, rows), tb_ref[view], preferred_element_type=F32)
         for n, first in enumerate(starts):
             deep_ref[rows, first : first + WIDE] = backward[n * group : (n + 1) * group].astype(BF16)

time: 44.8 us -> 44.6 us (level)
  no operation moved by 1% of the time
where the time goes in v5:
time: 44.6 us; the launch traced here: 44.2 us
  starting transfers between devices  23.6 us (53%)
  waiting for transfers between devices  11.2 us (25%)
  Pallas kernels  6.72 us (15%)
  other arithmetic  1.83 us (4%)
  local copies, waits for them, and re-layouts  0.77 us (2%)
    ppermute x12, starting transfers between devices, across(): return lax.ppermute(array, 'depth', [(i, i ^ step) for i in range(depth)])  18.8 us
    ppermute x12, waiting for transfers between devices, across(): return lax.ppermute(array, 'depth', [(i, i ^ step) for i in range(depth)])  8.89 us
    ppermute x3, starting transfers between devices, beside(): return lax.ppermute(array, ('tile', 'depth'), pairs)  4.24 us
    pallas_call x1, Pallas kernels, shards(): call(functools.partial(main_kernel, planes, view_rows), (shape(halves, F3...  3.84 us
    ppermute x3, waiting for transfers between devices, beside(): return lax.ppermute(array, ('tile', 'depth'), pairs)  2.31 us
    pallas_call x1, Pallas kernels, shards(): call(functools.partial(matrices_kernel, planes, strip), (shape((rows, spa...  1.88 us
    convert_element_type x1, other arithmetic, shards(): own = estimate.astype(BF16)  1.05 us
  transfers between devices with their start and end apart: 17, of which 7 were waited for; matrix products, arithmetic and copies ran while one was open for 3% of the time, Pallas kernels for 5%

profile of v5, /device:TPU:0, one launch (start us, length us, event | category | flops | bytes accessed | tf_op | source)
XLA Modules:
  0.0 44.2 jit_solution(17515634398816988753)
XLA Ops:
  0.0 0.0 copy-start.1
  0.0 1.1 %convert_element_type.4 = bf16[2,32,1024]{2,1,0:T(8,128)(2,1)S(1)} convert(f32[2,32,1024]{2,1,0:T(8,128)} %estimate_ref.1) | non-fusion elementwise | flops 65536 | bytes 393216 | tf_op jit(solution)/shard_map/convert_element_type | solution.py:238
  1.1 5.1 %collective-permute-start.2 = (bf16[2,16,1024]{2,1,0:T(8,128)(2,1)S(1)}, bf16[2,16,1024]{2,1,0:T(8,128)(2,1)S(1)}, u32[]{:S(2)}, u32[]{:S(2)}) collective-permute-start(bf16[2,16,1024]{2,1,0:T(8,128)(2,1)S(1)} %get-tuple-element.62), channel_id=1, source_target_pairs={{0,3},{1,2},{2,1},{3,0},{4,7},{5,6},{6,5},{7,4},{8,11},{9,10},{10,... | collective-permute-start | bytes 196616 | tf_op jit(solution)/shard_map/ppermute | solution.py:223
  6.2 0.0 collective-permute-start.1
  6.2 0.6 %collective-permute-start = (bf16[2,16,1024]{2,1,0:T(8,128)(2,1)S(1)}, bf16[2,16,1024]{2,1,0:T(8,128)(2,1)S(1)}, u32[]{:S(2)}, u32[]{:S(2)}) collective-permute-start(bf16[2,16,1024]{2,1,0:T(8,128)(2,1)S(1)} %get-tuple-element.62), channel_id=1, source_target_pairs={{0,1},{1,0},{2,3},{3,2},{4,5},{5,4},{6,7},{7,6},{8,9},{9,8},{10,11... | collective-permute-start | bytes 196616 | tf_op jit(solution)/shard_map/ppermute | solution.py:223
  6.8 0.7 %concatenate.9.device_ref.info_ref = s32[12]{0:T(128)S(1)} concatenate(s32[1]{0:T(128)} %bitcast, s32[1]{0:T(128)} %bitcast.1, s32[1]{0:T(128)} %bitcast.2, s32[1]{0:T(128)} %bitcast.3, s32[8]{0:T(128)} %param.11), dimensions={0} | concatenate | bytes 96 | tf_op jit(solution)/shard_map/concatenate | solution.py:219
  7.6 0.7 %pad_maximum_fusion.1.kernels_ref = f32[3,8,31]{2,1,0:T(8,128)S(1)} fusion(f32[1,8,31]{2,1,0:T(8,128)} %bitcast.9, f32[1,8,31]{2,1,0:T(8,128)} %bitcast.10, f32[1,8,31]{2,1,0:T(8,128)} %bitcast.11), kind=kLoop, calls=%fused_computation.3 | loop fusion | flops 1488 | bytes 5952 | tf_op jit(solution)/shard_map/stack | solution.py:245
  8.3 0.5 %collective-permute-done.2 = bf16[2,16,1024]{2,1,0:T(8,128)(2,1)S(1)} collective-permute-done((bf16[2,16,1024]{2,1,0:T(8,128)(2,1)S(1)}, bf16[2,16,1024]{2,1,0:T(8,128)(2,1)S(1)}, u32[]{:S(2)}, u32[]{:S(2)}) %collective-permute-start.2) | collective-permute-done | bytes 65568 | tf_op jit(solution)/shard_map/ppermute | solution.py:223
  8.8 4.2 %collective-permute-start.6 = (bf16[2,16,1024]{2,1,0:T(8,128)(2,1)S(1)}, bf16[2,16,1024]{2,1,0:T(8,128)(2,1)S(1)}, u32[]{:S(2)}, u32[]{:S(2)}) collective-permute-start(bf16[2,16,1024]{2,1,0:T(8,128)(2,1)S(1)} %get-tuple-element.36), channel_id=1, source_target_pairs={{0,3},{1,2},{2,1},{3,0},{4,7},{5,6},{6,5},{7,4},{8,11},{9,10},{10,... | collective-permute-start | bytes 196616 | tf_op jit(solution)/shard_map/ppermute | solution.py:223
  13.0 0.0 collective-permute-start.5
  13.0 0.6 %collective-permute-start.4 = (bf16[2,16,1024]{2,1,0:T(8,128)(2,1)S(1)}, bf16[2,16,1024]{2,1,0:T(8,128)(2,1)S(1)}, u32[]{:S(2)}, u32[]{:S(2)}) collective-permute-start(bf16[2,16,1024]{2,1,0:T(8,128)(2,1)S(1)} %get-tuple-element.36), channel_id=1, source_target_pairs={{0,1},{1,0},{2,3},{3,2},{4,5},{5,4},{6,7},{7,6},{8,9},{9,8},{10,11... | collective-permute-start | bytes 196616 | tf_op jit(solution)/shard_map/ppermute | solution.py:223
  13.5 0.0 collective-permute-done.1
  13.5 0.0 collective-permute-done
  13.6 1.5 %collective-permute-start.3 = (bf16[8,16,1024]{2,1,0:T(8,128)(2,1)S(1)}, bf16[8,16,1024]{2,1,0:T(8,128)(2,1)S(1)}, u32[]{:S(2)}, u32[]{:S(2)}) collective-permute-start(bf16[8,16,1024]{2,1,0:T(8,128)(2,1)S(1)} %pad_maximum_fusion.refs_1_), channel_id=1, source_target_pairs={{0,1},{4,8},{8,4},{12,16},{16,12},{20,24},{24,20},{28,29},{1,0},{5... | collective-permute-start | bytes 786440 | tf_op jit(solution)/shard_map/ppermute | solution.py:233
  15.1 1.9 %shard_map.64 = (bf16[512,512]{1,0:T(8,128)(2,1)S(1)}, bf16[512,512]{1,0:T(8,128)(2,1)S(1)}, bf16[8,512,256]{2,1,0:T(8,128)(2,1)S(1)}, bf16[8,512,256]{2,1,0:T(8,128)(2,1)S(1)}) custom-call(s32[12]{0:T(128)S(1)} %concatenate.9.device_ref.info_ref, f32[3,8,31]{2,1,0:T(8,128)S(1)} %pad_maximum_fusion.1.kernels_ref), custom_call_target="tpu_custom_call" | custom-call | flops 100000000 | bytes 5242880 | tf_op jit(solution)/shard_map/pallas_call | solution.py:246
  17.0 0.0 collective-permute-done.6
  17.0 1.3 %collective-permute-done.5 = bf16[2,16,1024]{2,1,0:T(8,128)(2,1)S(1)} collective-permute-done((bf16[2,16,1024]{2,1,0:T(8,128)(2,1)S(1)}, bf16[2,16,1024]{2,1,0:T(8,128)(2,1)S(1)}, u32[]{:S(2)}, u32[]{:S(2)}) %collective-permute-start.5) | collective-permute-done | bytes 65568 | tf_op jit(solution)/shard_map/ppermute | solution.py:223
  18.3 0.0 collective-permute-done.4
  18.4 0.1 collective-permute-start.7
  18.5 2.3 %collective-permute-done.3.refs_0_ = bf16[8,16,1024]{2,1,0:T(8,128)(2,1)S(1)} collective-permute-done((bf16[8,16,1024]{2,1,0:T(8,128)(2,1)S(1)}, bf16[8,16,1024]{2,1,0:T(8,128)(2,1)S(1)}, u32[]{:S(2)}, u32[]{:S(2)}) %collective-permute-start.3) | collective-permute-done | bytes 262176 | tf_op jit(solution)/shard_map/ppermute | solution.py:233
  20.8 0.0 collective-permute-done.7.refs_3_
  20.8 0.0 copy-done.1
  20.8 0.0 copy-start
  20.8 3.8 %shard_map.65 = (f32[8,16,1024]{2,1,0:T(8,128)S(1)}, bf16[8,16,1024]{2,1,0:T(8,128)(2,1)S(1)}, f32[4,16,1024]{2,1,0:T(8,128)S(1)}, f32[4,16,1024]{2,1,0:T(8,128)...) custom-call(s32[12]{0:T(128)S(1)} %concatenate.9.device_ref.info_ref, ...), custom_call_target="tpu_custom_call" | custom-call | flops 2000000000 | bytes 10485760 | tf_op jit(solution)/shard_map/pallas_call | solution.py:258
  24.6 0.5 %collective-permute-start.8 = (bf16[8,16,1024]{2,1,0:T(8,128)(2,1)S(1)}, bf16[8,16,1024]{2,1,0:T(8,128)(2,1)S(1)}, u32[]{:S(2)}, u32[]{:S(2)}) collective-permute-start(bf16[8,16,1024]{2,1,0:T(8,128)(2,1)S(1)} %get-tuple-element.46), channel_id=1, source_target_pairs={{0,4},{4,0},{8,12},{12,8},{16,20},{20,16},{24,28},{28,24},{1,5},{5... | collective-permute-start | bytes 786440 | tf_op jit(solution)/shard_map/ppermute | solution.py:236
  25.1 2.7 %collective-permute-start.12 = (bf16[4,16,1024]{2,1,0:T(8,128)(2,1)S(1)}, bf16[4,16,1024]{2,1,0:T(8,128)(2,1)S(1)}, u32[]{:S(2)}, u32[]{:S(2)}) collective-permute-start(bf16[4,16,1024]{2,1,0:T(8,128)(2,1)S(1)} %get-tuple-element.54), channel_id=1, source_target_pairs={{0,28},{4,8},{8,4},{12,16},{16,12},{20,24},{24,20},{28,0},{1,29},{... | collective-permute-start | bytes 393224 | tf_op jit(solution)/shard_map/ppermute | solution.py:233
  27.8 0.0 collective-permute-start.13
  27.8 0.0 collective-permute-done.8.other_ref
  27.8 0.1 shard_map.66
  27.9 1.5 %collective-permute-start.9 = (bf16[2,16,1024]{2,1,0:T(8,128)(2,1)S(1)}, bf16[2,16,1024]{2,1,0:T(8,128)(2,1)S(1)}, u32[]{:S(2)}, u32[]{:S(2)}) collective-permute-start(bf16[2,16,1024]{2,1,0:T(8,128)(2,1)S(1)} %get-tuple-element.48), channel_id=1, source_target_pairs={{0,1},{1,0},{2,3},{3,2},{4,5},{5,4},{6,7},{7,6},{8,9},{9,8},{10,11... | collective-permute-start | bytes 196616 | tf_op jit(solution)/shard_map/ppermute | solution.py:223
  29.5 2.9 %collective-permute-start.10 = (bf16[2,16,1024]{2,1,0:T(8,128)(2,1)S(1)}, bf16[2,16,1024]{2,1,0:T(8,128)(2,1)S(1)}, u32[]{:S(2)}, u32[]{:S(2)}) collective-permute-start(bf16[2,16,1024]{2,1,0:T(8,128)(2,1)S(1)} %get-tuple-element.49), channel_id=1, source_target_pairs={{0,2},{1,3},{2,0},{3,1},{4,6},{5,7},{6,4},{7,5},{8,10},{9,11},{10,... | collective-permute-start | bytes 196616 | tf_op jit(solution)/shard_map/ppermute | solution.py:223
  32.4 0.0 collective-permute-start.11
  32.4 0.4 collective-permute-done.9.refs_1_
  32.8 0.0 collective-permute-done.12.other_ref
  32.8 1.9 %collective-permute-start.15 = (bf16[2,16,1024]{2,1,0:T(8,128)(2,1)S(1)}, bf16[2,16,1024]{2,1,0:T(8,128)(2,1)S(1)}, u32[]{:S(2)}, u32[]{:S(2)}) collective-permute-start(bf16[2,16,1024]{2,1,0:T(8,128)(2,1)S(1)} %get-tuple-element.55), channel_id=1, source_target_pairs={{0,2},{1,3},{2,0},{3,1},{4,6},{5,7},{6,4},{7,5},{8,10},{9,11},{10,... | collective-permute-start | bytes 196616 | tf_op jit(solution)/shard_map/ppermute | solution.py:223
  34.8 1.7 %collective-permute-start.16 = (bf16[2,16,1024]{2,1,0:T(8,128)(2,1)S(1)}, bf16[2,16,1024]{2,1,0:T(8,128)(2,1)S(1)}, u32[]{:S(2)}, u32[]{:S(2)}) collective-permute-start(bf16[2,16,1024]{2,1,0:T(8,128)(2,1)S(1)} %get-tuple-element.56), channel_id=1, source_target_pairs={{0,3},{1,2},{2,1},{3,0},{4,7},{5,6},{6,5},{7,4},{8,11},{9,10},{10,... | collective-permute-start | bytes 196616 | tf_op jit(solution)/shard_map/ppermute | solution.py:223
  36.4 2.6 %collective-permute-done.10.refs_2_ = bf16[2,16,1024]{2,1,0:T(8,128)(2,1)S(1)} collective-permute-done((bf16[2,16,1024]{2,1,0:T(8,128)(2,1)S(1)}, bf16[2,16,1024]{2,1,0:T(8,128)(2,1)S(1)}, u32[]{:S(2)}, u32[]{:S(2)}) %collective-permute-start.10) | collective-permute-done | bytes 65568 | tf_op jit(solution)/shard_map/ppermute | solution.py:223
  39.0 0.0 collective-permute-done.13.other_ref
  39.0 0.2 collective-permute-start.14
  39.2 0.0 collective-permute-done.11.refs_3_
  39.2 3.4 %collective-permute-done.15.refs_6_ = bf16[2,16,1024]{2,1,0:T(8,128)(2,1)S(1)} collective-permute-done((bf16[2,16,1024]{2,1,0:T(8,128)(2,1)S(1)}, bf16[2,16,1024]{2,1,0:T(8,128)(2,1)S(1)}, u32[]{:S(2)}, u32[]{:S(2)}) %collective-permute-start.15) | collective-permute-done | bytes 65568 | tf_op jit(solution)/shard_map/ppermute | solution.py:223
  42.6 0.0 collective-permute-done.16.refs_7_
  42.6 0.7 %collective-permute-done.14.refs_5_ = bf16[2,16,1024]{2,1,0:T(8,128)(2,1)S(1)} collective-permute-done((bf16[2,16,1024]{2,1,0:T(8,128)(2,1)S(1)}, bf16[2,16,1024]{2,1,0:T(8,128)(2,1)S(1)}, u32[]{:S(2)}, u32[]{:S(2)}) %collective-permute-start.14) | collective-permute-done | bytes 65568 | tf_op jit(solution)/shard_map/ppermute | solution.py:223
  43.4 0.0 copy-done
  43.4 0.8 %shard_map.69 = f32[2,32,1024]{2,1,0:T(8,128)} custom-call(f32[2,32,1024]{2,1,0:T(8,128)S(1)} %copy-done, f32[32,128]{1,0:T(8,128)S(1)} %get-tuple-element.43.scale_ref, s32[16,128]{1,0:T(8,128)S(1)} %get-tuple-element.44.odd_ref, f32[2,16,1024]{2,1,0:T(8,128)S(1)} %get-tuple-element.47.refs_0_, bf16[2,16,1024]{2,1,0:T(8,128)(2,1)S(1)} %collective-permute-done.9.refs_1_, ...), custom_call_target="tpu_custom_call" | custom-call | flops 1000000 | bytes 1048576 | tf_op jit(solution)/shard_map/pallas_call | solution.py:287
  (8 shorter events, 0.2 us)
Async XLA Ops:
  0.0 20.8 %copy-start.1 = (bf16[8,2,32,1024]{3,2,1,0:T(8,128)(2,1)S(1)}, bf16[8,2,32,1024]{3,2,1,0:T(8,128)(2,1)}, u32[]{:S(2)}) copy-start(bf16[8,2,32,1024]{3,2,1,0:T(8,128)(2,1)} %param.7) | copy-start | bytes 3145732
  1.1 7.7 %collective-permute-start.2 = (bf16[2,16,1024]{2,1,0:T(8,128)(2,1)S(1)}, bf16[2,16,1024]{2,1,0:T(8,128)(2,1)S(1)}, u32[]{:S(2)}, u32[]{:S(2)}) collective-permute-start(bf16[2,16,1024]{2,1,0:T(8,128)(2,1)S(1)} %get-tuple-element.62), channel_id=1, source_target_pairs={{0,3},{1,2},{2,1},{3,0},{4,7},{5,6},{6,5},{7,4},{8,11},{9,10},{10,... | collective-permute-start | bytes 196616 | tf_op jit(solution)/shard_map/ppermute | solution.py:223
  6.2 7.4 %collective-permute-start.1 = (bf16[2,16,1024]{2,1,0:T(8,128)(2,1)S(1)}, bf16[2,16,1024]{2,1,0:T(8,128)(2,1)S(1)}, u32[]{:S(2)}, u32[]{:S(2)}) collective-permute-start(bf16[2,16,1024]{2,1,0:T(8,128)(2,1)S(1)} %get-tuple-element.62), channel_id=1, source_target_pairs={{0,2},{1,3},{2,0},{3,1},{4,6},{5,7},{6,4},{7,5},{8,10},{9,11},{10,... | collective-permute-start | bytes 196616 | tf_op jit(solution)/shard_map/ppermute | solution.py:223
  6.2 7.4 %collective-permute-start = (bf16[2,16,1024]{2,1,0:T(8,128)(2,1)S(1)}, bf16[2,16,1024]{2,1,0:T(8,128)(2,1)S(1)}, u32[]{:S(2)}, u32[]{:S(2)}) collective-permute-start(bf16[2,16,1024]{2,1,0:T(8,128)(2,1)S(1)} %get-tuple-element.62), channel_id=1, source_target_pairs={{0,1},{1,0},{2,3},{3,2},{4,5},{5,4},{6,7},{7,6},{8,9},{9,8},{10,11... | collective-permute-start | bytes 196616 | tf_op jit(solution)/shard_map/ppermute | solution.py:223
  8.8 8.2 %collective-permute-start.6 = (bf16[2,16,1024]{2,1,0:T(8,128)(2,1)S(1)}, bf16[2,16,1024]{2,1,0:T(8,128)(2,1)S(1)}, u32[]{:S(2)}, u32[]{:S(2)}) collective-permute-start(bf16[2,16,1024]{2,1,0:T(8,128)(2,1)S(1)} %get-tuple-element.36), channel_id=1, source_target_pairs={{0,3},{1,2},{2,1},{3,0},{4,7},{5,6},{6,5},{7,4},{8,11},{9,10},{10,... | collective-permute-start | bytes 196616 | tf_op jit(solution)/shard_map/ppermute | solution.py:223
  13.0 5.3 %collective-permute-start.5 = (bf16[2,16,1024]{2,1,0:T(8,128)(2,1)S(1)}, bf16[2,16,1024]{2,1,0:T(8,128)(2,1)S(1)}, u32[]{:S(2)}, u32[]{:S(2)}) collective-permute-start(bf16[2,16,1024]{2,1,0:T(8,128)(2,1)S(1)} %get-tuple-element.36), channel_id=1, source_target_pairs={{0,2},{1,3},{2,0},{3,1},{4,6},{5,7},{6,4},{7,5},{8,10},{9,11},{10,... | collective-permute-start | bytes 196616 | tf_op jit(solution)/shard_map/ppermute | solution.py:223
  13.0 5.3 %collective-permute-start.4 = (bf16[2,16,1024]{2,1,0:T(8,128)(2,1)S(1)}, bf16[2,16,1024]{2,1,0:T(8,128)(2,1)S(1)}, u32[]{:S(2)}, u32[]{:S(2)}) collective-permute-start(bf16[2,16,1024]{2,1,0:T(8,128)(2,1)S(1)} %get-tuple-element.36), channel_id=1, source_target_pairs={{0,1},{1,0},{2,3},{3,2},{4,5},{5,4},{6,7},{7,6},{8,9},{9,8},{10,11... | collective-permute-start | bytes 196616 | tf_op jit(solution)/shard_map/ppermute | solution.py:223
  13.6 7.2 %collective-permute-start.3 = (bf16[8,16,1024]{2,1,0:T(8,128)(2,1)S(1)}, bf16[8,16,1024]{2,1,0:T(8,128)(2,1)S(1)}, u32[]{:S(2)}, u32[]{:S(2)}) collective-permute-start(bf16[8,16,1024]{2,1,0:T(8,128)(2,1)S(1)} %pad_maximum_fusion.refs_1_), channel_id=1, source_target_pairs={{0,1},{4,8},{8,4},{12,16},{16,12},{20,24},{24,20},{28,29},{1,0},{5... | collective-permute-start | bytes 786440 | tf_op jit(solution)/shard_map/ppermute | solution.py:233
  18.4 2.4 %collective-permute-start.7 = (bf16[8,16,1024]{2,1,0:T(8,128)(2,1)S(1)}, bf16[8,16,1024]{2,1,0:T(8,128)(2,1)S(1)}, u32[]{:S(2)}, u32[]{:S(2)}) collective-permute-start(bf16[8,16,1024]{2,1,0:T(8,128)(2,1)S(1)} %constant_dynamic-update-slice_fusion.refs_2_), channel_id=1, source_target_pairs={{0,4},{4,0},{8,12},{12,8},{16,20},{20,16},{24,28},{28,24},{1,5},{5... | collective-permute-start | bytes 786440 | tf_op jit(solution)/shard_map/ppermute | solution.py:236
  20.8 22.6 %copy-start = (f32[2,32,1024]{2,1,0:T(8,128)S(1)}, f32[2,32,1024]{2,1,0:T(8,128)}, u32[]{:S(2)}) copy-start(f32[2,32,1024]{2,1,0:T(8,128)} %estimate_ref.1) | copy-start | bytes 786436
  24.6 3.2 %collective-permute-start.8 = (bf16[8,16,1024]{2,1,0:T(8,128)(2,1)S(1)}, bf16[8,16,1024]{2,1,0:T(8,128)(2,1)S(1)}, u32[]{:S(2)}, u32[]{:S(2)}) collective-permute-start(bf16[8,16,1024]{2,1,0:T(8,128)(2,1)S(1)} %get-tuple-element.46), channel_id=1, source_target_pairs={{0,4},{4,0},{8,12},{12,8},{16,20},{20,16},{24,28},{28,24},{1,5},{5... | collective-permute-start | bytes 786440 | tf_op jit(solution)/shard_map/ppermute | solution.py:236
  25.1 7.7 %collective-permute-start.12 = (bf16[4,16,1024]{2,1,0:T(8,128)(2,1)S(1)}, bf16[4,16,1024]{2,1,0:T(8,128)(2,1)S(1)}, u32[]{:S(2)}, u32[]{:S(2)}) collective-permute-start(bf16[4,16,1024]{2,1,0:T(8,128)(2,1)S(1)} %get-tuple-element.54), channel_id=1, source_target_pairs={{0,28},{4,8},{8,4},{12,16},{16,12},{20,24},{24,20},{28,0},{1,29},{... | collective-permute-start | bytes 393224 | tf_op jit(solution)/shard_map/ppermute | solution.py:233
  27.8 11.2 %collective-permute-start.13 = (bf16[4,16,1024]{2,1,0:T(8,128)(2,1)S(1)}, bf16[4,16,1024]{2,1,0:T(8,128)(2,1)S(1)}, u32[]{:S(2)}, u32[]{:S(2)}) collective-permute-start(bf16[4,16,1024]{2,1,0:T(8,128)(2,1)S(1)} %get-tuple-element.58), channel_id=1, source_target_pairs={{0,28},{4,8},{8,4},{12,16},{16,12},{20,24},{24,20},{28,0},{1,29},{... | collective-permute-start | bytes 393224 | tf_op jit(solution)/shard_map/ppermute | solution.py:233
  27.9 4.9 %collective-permute-start.9 = (bf16[2,16,1024]{2,1,0:T(8,128)(2,1)S(1)}, bf16[2,16,1024]{2,1,0:T(8,128)(2,1)S(1)}, u32[]{:S(2)}, u32[]{:S(2)}) collective-permute-start(bf16[2,16,1024]{2,1,0:T(8,128)(2,1)S(1)} %get-tuple-element.48), channel_id=1, source_target_pairs={{0,1},{1,0},{2,3},{3,2},{4,5},{5,4},{6,7},{7,6},{8,9},{9,8},{10,11... | collective-permute-start | bytes 196616 | tf_op jit(solution)/shard_map/ppermute | solution.py:223
  29.5 9.5 %collective-permute-start.10 = (bf16[2,16,1024]{2,1,0:T(8,128)(2,1)S(1)}, bf16[2,16,1024]{2,1,0:T(8,128)(2,1)S(1)}, u32[]{:S(2)}, u32[]{:S(2)}) collective-permute-start(bf16[2,16,1024]{2,1,0:T(8,128)(2,1)S(1)} %get-tuple-element.49), channel_id=1, source_target_pairs={{0,2},{1,3},{2,0},{3,1},{4,6},{5,7},{6,4},{7,5},{8,10},{9,11},{10,... | collective-permute-start | bytes 196616 | tf_op jit(solution)/shard_map/ppermute | solution.py:223
  32.4 6.9 %collective-permute-start.11 = (bf16[2,16,1024]{2,1,0:T(8,128)(2,1)S(1)}, bf16[2,16,1024]{2,1,0:T(8,128)(2,1)S(1)}, u32[]{:S(2)}, u32[]{:S(2)}) collective-permute-start(bf16[2,16,1024]{2,1,0:T(8,128)(2,1)S(1)} %get-tuple-element.50), channel_id=1, source_target_pairs={{0,3},{1,2},{2,1},{3,0},{4,7},{5,6},{6,5},{7,4},{8,11},{9,10},{10,... | collective-permute-start | bytes 196616 | tf_op jit(solution)/shard_map/ppermute | solution.py:223
  32.8 9.8 %collective-permute-start.15 = (bf16[2,16,1024]{2,1,0:T(8,128)(2,1)S(1)}, bf16[2,16,1024]{2,1,0:T(8,128)(2,1)S(1)}, u32[]{:S(2)}, u32[]{:S(2)}) collective-permute-start(bf16[2,16,1024]{2,1,0:T(8,128)(2,1)S(1)} %get-tuple-element.55), channel_id=1, source_target_pairs={{0,2},{1,3},{2,0},{3,1},{4,6},{5,7},{6,4},{7,5},{8,10},{9,11},{10,... | collective-permute-start | bytes 196616 | tf_op jit(solution)/shard_map/ppermute | solution.py:223
  34.8 7.9 %collective-permute-start.16 = (bf16[2,16,1024]{2,1,0:T(8,128)(2,1)S(1)}, bf16[2,16,1024]{2,1,0:T(8,128)(2,1)S(1)}, u32[]{:S(2)}, u32[]{:S(2)}) collective-permute-start(bf16[2,16,1024]{2,1,0:T(8,128)(2,1)S(1)} %get-tuple-element.56), channel_id=1, source_target_pairs={{0,3},{1,2},{2,1},{3,0},{4,7},{5,6},{6,5},{7,4},{8,11},{9,10},{10,... | collective-permute-start | bytes 196616 | tf_op jit(solution)/shard_map/ppermute | solution.py:223
  39.0 4.3 %collective-permute-start.14 = (bf16[2,16,1024]{2,1,0:T(8,128)(2,1)S(1)}, bf16[2,16,1024]{2,1,0:T(8,128)(2,1)S(1)}, u32[]{:S(2)}, u32[]{:S(2)}) collective-permute-start(bf16[2,16,1024]{2,1,0:T(8,128)(2,1)S(1)} %get-tuple-element.60), channel_id=1, source_target_pairs={{0,1},{1,0},{2,3},{3,2},{4,5},{5,4},{6,7},{7,6},{8,9},{9,8},{10,11... | collective-permute-start | bytes 196616 | tf_op jit(solution)/shard_map/ppermute | solution.py:223

commit v6 on v5

--- a/solution.py
+++ b/solution.py
@@ -72,7 +72,7 @@
 
 
 def write_coded(out_ref, where, values):
-    pick = values.shape[-1] // 2 - LANES
+    pick = coded_base(values.shape[-1])
     base = values[..., pick : pick + LANES].astype(BF16)
     wide = base.astype(F32)
     for first in range(0, values.shape[-1], LANES):
@@ -81,8 +81,22 @@
         out_ref[where + (slice(first, first + LANES),)] = part
 
 
+def coded_base(columns):
+    return columns // 2 - LANES
+
+
+def write_coded_part(out_ref, plane, values, first):
+    pick = coded_base(out_ref.shape[-1])
+    begins = range(first, first + values.shape[-1], LANES)
+    for begin in sorted(begins, key=lambda begin: begin != pick):
+        part = values[:, begin - first : begin - first + LANES]
+        if begin != pick:
+            part = part - out_ref[plane, :, pick : pick + LANES].astype(F32)
+        out_ref[plane, :, begin : begin + LANES] = part.astype(BF16)
+
+
 def decoded(values, first):
-    pick = values.shape[-1] // 2 - LANES
+    pick = coded_base(values.shape[-1])
     base = values[..., pick : pick + LANES].astype(F32)
     if first == pick:
         return base
@@ -139,12 +153,17 @@
         backward = jnp.dot(windows(back_ref, rows), tb_ref[view], preferred_element_type=F32)
         for n, first in enumerate(starts):
             deep_ref[rows, first : first + WIDE] = backward[n * group : (n + 1) * group].astype(BF16)
-    for p in range(count):
-        part = jnp.dot(wt_ref[p * extent : (p + 1) * extent], deep_ref[...], preferred_element_type=F32)
-        write_coded(inner_ref, (p, slice(None)), part[:HALO])
-        core_ref[p] = part[HALO : 2 * HALO]
-        outer_refs[p // (count // 2)][p % (count // 2)] = part[2 * HALO : 3 * HALO]
-        write_coded(outer_refs[2 + p // (count // 2)], (p % (count // 2), slice(None)), part[3 * HALO :])
+    pick = coded_base(columns)
+    for first in sorted(starts, key=lambda first: first // WIDE != pick // WIDE):
+        block = jnp.dot(wt_ref[...], deep_ref[:, first : first + WIDE], preferred_element_type=F32)
+        lanes = slice(first, first + WIDE)
+        for p in range(count):
+            half, slot = p // (count // 2), p % (count // 2)
+            quarters = [block[p * extent + n * HALO : p * extent + (n + 1) * HALO] for n in range(4)]
+            core_ref[p, :, lanes] = quarters[1]
+            outer_refs[half][slot, :, lanes] = quarters[2]
+            write_coded_part(inner_ref, p, quarters[0], first)
+            write_coded_part(outer_refs[2 + half], slot, quarters[3], first)
     scale_ref[...] = 1.0 / jnp.maximum(coverage, 1.0)
     odd_ref[...] = jnp.full(odd_ref.shape, info_ref[1], jnp.int32)
 

time: 44.6 us -> 44.1 us (0.989)
  Pallas kernels: 6.72 us -> 6.19 us
    pallas_call x1, Pallas kernels: 3.84 us -> 3.31 us  [shards(): call(functools.partial(main_kernel, planes, view_rows), (shape(halves, F3...]
where the time goes in v6:
time: 44.1 us; the launch traced here: 43.6 us
  starting transfers between devices  23.6 us (54%)
  waiting for transfers between devices  11.1 us (25%)
  Pallas kernels  6.19 us (14%)
  other arithmetic  1.83 us (4%)
  local copies, waits for them, and re-layouts  0.77 us (2%)
    ppermute x12, starting transfers between devices, across(): return lax.ppermute(array, 'depth', [(i, i ^ step) for i in range(depth)])  18.8 us
    ppermute x12, waiting for transfers between devices, across(): return lax.ppermute(array, 'depth', [(i, i ^ step) for i in range(depth)])  8.79 us
    ppermute x3, starting transfers between devices, beside(): return lax.ppermute(array, ('tile', 'depth'), pairs)  4.24 us
    pallas_call x1, Pallas kernels, shards(): call(functools.partial(main_kernel, planes, view_rows), (shape(halves, F3...  3.31 us
    ppermute x3, waiting for transfers between devices, beside(): return lax.ppermute(array, ('tile', 'depth'), pairs)  2.31 us
    pallas_call x1, Pallas kernels, shards(): call(functools.partial(matrices_kernel, planes, strip), (shape((rows, spa...  1.88 us
    convert_element_type x1, other arithmetic, shards(): own = estimate.astype(BF16)  1.05 us
  transfers between devices with their start and end apart: 17, of which 7 were waited for; matrix products, arithmetic and copies ran while one was open for 3% of the time, Pallas kernels for 5%

profile of v6, /device:TPU:0, one launch (start us, length us, event | category | flops | bytes accessed | tf_op | source)
XLA Modules:
  0.0 43.6 jit_solution(12496744303969511512)
XLA Ops:
  0.0 0.0 copy-start.1
  0.0 1.1 %convert_element_type.4 = bf16[2,32,1024]{2,1,0:T(8,128)(2,1)S(1)} convert(f32[2,32,1024]{2,1,0:T(8,128)} %estimate_ref.1) | non-fusion elementwise | flops 65536 | bytes 393216 | tf_op jit(solution)/shard_map/convert_element_type | solution.py:257
  1.1 5.1 %collective-permute-start.2 = (bf16[2,16,1024]{2,1,0:T(8,128)(2,1)S(1)}, bf16[2,16,1024]{2,1,0:T(8,128)(2,1)S(1)}, u32[]{:S(2)}, u32[]{:S(2)}) collective-permute-start(bf16[2,16,1024]{2,1,0:T(8,128)(2,1)S(1)} %get-tuple-element.62), channel_id=1, source_target_pairs={{0,3},{1,2},{2,1},{3,0},{4,7},{5,6},{6,5},{7,4},{8,11},{9,10},{10,... | collective-permute-start | bytes 196616 | tf_op jit(solution)/shard_map/ppermute | solution.py:242
  6.2 0.0 collective-permute-start.1
  6.2 0.6 %collective-permute-start = (bf16[2,16,1024]{2,1,0:T(8,128)(2,1)S(1)}, bf16[2,16,1024]{2,1,0:T(8,128)(2,1)S(1)}, u32[]{:S(2)}, u32[]{:S(2)}) collective-permute-start(bf16[2,16,1024]{2,1,0:T(8,128)(2,1)S(1)} %get-tuple-element.62), channel_id=1, source_target_pairs={{0,1},{1,0},{2,3},{3,2},{4,5},{5,4},{6,7},{7,6},{8,9},{9,8},{10,11... | collective-permute-start | bytes 196616 | tf_op jit(solution)/shard_map/ppermute | solution.py:242
  6.8 0.7 %concatenate.9.device_ref.info_ref = s32[12]{0:T(128)S(1)} concatenate(s32[1]{0:T(128)} %bitcast, s32[1]{0:T(128)} %bitcast.1, s32[1]{0:T(128)} %bitcast.2, s32[1]{0:T(128)} %bitcast.3, s32[8]{0:T(128)} %param.11), dimensions={0} | concatenate | bytes 96 | tf_op jit(solution)/shard_map/concatenate | solution.py:238
  7.6 0.7 %pad_maximum_fusion.1.kernels_ref = f32[3,8,31]{2,1,0:T(8,128)S(1)} fusion(f32[1,8,31]{2,1,0:T(8,128)} %bitcast.9, f32[1,8,31]{2,1,0:T(8,128)} %bitcast.10, f32[1,8,31]{2,1,0:T(8,128)} %bitcast.11), kind=kLoop, calls=%fused_computation.3 | loop fusion | flops 1488 | bytes 5952 | tf_op jit(solution)/shard_map/stack | solution.py:264
  8.3 0.5 %collective-permute-done.2 = bf16[2,16,1024]{2,1,0:T(8,128)(2,1)S(1)} collective-permute-done((bf16[2,16,1024]{2,1,0:T(8,128)(2,1)S(1)}, bf16[2,16,1024]{2,1,0:T(8,128)(2,1)S(1)}, u32[]{:S(2)}, u32[]{:S(2)}) %collective-permute-start.2) | collective-permute-done | bytes 65568 | tf_op jit(solution)/shard_map/ppermute | solution.py:242
  8.8 4.2 %collective-permute-start.6 = (bf16[2,16,1024]{2,1,0:T(8,128)(2,1)S(1)}, bf16[2,16,1024]{2,1,0:T(8,128)(2,1)S(1)}, u32[]{:S(2)}, u32[]{:S(2)}) collective-permute-start(bf16[2,16,1024]{2,1,0:T(8,128)(2,1)S(1)} %get-tuple-element.36), channel_id=1, source_target_pairs={{0,3},{1,2},{2,1},{3,0},{4,7},{5,6},{6,5},{7,4},{8,11},{9,10},{10,... | collective-permute-start | bytes 196616 | tf_op jit(solution)/shard_map/ppermute | solution.py:242
  13.0 0.0 collective-permute-start.5
  13.0 0.6 %collective-permute-start.4 = (bf16[2,16,1024]{2,1,0:T(8,128)(2,1)S(1)}, bf16[2,16,1024]{2,1,0:T(8,128)(2,1)S(1)}, u32[]{:S(2)}, u32[]{:S(2)}) collective-permute-start(bf16[2,16,1024]{2,1,0:T(8,128)(2,1)S(1)} %get-tuple-element.36), channel_id=1, source_target_pairs={{0,1},{1,0},{2,3},{3,2},{4,5},{5,4},{6,7},{7,6},{8,9},{9,8},{10,11... | collective-permute-start | bytes 196616 | tf_op jit(solution)/shard_map/ppermute | solution.py:242
  13.5 0.0 collective-permute-done.1
  13.5 0.0 collective-permute-done
  13.6 1.5 %collective-permute-start.3 = (bf16[8,16,1024]{2,1,0:T(8,128)(2,1)S(1)}, bf16[8,16,1024]{2,1,0:T(8,128)(2,1)S(1)}, u32[]{:S(2)}, u32[]{:S(2)}) collective-permute-start(bf16[8,16,1024]{2,1,0:T(8,128)(2,1)S(1)} %pad_maximum_fusion.refs_1_), channel_id=1, source_target_pairs={{0,1},{4,8},{8,4},{12,16},{16,12},{20,24},{24,20},{28,29},{1,0},{5... | collective-permute-start | bytes 786440 | tf_op jit(solution)/shard_map/ppermute | solution.py:252
  15.1 1.9 %shard_map.64 = (bf16[512,512]{1,0:T(8,128)(2,1)S(1)}, bf16[512,512]{1,0:T(8,128)(2,1)S(1)}, bf16[8,512,256]{2,1,0:T(8,128)(2,1)S(1)}, bf16[8,512,256]{2,1,0:T(8,128)(2,1)S(1)}) custom-call(s32[12]{0:T(128)S(1)} %concatenate.9.device_ref.info_ref, f32[3,8,31]{2,1,0:T(8,128)S(1)} %pad_maximum_fusion.1.kernels_ref), custom_call_target="tpu_custom_call" | custom-call | flops 100000000 | bytes 5242880 | tf_op jit(solution)/shard_map/pallas_call | solution.py:265
  17.0 0.0 collective-permute-done.6
  17.0 1.3 %collective-permute-done.5 = bf16[2,16,1024]{2,1,0:T(8,128)(2,1)S(1)} collective-permute-done((bf16[2,16,1024]{2,1,0:T(8,128)(2,1)S(1)}, bf16[2,16,1024]{2,1,0:T(8,128)(2,1)S(1)}, u32[]{:S(2)}, u32[]{:S(2)}) %collective-permute-start.5) | collective-permute-done | bytes 65568 | tf_op jit(solution)/shard_map/ppermute | solution.py:242
  18.3 0.0 collective-permute-done.4
  18.4 0.1 collective-permute-start.7
  18.5 2.3 %collective-permute-done.3.refs_0_ = bf16[8,16,1024]{2,1,0:T(8,128)(2,1)S(1)} collective-permute-done((bf16[8,16,1024]{2,1,0:T(8,128)(2,1)S(1)}, bf16[8,16,1024]{2,1,0:T(8,128)(2,1)S(1)}, u32[]{:S(2)}, u32[]{:S(2)}) %collective-permute-start.3) | collective-permute-done | bytes 262176 | tf_op jit(solution)/shard_map/ppermute | solution.py:252
  20.8 0.0 collective-permute-done.7.refs_3_
  20.8 0.0 copy-done.1
  20.8 0.0 copy-start
  20.8 3.3 %shard_map.65 = (f32[8,16,1024]{2,1,0:T(8,128)S(1)}, bf16[8,16,1024]{2,1,0:T(8,128)(2,1)S(1)}, f32[4,16,1024]{2,1,0:T(8,128)S(1)}, f32[4,16,1024]{2,1,0:T(8,128)...) custom-call(s32[12]{0:T(128)S(1)} %concatenate.9.device_ref.info_ref, ...), custom_call_target="tpu_custom_call" | custom-call | flops 2000000000 | bytes 10485760 | tf_op jit(solution)/shard_map/pallas_call | solution.py:277
  24.1 0.5 %collective-permute-start.8 = (bf16[8,16,1024]{2,1,0:T(8,128)(2,1)S(1)}, bf16[8,16,1024]{2,1,0:T(8,128)(2,1)S(1)}, u32[]{:S(2)}, u32[]{:S(2)}) collective-permute-start(bf16[8,16,1024]{2,1,0:T(8,128)(2,1)S(1)} %get-tuple-element.46), channel_id=1, source_target_pairs={{0,4},{4,0},{8,12},{12,8},{16,20},{20,16},{24,28},{28,24},{1,5},{5... | collective-permute-start | bytes 786440 | tf_op jit(solution)/shard_map/ppermute | solution.py:255
  24.6 2.7 %collective-permute-start.12 = (bf16[4,16,1024]{2,1,0:T(8,128)(2,1)S(1)}, bf16[4,16,1024]{2,1,0:T(8,128)(2,1)S(1)}, u32[]{:S(2)}, u32[]{:S(2)}) collective-permute-start(bf16[4,16,1024]{2,1,0:T(8,128)(2,1)S(1)} %get-tuple-element.54), channel_id=1, source_target_pairs={{0,28},{4,8},{8,4},{12,16},{16,12},{20,24},{24,20},{28,0},{1,29},{... | collective-permute-start | bytes 393224 | tf_op jit(solution)/shard_map/ppermute | solution.py:252
  27.3 0.0 collective-permute-start.13
  27.3 0.0 collective-permute-done.8.other_ref
  27.3 0.1 shard_map.66
  27.4 1.5 %collective-permute-start.9 = (bf16[2,16,1024]{2,1,0:T(8,128)(2,1)S(1)}, bf16[2,16,1024]{2,1,0:T(8,128)(2,1)S(1)}, u32[]{:S(2)}, u32[]{:S(2)}) collective-permute-start(bf16[2,16,1024]{2,1,0:T(8,128)(2,1)S(1)} %get-tuple-element.48), channel_id=1, source_target_pairs={{0,1},{1,0},{2,3},{3,2},{4,5},{5,4},{6,7},{7,6},{8,9},{9,8},{10,11... | collective-permute-start | bytes 196616 | tf_op jit(solution)/shard_map/ppermute | solution.py:242
  28.9 2.9 %collective-permute-start.10 = (bf16[2,16,1024]{2,1,0:T(8,128)(2,1)S(1)}, bf16[2,16,1024]{2,1,0:T(8,128)(2,1)S(1)}, u32[]{:S(2)}, u32[]{:S(2)}) collective-permute-start(bf16[2,16,1024]{2,1,0:T(8,128)(2,1)S(1)} %get-tuple-element.49), channel_id=1, source_target_pairs={{0,2},{1,3},{2,0},{3,1},{4,6},{5,7},{6,4},{7,5},{8,10},{9,11},{10,... | collective-permute-start | bytes 196616 | tf_op jit(solution)/shard_map/ppermute | solution.py:242
  31.8 0.0 collective-permute-start.11
  31.8 0.4 collective-permute-done.9.refs_1_
  32.2 0.0 collective-permute-done.12.other_ref
  32.3 1.9 %collective-permute-start.15 = (bf16[2,16,1024]{2,1,0:T(8,128)(2,1)S(1)}, bf16[2,16,1024]{2,1,0:T(8,128)(2,1)S(1)}, u32[]{:S(2)}, u32[]{:S(2)}) collective-permute-start(bf16[2,16,1024]{2,1,0:T(8,128)(2,1)S(1)} %get-tuple-element.55), channel_id=1, source_target_pairs={{0,2},{1,3},{2,0},{3,1},{4,6},{5,7},{6,4},{7,5},{8,10},{9,11},{10,... | collective-permute-start | bytes 196616 | tf_op jit(solution)/shard_map/ppermute | solution.py:242
  34.2 1.7 %collective-permute-start.16 = (bf16[2,16,1024]{2,1,0:T(8,128)(2,1)S(1)}, bf16[2,16,1024]{2,1,0:T(8,128)(2,1)S(1)}, u32[]{:S(2)}, u32[]{:S(2)}) collective-permute-start(bf16[2,16,1024]{2,1,0:T(8,128)(2,1)S(1)} %get-tuple-element.56), channel_id=1, source_target_pairs={{0,3},{1,2},{2,1},{3,0},{4,7},{5,6},{6,5},{7,4},{8,11},{9,10},{10,... | collective-permute-start | bytes 196616 | tf_op jit(solution)/shard_map/ppermute | solution.py:242
  35.9 2.5 %collective-permute-done.10.refs_2_ = bf16[2,16,1024]{2,1,0:T(8,128)(2,1)S(1)} collective-permute-done((bf16[2,16,1024]{2,1,0:T(8,128)(2,1)S(1)}, bf16[2,16,1024]{2,1,0:T(8,128)(2,1)S(1)}, u32[]{:S(2)}, u32[]{:S(2)}) %collective-permute-start.10) | collective-permute-done | bytes 65568 | tf_op jit(solution)/shard_map/ppermute | solution.py:242
  38.4 0.0 collective-permute-done.13.other_ref
  38.4 0.3 collective-permute-start.14
  38.7 0.0 collective-permute-done.11.refs_3_
  38.7 3.4 %collective-permute-done.15.refs_6_ = bf16[2,16,1024]{2,1,0:T(8,128)(2,1)S(1)} collective-permute-done((bf16[2,16,1024]{2,1,0:T(8,128)(2,1)S(1)}, bf16[2,16,1024]{2,1,0:T(8,128)(2,1)S(1)}, u32[]{:S(2)}, u32[]{:S(2)}) %collective-permute-start.15) | collective-permute-done | bytes 65568 | tf_op jit(solution)/shard_map/ppermute | solution.py:242
  42.1 0.0 collective-permute-done.16.refs_7_
  42.1 0.7 %collective-permute-done.14.refs_5_ = bf16[2,16,1024]{2,1,0:T(8,128)(2,1)S(1)} collective-permute-done((bf16[2,16,1024]{2,1,0:T(8,128)(2,1)S(1)}, bf16[2,16,1024]{2,1,0:T(8,128)(2,1)S(1)}, u32[]{:S(2)}, u32[]{:S(2)}) %collective-permute-start.14) | collective-permute-done | bytes 65568 | tf_op jit(solution)/shard_map/ppermute | solution.py:242
  42.8 0.0 copy-done
  42.8 0.8 %shard_map.69 = f32[2,32,1024]{2,1,0:T(8,128)} custom-call(f32[2,32,1024]{2,1,0:T(8,128)S(1)} %copy-done, f32[32,128]{1,0:T(8,128)S(1)} %get-tuple-element.43.scale_ref, s32[16,128]{1,0:T(8,128)S(1)} %get-tuple-element.44.odd_ref, f32[2,16,1024]{2,1,0:T(8,128)S(1)} %get-tuple-element.47.refs_0_, bf16[2,16,1024]{2,1,0:T(8,128)(2,1)S(1)} %collective-permute-done.9.refs_1_, ...), custom_call_target="tpu_custom_call" | custom-call | flops 1000000 | bytes 1048576 | tf_op jit(solution)/shard_map/pallas_call | solution.py:306
  (8 shorter events, 0.2 us)
Async XLA Ops:
  0.0 20.8 %copy-start.1 = (bf16[8,2,32,1024]{3,2,1,0:T(8,128)(2,1)S(1)}, bf16[8,2,32,1024]{3,2,1,0:T(8,128)(2,1)}, u32[]{:S(2)}) copy-start(bf16[8,2,32,1024]{3,2,1,0:T(8,128)(2,1)} %param.7) | copy-start | bytes 3145732
  1.1 7.7 %collective-permute-start.2 = (bf16[2,16,1024]{2,1,0:T(8,128)(2,1)S(1)}, bf16[2,16,1024]{2,1,0:T(8,128)(2,1)S(1)}, u32[]{:S(2)}, u32[]{:S(2)}) collective-permute-start(bf16[2,16,1024]{2,1,0:T(8,128)(2,1)S(1)} %get-tuple-element.62), channel_id=1, source_target_pairs={{0,3},{1,2},{2,1},{3,0},{4,7},{5,6},{6,5},{7,4},{8,11},{9,10},{10,... | collective-permute-start | bytes 196616 | tf_op jit(solution)/shard_map/ppermute | solution.py:242
  6.2 7.4 %collective-permute-start.1 = (bf16[2,16,1024]{2,1,0:T(8,128)(2,1)S(1)}, bf16[2,16,1024]{2,1,0:T(8,128)(2,1)S(1)}, u32[]{:S(2)}, u32[]{:S(2)}) collective-permute-start(bf16[2,16,1024]{2,1,0:T(8,128)(2,1)S(1)} %get-tuple-element.62), channel_id=1, source_target_pairs={{0,2},{1,3},{2,0},{3,1},{4,6},{5,7},{6,4},{7,5},{8,10},{9,11},{10,... | collective-permute-start | bytes 196616 | tf_op jit(solution)/shard_map/ppermute | solution.py:242
  6.2 7.4 %collective-permute-start = (bf16[2,16,1024]{2,1,0:T(8,128)(2,1)S(1)}, bf16[2,16,1024]{2,1,0:T(8,128)(2,1)S(1)}, u32[]{:S(2)}, u32[]{:S(2)}) collective-permute-start(bf16[2,16,1024]{2,1,0:T(8,128)(2,1)S(1)} %get-tuple-element.62), channel_id=1, source_target_pairs={{0,1},{1,0},{2,3},{3,2},{4,5},{5,4},{6,7},{7,6},{8,9},{9,8},{10,11... | collective-permute-start | bytes 196616 | tf_op jit(solution)/shard_map/ppermute | solution.py:242
  8.8 8.2 %collective-permute-start.6 = (bf16[2,16,1024]{2,1,0:T(8,128)(2,1)S(1)}, bf16[2,16,1024]{2,1,0:T(8,128)(2,1)S(1)}, u32[]{:S(2)}, u32[]{:S(2)}) collective-permute-start(bf16[2,16,1024]{2,1,0:T(8,128)(2,1)S(1)} %get-tuple-element.36), channel_id=1, source_target_pairs={{0,3},{1,2},{2,1},{3,0},{4,7},{5,6},{6,5},{7,4},{8,11},{9,10},{10,... | collective-permute-start | bytes 196616 | tf_op jit(solution)/shard_map/ppermute | solution.py:242
  13.0 5.3 %collective-permute-start.5 = (bf16[2,16,1024]{2,1,0:T(8,128)(2,1)S(1)}, bf16[2,16,1024]{2,1,0:T(8,128)(2,1)S(1)}, u32[]{:S(2)}, u32[]{:S(2)}) collective-permute-start(bf16[2,16,1024]{2,1,0:T(8,128)(2,1)S(1)} %get-tuple-element.36), channel_id=1, source_target_pairs={{0,2},{1,3},{2,0},{3,1},{4,6},{5,7},{6,4},{7,5},{8,10},{9,11},{10,... | collective-permute-start | bytes 196616 | tf_op jit(solution)/shard_map/ppermute | solution.py:242
  13.0 5.3 %collective-permute-start.4 = (bf16[2,16,1024]{2,1,0:T(8,128)(2,1)S(1)}, bf16[2,16,1024]{2,1,0:T(8,128)(2,1)S(1)}, u32[]{:S(2)}, u32[]{:S(2)}) collective-permute-start(bf16[2,16,1024]{2,1,0:T(8,128)(2,1)S(1)} %get-tuple-element.36), channel_id=1, source_target_pairs={{0,1},{1,0},{2,3},{3,2},{4,5},{5,4},{6,7},{7,6},{8,9},{9,8},{10,11... | collective-permute-start | bytes 196616 | tf_op jit(solution)/shard_map/ppermute | solution.py:242
  13.6 7.2 %collective-permute-start.3 = (bf16[8,16,1024]{2,1,0:T(8,128)(2,1)S(1)}, bf16[8,16,1024]{2,1,0:T(8,128)(2,1)S(1)}, u32[]{:S(2)}, u32[]{:S(2)}) collective-permute-start(bf16[8,16,1024]{2,1,0:T(8,128)(2,1)S(1)} %pad_maximum_fusion.refs_1_), channel_id=1, source_target_pairs={{0,1},{4,8},{8,4},{12,16},{16,12},{20,24},{24,20},{28,29},{1,0},{5... | collective-permute-start | bytes 786440 | tf_op jit(solution)/shard_map/ppermute | solution.py:252
  18.4 2.4 %collective-permute-start.7 = (bf16[8,16,1024]{2,1,0:T(8,128)(2,1)S(1)}, bf16[8,16,1024]{2,1,0:T(8,128)(2,1)S(1)}, u32[]{:S(2)}, u32[]{:S(2)}) collective-permute-start(bf16[8,16,1024]{2,1,0:T(8,128)(2,1)S(1)} %constant_dynamic-update-slice_fusion.refs_2_), channel_id=1, source_target_pairs={{0,4},{4,0},{8,12},{12,8},{16,20},{20,16},{24,28},{28,24},{1,5},{5... | collective-permute-start | bytes 786440 | tf_op jit(solution)/shard_map/ppermute | solution.py:255
  20.8 22.0 %copy-start = (f32[2,32,1024]{2,1,0:T(8,128)S(1)}, f32[2,32,1024]{2,1,0:T(8,128)}, u32[]{:S(2)}) copy-start(f32[2,32,1024]{2,1,0:T(8,128)} %estimate_ref.1) | copy-start | bytes 786436
  24.1 3.2 %collective-permute-start.8 = (bf16[8,16,1024]{2,1,0:T(8,128)(2,1)S(1)}, bf16[8,16,1024]{2,1,0:T(8,128)(2,1)S(1)}, u32[]{:S(2)}, u32[]{:S(2)}) collective-permute-start(bf16[8,16,1024]{2,1,0:T(8,128)(2,1)S(1)} %get-tuple-element.46), channel_id=1, source_target_pairs={{0,4},{4,0},{8,12},{12,8},{16,20},{20,16},{24,28},{28,24},{1,5},{5... | collective-permute-start | bytes 786440 | tf_op jit(solution)/shard_map/ppermute | solution.py:255
  24.6 7.7 %collective-permute-start.12 = (bf16[4,16,1024]{2,1,0:T(8,128)(2,1)S(1)}, bf16[4,16,1024]{2,1,0:T(8,128)(2,1)S(1)}, u32[]{:S(2)}, u32[]{:S(2)}) collective-permute-start(bf16[4,16,1024]{2,1,0:T(8,128)(2,1)S(1)} %get-tuple-element.54), channel_id=1, source_target_pairs={{0,28},{4,8},{8,4},{12,16},{16,12},{20,24},{24,20},{28,0},{1,29},{... | collective-permute-start | bytes 393224 | tf_op jit(solution)/shard_map/ppermute | solution.py:252
  27.3 11.1 %collective-permute-start.13 = (bf16[4,16,1024]{2,1,0:T(8,128)(2,1)S(1)}, bf16[4,16,1024]{2,1,0:T(8,128)(2,1)S(1)}, u32[]{:S(2)}, u32[]{:S(2)}) collective-permute-start(bf16[4,16,1024]{2,1,0:T(8,128)(2,1)S(1)} %get-tuple-element.58), channel_id=1, source_target_pairs={{0,28},{4,8},{8,4},{12,16},{16,12},{20,24},{24,20},{28,0},{1,29},{... | collective-permute-start | bytes 393224 | tf_op jit(solution)/shard_map/ppermute | solution.py:252
  27.4 4.9 %collective-permute-start.9 = (bf16[2,16,1024]{2,1,0:T(8,128)(2,1)S(1)}, bf16[2,16,1024]{2,1,0:T(8,128)(2,1)S(1)}, u32[]{:S(2)}, u32[]{:S(2)}) collective-permute-start(bf16[2,16,1024]{2,1,0:T(8,128)(2,1)S(1)} %get-tuple-element.48), channel_id=1, source_target_pairs={{0,1},{1,0},{2,3},{3,2},{4,5},{5,4},{6,7},{7,6},{8,9},{9,8},{10,11... | collective-permute-start | bytes 196616 | tf_op jit(solution)/shard_map/ppermute | solution.py:242
  28.9 9.5 %collective-permute-start.10 = (bf16[2,16,1024]{2,1,0:T(8,128)(2,1)S(1)}, bf16[2,16,1024]{2,1,0:T(8,128)(2,1)S(1)}, u32[]{:S(2)}, u32[]{:S(2)}) collective-permute-start(bf16[2,16,1024]{2,1,0:T(8,128)(2,1)S(1)} %get-tuple-element.49), channel_id=1, source_target_pairs={{0,2},{1,3},{2,0},{3,1},{4,6},{5,7},{6,4},{7,5},{8,10},{9,11},{10,... | collective-permute-start | bytes 196616 | tf_op jit(solution)/shard_map/ppermute | solution.py:242
  31.8 6.9 %collective-permute-start.11 = (bf16[2,16,1024]{2,1,0:T(8,128)(2,1)S(1)}, bf16[2,16,1024]{2,1,0:T(8,128)(2,1)S(1)}, u32[]{:S(2)}, u32[]{:S(2)}) collective-permute-start(bf16[2,16,1024]{2,1,0:T(8,128)(2,1)S(1)} %get-tuple-element.50), channel_id=1, source_target_pairs={{0,3},{1,2},{2,1},{3,0},{4,7},{5,6},{6,5},{7,4},{8,11},{9,10},{10,... | collective-permute-start | bytes 196616 | tf_op jit(solution)/shard_map/ppermute | solution.py:242
  32.3 9.8 %collective-permute-start.15 = (bf16[2,16,1024]{2,1,0:T(8,128)(2,1)S(1)}, bf16[2,16,1024]{2,1,0:T(8,128)(2,1)S(1)}, u32[]{:S(2)}, u32[]{:S(2)}) collective-permute-start(bf16[2,16,1024]{2,1,0:T(8,128)(2,1)S(1)} %get-tuple-element.55), channel_id=1, source_target_pairs={{0,2},{1,3},{2,0},{3,1},{4,6},{5,7},{6,4},{7,5},{8,10},{9,11},{10,... | collective-permute-start | bytes 196616 | tf_op jit(solution)/shard_map/ppermute | solution.py:242
  34.2 7.9 %collective-permute-start.16 = (bf16[2,16,1024]{2,1,0:T(8,128)(2,1)S(1)}, bf16[2,16,1024]{2,1,0:T(8,128)(2,1)S(1)}, u32[]{:S(2)}, u32[]{:S(2)}) collective-permute-start(bf16[2,16,1024]{2,1,0:T(8,128)(2,1)S(1)} %get-tuple-element.56), channel_id=1, source_target_pairs={{0,3},{1,2},{2,1},{3,0},{4,7},{5,6},{6,5},{7,4},{8,11},{9,10},{10,... | collective-permute-start | bytes 196616 | tf_op jit(solution)/shard_map/ppermute | solution.py:242
  38.4 4.4 %collective-permute-start.14 = (bf16[2,16,1024]{2,1,0:T(8,128)(2,1)S(1)}, bf16[2,16,1024]{2,1,0:T(8,128)(2,1)S(1)}, u32[]{:S(2)}, u32[]{:S(2)}) collective-permute-start(bf16[2,16,1024]{2,1,0:T(8,128)(2,1)S(1)} %get-tuple-element.60), channel_id=1, source_target_pairs={{0,1},{1,0},{2,3},{3,2},{4,5},{5,4},{6,7},{7,6},{8,9},{9,8},{10,11... | collective-permute-start | bytes 196616 | tf_op jit(solution)/shard_map/ppermute | solution.py:242

commit v7 on v6

--- a/solution.py
+++ b/solution.py
@@ -301,7 +301,7 @@
 
     far_edge = beside(far_edge, False)
     totals, sums = joined(core, within(to_core), 0)
-    totals, far = joined(far, far_edge, depth // 2, [totals, sums[1]])
+    totals, far = joined(far, far_edge, depth // 2, [totals, sums[depth - 1]])
     sums += joined(near, beside(near_edge, False), 0, [totals, sums[2]])[1] + far
     return call(
         update_kernel,

time: 44.1 us -> 46.6 us (1.057)
  waiting for transfers between devices: 11.1 us -> 13.3 us
  starting transfers between devices: 23.6 us -> 24.3 us
    ppermute x12, waiting for transfers between devices: 8.79 us -> 10.9 us  [across(): return lax.ppermute(array, 'depth', [(i, i ^ step) for i in range(depth)])]
    ppermute x12, starting transfers between devices: 18.8 us -> 19.5 us  [across(): return lax.ppermute(array, 'depth', [(i, i ^ step) for i in range(depth)])]
  transfers between devices with their start and end apart: 17 -> 17, of which waited for: 7 -> 7; matrix products, arithmetic and copies ran while one was open for 3% -> 3% of each run, Pallas kernels for 5% -> 4%
where the time goes in v7:
time: 46.6 us; the launch traced here: 46.4 us
  starting transfers between devices  24.3 us (52%)
  waiting for transfers between devices  13.3 us (29%)
  Pallas kernels  6.18 us (13%)
  other arithmetic  1.83 us (4%)
  local copies, waits for them, and re-layouts  0.77 us (2%)
    ppermute x12, starting transfers between devices, across(): return lax.ppermute(array, 'depth', [(i, i ^ step) for i in range(depth)])  19.5 us
    ppermute x12, waiting for transfers between devices, across(): return lax.ppermute(array, 'depth', [(i, i ^ step) for i in range(depth)])  10.9 us
    ppermute x3, starting transfers between devices, beside(): return lax.ppermute(array, ('tile', 'depth'), pairs)  4.24 us
    pallas_call x1, Pallas kernels, shards(): call(functools.partial(main_kernel, planes, view_rows), (shape(halves, F3...  3.31 us
    ppermute x3, waiting for transfers between devices, beside(): return lax.ppermute(array, ('tile', 'depth'), pairs)  2.31 us
    pallas_call x1, Pallas kernels, shards(): call(functools.partial(matrices_kernel, planes, strip), (shape((rows, spa...  1.88 us
    convert_element_type x1, other arithmetic, shards(): own = estimate.astype(BF16)  1.05 us
  transfers between devices with their start and end apart: 17, of which 7 were waited for; matrix products, arithmetic and copies ran while one was open for 3% of the time, Pallas kernels for 4%

profile of v7, /device:TPU:0, one launch (start us, length us, event | category | flops | bytes accessed | tf_op | source)
XLA Modules:
  0.0 46.4 jit_solution(17828894927387073177)
XLA Ops:
  0.0 0.0 copy-start.1
  0.0 1.1 %convert_element_type.4 = bf16[2,32,1024]{2,1,0:T(8,128)(2,1)S(1)} convert(f32[2,32,1024]{2,1,0:T(8,128)} %estimate_ref.1) | non-fusion elementwise | flops 65536 | bytes 393216 | tf_op jit(solution)/shard_map/convert_element_type | solution.py:257
  1.1 5.1 %collective-permute-start.2 = (bf16[2,16,1024]{2,1,0:T(8,128)(2,1)S(1)}, bf16[2,16,1024]{2,1,0:T(8,128)(2,1)S(1)}, u32[]{:S(2)}, u32[]{:S(2)}) collective-permute-start(bf16[2,16,1024]{2,1,0:T(8,128)(2,1)S(1)} %get-tuple-element.62), channel_id=1, source_target_pairs={{0,3},{1,2},{2,1},{3,0},{4,7},{5,6},{6,5},{7,4},{8,11},{9,10},{10,... | collective-permute-start | bytes 196616 | tf_op jit(solution)/shard_map/ppermute | solution.py:242
  6.2 0.0 collective-permute-start.1
  6.2 0.6 %collective-permute-start = (bf16[2,16,1024]{2,1,0:T(8,128)(2,1)S(1)}, bf16[2,16,1024]{2,1,0:T(8,128)(2,1)S(1)}, u32[]{:S(2)}, u32[]{:S(2)}) collective-permute-start(bf16[2,16,1024]{2,1,0:T(8,128)(2,1)S(1)} %get-tuple-element.62), channel_id=1, source_target_pairs={{0,1},{1,0},{2,3},{3,2},{4,5},{5,4},{6,7},{7,6},{8,9},{9,8},{10,11... | collective-permute-start | bytes 196616 | tf_op jit(solution)/shard_map/ppermute | solution.py:242
  6.8 0.7 %concatenate.9.device_ref.info_ref = s32[12]{0:T(128)S(1)} concatenate(s32[1]{0:T(128)} %bitcast, s32[1]{0:T(128)} %bitcast.1, s32[1]{0:T(128)} %bitcast.2, s32[1]{0:T(128)} %bitcast.3, s32[8]{0:T(128)} %param.11), dimensions={0} | concatenate | bytes 96 | tf_op jit(solution)/shard_map/concatenate | solution.py:238
  7.6 0.7 %pad_maximum_fusion.1.kernels_ref = f32[3,8,31]{2,1,0:T(8,128)S(1)} fusion(f32[1,8,31]{2,1,0:T(8,128)} %bitcast.9, f32[1,8,31]{2,1,0:T(8,128)} %bitcast.10, f32[1,8,31]{2,1,0:T(8,128)} %bitcast.11), kind=kLoop, calls=%fused_computation.3 | loop fusion | flops 1488 | bytes 5952 | tf_op jit(solution)/shard_map/stack | solution.py:264
  8.3 0.5 %collective-permute-done.2 = bf16[2,16,1024]{2,1,0:T(8,128)(2,1)S(1)} collective-permute-done((bf16[2,16,1024]{2,1,0:T(8,128)(2,1)S(1)}, bf16[2,16,1024]{2,1,0:T(8,128)(2,1)S(1)}, u32[]{:S(2)}, u32[]{:S(2)}) %collective-permute-start.2) | collective-permute-done | bytes 65568 | tf_op jit(solution)/shard_map/ppermute | solution.py:242
  8.8 4.2 %collective-permute-start.6 = (bf16[2,16,1024]{2,1,0:T(8,128)(2,1)S(1)}, bf16[2,16,1024]{2,1,0:T(8,128)(2,1)S(1)}, u32[]{:S(2)}, u32[]{:S(2)}) collective-permute-start(bf16[2,16,1024]{2,1,0:T(8,128)(2,1)S(1)} %get-tuple-element.36), channel_id=1, source_target_pairs={{0,3},{1,2},{2,1},{3,0},{4,7},{5,6},{6,5},{7,4},{8,11},{9,10},{10,... | collective-permute-start | bytes 196616 | tf_op jit(solution)/shard_map/ppermute | solution.py:242
  13.0 0.0 collective-permute-start.5
  13.0 0.6 %collective-permute-start.4 = (bf16[2,16,1024]{2,1,0:T(8,128)(2,1)S(1)}, bf16[2,16,1024]{2,1,0:T(8,128)(2,1)S(1)}, u32[]{:S(2)}, u32[]{:S(2)}) collective-permute-start(bf16[2,16,1024]{2,1,0:T(8,128)(2,1)S(1)} %get-tuple-element.36), channel_id=1, source_target_pairs={{0,1},{1,0},{2,3},{3,2},{4,5},{5,4},{6,7},{7,6},{8,9},{9,8},{10,11... | collective-permute-start | bytes 196616 | tf_op jit(solution)/shard_map/ppermute | solution.py:242
  13.5 0.0 collective-permute-done.1
  13.5 0.0 collective-permute-done
  13.6 1.5 %collective-permute-start.3 = (bf16[8,16,1024]{2,1,0:T(8,128)(2,1)S(1)}, bf16[8,16,1024]{2,1,0:T(8,128)(2,1)S(1)}, u32[]{:S(2)}, u32[]{:S(2)}) collective-permute-start(bf16[8,16,1024]{2,1,0:T(8,128)(2,1)S(1)} %pad_maximum_fusion.refs_1_), channel_id=1, source_target_pairs={{0,1},{4,8},{8,4},{12,16},{16,12},{20,24},{24,20},{28,29},{1,0},{5... | collective-permute-start | bytes 786440 | tf_op jit(solution)/shard_map/ppermute | solution.py:252
  15.1 1.9 %shard_map.64 = (bf16[512,512]{1,0:T(8,128)(2,1)S(1)}, bf16[512,512]{1,0:T(8,128)(2,1)S(1)}, bf16[8,512,256]{2,1,0:T(8,128)(2,1)S(1)}, bf16[8,512,256]{2,1,0:T(8,128)(2,1)S(1)}) custom-call(s32[12]{0:T(128)S(1)} %concatenate.9.device_ref.info_ref, f32[3,8,31]{2,1,0:T(8,128)S(1)} %pad_maximum_fusion.1.kernels_ref), custom_call_target="tpu_custom_call" | custom-call | flops 100000000 | bytes 5242880 | tf_op jit(solution)/shard_map/pallas_call | solution.py:265
  17.0 0.0 collective-permute-done.6
  17.0 1.3 %collective-permute-done.5 = bf16[2,16,1024]{2,1,0:T(8,128)(2,1)S(1)} collective-permute-done((bf16[2,16,1024]{2,1,0:T(8,128)(2,1)S(1)}, bf16[2,16,1024]{2,1,0:T(8,128)(2,1)S(1)}, u32[]{:S(2)}, u32[]{:S(2)}) %collective-permute-start.5) | collective-permute-done | bytes 65568 | tf_op jit(solution)/shard_map/ppermute | solution.py:242
  18.3 0.0 collective-permute-done.4
  18.4 0.1 collective-permute-start.7
  18.5 2.3 %collective-permute-done.3.refs_0_ = bf16[8,16,1024]{2,1,0:T(8,128)(2,1)S(1)} collective-permute-done((bf16[8,16,1024]{2,1,0:T(8,128)(2,1)S(1)}, bf16[8,16,1024]{2,1,0:T(8,128)(2,1)S(1)}, u32[]{:S(2)}, u32[]{:S(2)}) %collective-permute-start.3) | collective-permute-done | bytes 262176 | tf_op jit(solution)/shard_map/ppermute | solution.py:252
  20.8 0.0 collective-permute-done.7.refs_3_
  20.8 0.0 copy-done.1
  20.8 0.0 copy-start
  20.8 3.3 %shard_map.65 = (f32[8,16,1024]{2,1,0:T(8,128)S(1)}, bf16[8,16,1024]{2,1,0:T(8,128)(2,1)S(1)}, f32[4,16,1024]{2,1,0:T(8,128)S(1)}, f32[4,16,1024]{2,1,0:T(8,128)...) custom-call(s32[12]{0:T(128)S(1)} %concatenate.9.device_ref.info_ref, ...), custom_call_target="tpu_custom_call" | custom-call | flops 2000000000 | bytes 10485760 | tf_op jit(solution)/shard_map/pallas_call | solution.py:277
  24.1 0.5 %collective-permute-start.8 = (bf16[8,16,1024]{2,1,0:T(8,128)(2,1)S(1)}, bf16[8,16,1024]{2,1,0:T(8,128)(2,1)S(1)}, u32[]{:S(2)}, u32[]{:S(2)}) collective-permute-start(bf16[8,16,1024]{2,1,0:T(8,128)(2,1)S(1)} %get-tuple-element.46), channel_id=1, source_target_pairs={{0,4},{4,0},{8,12},{12,8},{16,20},{20,16},{24,28},{28,24},{1,5},{5... | collective-permute-start | bytes 786440 | tf_op jit(solution)/shard_map/ppermute | solution.py:255
  24.6 2.7 %collective-permute-start.12 = (bf16[4,16,1024]{2,1,0:T(8,128)(2,1)S(1)}, bf16[4,16,1024]{2,1,0:T(8,128)(2,1)S(1)}, u32[]{:S(2)}, u32[]{:S(2)}) collective-permute-start(bf16[4,16,1024]{2,1,0:T(8,128)(2,1)S(1)} %get-tuple-element.54), channel_id=1, source_target_pairs={{0,28},{4,8},{8,4},{12,16},{16,12},{20,24},{24,20},{28,0},{1,29},{... | collective-permute-start | bytes 393224 | tf_op jit(solution)/shard_map/ppermute | solution.py:252
  27.3 0.0 collective-permute-start.13
  27.3 0.0 collective-permute-done.8.other_ref
  27.3 0.1 shard_map.66
  27.4 3.9 %collective-permute-start.11 = (bf16[2,16,1024]{2,1,0:T(8,128)(2,1)S(1)}, bf16[2,16,1024]{2,1,0:T(8,128)(2,1)S(1)}, u32[]{:S(2)}, u32[]{:S(2)}) collective-permute-start(bf16[2,16,1024]{2,1,0:T(8,128)(2,1)S(1)} %get-tuple-element.50), channel_id=1, source_target_pairs={{0,3},{1,2},{2,1},{3,0},{4,7},{5,6},{6,5},{7,4},{8,11},{9,10},{10,... | collective-permute-start | bytes 196616 | tf_op jit(solution)/shard_map/ppermute | solution.py:242
  31.3 0.0 collective-permute-start.10
  31.3 0.6 %collective-permute-start.9 = (bf16[2,16,1024]{2,1,0:T(8,128)(2,1)S(1)}, bf16[2,16,1024]{2,1,0:T(8,128)(2,1)S(1)}, u32[]{:S(2)}, u32[]{:S(2)}) collective-permute-start(bf16[2,16,1024]{2,1,0:T(8,128)(2,1)S(1)} %get-tuple-element.48), channel_id=1, source_target_pairs={{0,1},{1,0},{2,3},{3,2},{4,5},{5,4},{6,7},{7,6},{8,9},{9,8},{10,11... | collective-permute-start | bytes 196616 | tf_op jit(solution)/shard_map/ppermute | solution.py:242
  31.9 1.8 %collective-permute-done.11.refs_3_ = bf16[2,16,1024]{2,1,0:T(8,128)(2,1)S(1)} collective-permute-done((bf16[2,16,1024]{2,1,0:T(8,128)(2,1)S(1)}, bf16[2,16,1024]{2,1,0:T(8,128)(2,1)S(1)}, u32[]{:S(2)}, u32[]{:S(2)}) %collective-permute-start.11) | collective-permute-done | bytes 65568 | tf_op jit(solution)/shard_map/ppermute | solution.py:242
  33.7 0.0 collective-permute-done.12.other_ref
  33.7 2.8 %collective-permute-done.10.refs_2_ = bf16[2,16,1024]{2,1,0:T(8,128)(2,1)S(1)} collective-permute-done((bf16[2,16,1024]{2,1,0:T(8,128)(2,1)S(1)}, bf16[2,16,1024]{2,1,0:T(8,128)(2,1)S(1)}, u32[]{:S(2)}, u32[]{:S(2)}) %collective-permute-start.10) | collective-permute-done | bytes 65568 | tf_op jit(solution)/shard_map/ppermute | solution.py:242
  36.5 0.0 collective-permute-done.13.other_ref
  36.5 0.1 collective-permute-start.14
  36.6 2.9 %collective-permute-start.15 = (bf16[2,16,1024]{2,1,0:T(8,128)(2,1)S(1)}, bf16[2,16,1024]{2,1,0:T(8,128)(2,1)S(1)}, u32[]{:S(2)}, u32[]{:S(2)}) collective-permute-start(bf16[2,16,1024]{2,1,0:T(8,128)(2,1)S(1)} %get-tuple-element.55), channel_id=1, source_target_pairs={{0,2},{1,3},{2,0},{3,1},{4,6},{5,7},{6,4},{7,5},{8,10},{9,11},{10,... | collective-permute-start | bytes 196616 | tf_op jit(solution)/shard_map/ppermute | solution.py:242
  39.6 1.4 %collective-permute-start.16 = (bf16[2,16,1024]{2,1,0:T(8,128)(2,1)S(1)}, bf16[2,16,1024]{2,1,0:T(8,128)(2,1)S(1)}, u32[]{:S(2)}, u32[]{:S(2)}) collective-permute-start(bf16[2,16,1024]{2,1,0:T(8,128)(2,1)S(1)} %get-tuple-element.56), channel_id=1, source_target_pairs={{0,3},{1,2},{2,1},{3,0},{4,7},{5,6},{6,5},{7,4},{8,11},{9,10},{10,... | collective-permute-start | bytes 196616 | tf_op jit(solution)/shard_map/ppermute | solution.py:242
  41.0 0.0 collective-permute-done.9.refs_1_
  41.0 0.0 collective-permute-done.14.refs_5_
  41.0 2.3 %collective-permute-done.15.refs_6_ = bf16[2,16,1024]{2,1,0:T(8,128)(2,1)S(1)} collective-permute-done((bf16[2,16,1024]{2,1,0:T(8,128)(2,1)S(1)}, bf16[2,16,1024]{2,1,0:T(8,128)(2,1)S(1)}, u32[]{:S(2)}, u32[]{:S(2)}) %collective-permute-start.15) | collective-permute-done | bytes 65568 | tf_op jit(solution)/shard_map/ppermute | solution.py:242
  43.3 2.3 %collective-permute-done.16.refs_7_ = bf16[2,16,1024]{2,1,0:T(8,128)(2,1)S(1)} collective-permute-done((bf16[2,16,1024]{2,1,0:T(8,128)(2,1)S(1)}, bf16[2,16,1024]{2,1,0:T(8,128)(2,1)S(1)}, u32[]{:S(2)}, u32[]{:S(2)}) %collective-permute-start.16) | collective-permute-done | bytes 65568 | tf_op jit(solution)/shard_map/ppermute | solution.py:242
  45.6 0.0 copy-done
  45.6 0.8 %shard_map.69 = f32[2,32,1024]{2,1,0:T(8,128)} custom-call(f32[2,32,1024]{2,1,0:T(8,128)S(1)} %copy-done, f32[32,128]{1,0:T(8,128)S(1)} %get-tuple-element.43.scale_ref, s32[16,128]{1,0:T(8,128)S(1)} %get-tuple-element.44.odd_ref, f32[2,16,1024]{2,1,0:T(8,128)S(1)} %get-tuple-element.47.refs_0_, bf16[2,16,1024]{2,1,0:T(8,128)(2,1)S(1)} %collective-permute-done.9.refs_1_, ...), custom_call_target="tpu_custom_call" | custom-call | flops 1000000 | bytes 1048576 | tf_op jit(solution)/shard_map/pallas_call | solution.py:306
  (8 shorter events, 0.2 us)
Async XLA Ops:
  0.0 20.8 %copy-start.1 = (bf16[8,2,32,1024]{3,2,1,0:T(8,128)(2,1)S(1)}, bf16[8,2,32,1024]{3,2,1,0:T(8,128)(2,1)}, u32[]{:S(2)}) copy-start(bf16[8,2,32,1024]{3,2,1,0:T(8,128)(2,1)} %param.7) | copy-start | bytes 3145732
  1.1 7.7 %collective-permute-start.2 = (bf16[2,16,1024]{2,1,0:T(8,128)(2,1)S(1)}, bf16[2,16,1024]{2,1,0:T(8,128)(2,1)S(1)}, u32[]{:S(2)}, u32[]{:S(2)}) collective-permute-start(bf16[2,16,1024]{2,1,0:T(8,128)(2,1)S(1)} %get-tuple-element.62), channel_id=1, source_target_pairs={{0,3},{1,2},{2,1},{3,0},{4,7},{5,6},{6,5},{7,4},{8,11},{9,10},{10,... | collective-permute-start | bytes 196616 | tf_op jit(solution)/shard_map/ppermute | solution.py:242
  6.2 7.4 %collective-permute-start.1 = (bf16[2,16,1024]{2,1,0:T(8,128)(2,1)S(1)}, bf16[2,16,1024]{2,1,0:T(8,128)(2,1)S(1)}, u32[]{:S(2)}, u32[]{:S(2)}) collective-permute-start(bf16[2,16,1024]{2,1,0:T(8,128)(2,1)S(1)} %get-tuple-element.62), channel_id=1, source_target_pairs={{0,2},{1,3},{2,0},{3,1},{4,6},{5,7},{6,4},{7,5},{8,10},{9,11},{10,... | collective-permute-start | bytes 196616 | tf_op jit(solution)/shard_map/ppermute | solution.py:242
  6.2 7.4 %collective-permute-start = (bf16[2,16,1024]{2,1,0:T(8,128)(2,1)S(1)}, bf16[2,16,1024]{2,1,0:T(8,128)(2,1)S(1)}, u32[]{:S(2)}, u32[]{:S(2)}) collective-permute-start(bf16[2,16,1024]{2,1,0:T(8,128)(2,1)S(1)} %get-tuple-element.62), channel_id=1, source_target_pairs={{0,1},{1,0},{2,3},{3,2},{4,5},{5,4},{6,7},{7,6},{8,9},{9,8},{10,11... | collective-permute-start | bytes 196616 | tf_op jit(solution)/shard_map/ppermute | solution.py:242
  8.8 8.2 %collective-permute-start.6 = (bf16[2,16,1024]{2,1,0:T(8,128)(2,1)S(1)}, bf16[2,16,1024]{2,1,0:T(8,128)(2,1)S(1)}, u32[]{:S(2)}, u32[]{:S(2)}) collective-permute-start(bf16[2,16,1024]{2,1,0:T(8,128)(2,1)S(1)} %get-tuple-element.36), channel_id=1, source_target_pairs={{0,3},{1,2},{2,1},{3,0},{4,7},{5,6},{6,5},{7,4},{8,11},{9,10},{10,... | collective-permute-start | bytes 196616 | tf_op jit(solution)/shard_map/ppermute | solution.py:242
  13.0 5.3 %collective-permute-start.5 = (bf16[2,16,1024]{2,1,0:T(8,128)(2,1)S(1)}, bf16[2,16,1024]{2,1,0:T(8,128)(2,1)S(1)}, u32[]{:S(2)}, u32[]{:S(2)}) collective-permute-start(bf16[2,16,1024]{2,1,0:T(8,128)(2,1)S(1)} %get-tuple-element.36), channel_id=1, source_target_pairs={{0,2},{1,3},{2,0},{3,1},{4,6},{5,7},{6,4},{7,5},{8,10},{9,11},{10,... | collective-permute-start | bytes 196616 | tf_op jit(solution)/shard_map/ppermute | solution.py:242
  13.0 5.3 %collective-permute-start.4 = (bf16[2,16,1024]{2,1,0:T(8,128)(2,1)S(1)}, bf16[2,16,1024]{2,1,0:T(8,128)(2,1)S(1)}, u32[]{:S(2)}, u32[]{:S(2)}) collective-permute-start(bf16[2,16,1024]{2,1,0:T(8,128)(2,1)S(1)} %get-tuple-element.36), channel_id=1, source_target_pairs={{0,1},{1,0},{2,3},{3,2},{4,5},{5,4},{6,7},{7,6},{8,9},{9,8},{10,11... | collective-permute-start | bytes 196616 | tf_op jit(solution)/shard_map/ppermute | solution.py:242
  13.6 7.2 %collective-permute-start.3 = (bf16[8,16,1024]{2,1,0:T(8,128)(2,1)S(1)}, bf16[8,16,1024]{2,1,0:T(8,128)(2,1)S(1)}, u32[]{:S(2)}, u32[]{:S(2)}) collective-permute-start(bf16[8,16,1024]{2,1,0:T(8,128)(2,1)S(1)} %pad_maximum_fusion.refs_1_), channel_id=1, source_target_pairs={{0,1},{4,8},{8,4},{12,16},{16,12},{20,24},{24,20},{28,29},{1,0},{5... | collective-permute-start | bytes 786440 | tf_op jit(solution)/shard_map/ppermute | solution.py:252
  18.4 2.4 %collective-permute-start.7 = (bf16[8,16,1024]{2,1,0:T(8,128)(2,1)S(1)}, bf16[8,16,1024]{2,1,0:T(8,128)(2,1)S(1)}, u32[]{:S(2)}, u32[]{:S(2)}) collective-permute-start(bf16[8,16,1024]{2,1,0:T(8,128)(2,1)S(1)} %constant_dynamic-update-slice_fusion.refs_2_), channel_id=1, source_target_pairs={{0,4},{4,0},{8,12},{12,8},{16,20},{20,16},{24,28},{28,24},{1,5},{5... | collective-permute-start | bytes 786440 | tf_op jit(solution)/shard_map/ppermute | solution.py:255
  20.8 24.9 %copy-start = (f32[2,32,1024]{2,1,0:T(8,128)S(1)}, f32[2,32,1024]{2,1,0:T(8,128)}, u32[]{:S(2)}) copy-start(f32[2,32,1024]{2,1,0:T(8,128)} %estimate_ref.1) | copy-start | bytes 786436
  24.1 3.2 %collective-permute-start.8 = (bf16[8,16,1024]{2,1,0:T(8,128)(2,1)S(1)}, bf16[8,16,1024]{2,1,0:T(8,128)(2,1)S(1)}, u32[]{:S(2)}, u32[]{:S(2)}) collective-permute-start(bf16[8,16,1024]{2,1,0:T(8,128)(2,1)S(1)} %get-tuple-element.46), channel_id=1, source_target_pairs={{0,4},{4,0},{8,12},{12,8},{16,20},{20,16},{24,28},{28,24},{1,5},{5... | collective-permute-start | bytes 786440 | tf_op jit(solution)/shard_map/ppermute | solution.py:255
  24.6 9.1 %collective-permute-start.12 = (bf16[4,16,1024]{2,1,0:T(8,128)(2,1)S(1)}, bf16[4,16,1024]{2,1,0:T(8,128)(2,1)S(1)}, u32[]{:S(2)}, u32[]{:S(2)}) collective-permute-start(bf16[4,16,1024]{2,1,0:T(8,128)(2,1)S(1)} %get-tuple-element.54), channel_id=1, source_target_pairs={{0,28},{4,8},{8,4},{12,16},{16,12},{20,24},{24,20},{28,0},{1,29},{... | collective-permute-start | bytes 393224 | tf_op jit(solution)/shard_map/ppermute | solution.py:252
  27.3 9.2 %collective-permute-start.13 = (bf16[4,16,1024]{2,1,0:T(8,128)(2,1)S(1)}, bf16[4,16,1024]{2,1,0:T(8,128)(2,1)S(1)}, u32[]{:S(2)}, u32[]{:S(2)}) collective-permute-start(bf16[4,16,1024]{2,1,0:T(8,128)(2,1)S(1)} %get-tuple-element.58), channel_id=1, source_target_pairs={{0,28},{4,8},{8,4},{12,16},{16,12},{20,24},{24,20},{28,0},{1,29},{... | collective-permute-start | bytes 393224 | tf_op jit(solution)/shard_map/ppermute | solution.py:252
  27.4 6.3 %collective-permute-start.11 = (bf16[2,16,1024]{2,1,0:T(8,128)(2,1)S(1)}, bf16[2,16,1024]{2,1,0:T(8,128)(2,1)S(1)}, u32[]{:S(2)}, u32[]{:S(2)}) collective-permute-start(bf16[2,16,1024]{2,1,0:T(8,128)(2,1)S(1)} %get-tuple-element.50), channel_id=1, source_target_pairs={{0,3},{1,2},{2,1},{3,0},{4,7},{5,6},{6,5},{7,4},{8,11},{9,10},{10,... | collective-permute-start | bytes 196616 | tf_op jit(solution)/shard_map/ppermute | solution.py:242
  31.3 5.2 %collective-permute-start.10 = (bf16[2,16,1024]{2,1,0:T(8,128)(2,1)S(1)}, bf16[2,16,1024]{2,1,0:T(8,128)(2,1)S(1)}, u32[]{:S(2)}, u32[]{:S(2)}) collective-permute-start(bf16[2,16,1024]{2,1,0:T(8,128)(2,1)S(1)} %get-tuple-element.49), channel_id=1, source_target_pairs={{0,2},{1,3},{2,0},{3,1},{4,6},{5,7},{6,4},{7,5},{8,10},{9,11},{10,... | collective-permute-start | bytes 196616 | tf_op jit(solution)/shard_map/ppermute | solution.py:242
  31.3 9.7 %collective-permute-start.9 = (bf16[2,16,1024]{2,1,0:T(8,128)(2,1)S(1)}, bf16[2,16,1024]{2,1,0:T(8,128)(2,1)S(1)}, u32[]{:S(2)}, u32[]{:S(2)}) collective-permute-start(bf16[2,16,1024]{2,1,0:T(8,128)(2,1)S(1)} %get-tuple-element.48), channel_id=1, source_target_pairs={{0,1},{1,0},{2,3},{3,2},{4,5},{5,4},{6,7},{7,6},{8,9},{9,8},{10,11... | collective-permute-start | bytes 196616 | tf_op jit(solution)/shard_map/ppermute | solution.py:242
  36.5 4.5 %collective-permute-start.14 = (bf16[2,16,1024]{2,1,0:T(8,128)(2,1)S(1)}, bf16[2,16,1024]{2,1,0:T(8,128)(2,1)S(1)}, u32[]{:S(2)}, u32[]{:S(2)}) collective-permute-start(bf16[2,16,1024]{2,1,0:T(8,128)(2,1)S(1)} %get-tuple-element.60), channel_id=1, source_target_pairs={{0,1},{1,0},{2,3},{3,2},{4,5},{5,4},{6,7},{7,6},{8,9},{9,8},{10,11... | collective-permute-start | bytes 196616 | tf_op jit(solution)/shard_map/ppermute | solution.py:242
  36.6 6.7 %collective-permute-start.15 = (bf16[2,16,1024]{2,1,0:T(8,128)(2,1)S(1)}, bf16[2,16,1024]{2,1,0:T(8,128)(2,1)S(1)}, u32[]{:S(2)}, u32[]{:S(2)}) collective-permute-start(bf16[2,16,1024]{2,1,0:T(8,128)(2,1)S(1)} %get-tuple-element.55), channel_id=1, source_target_pairs={{0,2},{1,3},{2,0},{3,1},{4,6},{5,7},{6,4},{7,5},{8,10},{9,11},{10,... | collective-permute-start | bytes 196616 | tf_op jit(solution)/shard_map/ppermute | solution.py:242
  39.6 6.1 %collective-permute-start.16 = (bf16[2,16,1024]{2,1,0:T(8,128)(2,1)S(1)}, bf16[2,16,1024]{2,1,0:T(8,128)(2,1)S(1)}, u32[]{:S(2)}, u32[]{:S(2)}) collective-permute-start(bf16[2,16,1024]{2,1,0:T(8,128)(2,1)S(1)} %get-tuple-element.56), channel_id=1, source_target_pairs={{0,3},{1,2},{2,1},{3,0},{4,7},{5,6},{6,5},{7,4},{8,11},{9,10},{10,... | collective-permute-start | bytes 196616 | tf_op jit(solution)/shard_map/ppermute | solution.py:242

commit v8 on v6

--- a/solution.py
+++ b/solution.py
@@ -302,7 +302,7 @@
     far_edge = beside(far_edge, False)
     totals, sums = joined(core, within(to_core), 0)
     totals, far = joined(far, far_edge, depth // 2, [totals, sums[1]])
-    sums += joined(near, beside(near_edge, False), 0, [totals, sums[2]])[1] + far
+    sums += joined(near, beside(near_edge, True), 0, [totals, sums[2]])[1] + far
     return call(
         update_kernel,
         shape(estimate.shape, F32),

time: 44.1 us -> 44.3 us (level)
  starting transfers between devices: 23.6 us -> 26.6 us
  waiting for transfers between devices: 11.1 us -> 8.54 us
    ppermute x12, waiting for transfers between devices: 8.79 us -> 6.23 us  [across(): return lax.ppermute(array, 'depth', [(i, i ^ step) for i in range(depth)])]
    ppermute x12, starting transfers between devices: 18.8 us -> 20.4 us  [across(): return lax.ppermute(array, 'depth', [(i, i ^ step) for i in range(depth)])]
    ppermute x3, starting transfers between devices: 4.24 us -> 5.67 us  [beside(): return lax.ppermute(array, ('tile', 'depth'), pairs)]
where the time goes in v8:
time: 44.3 us; the launch traced here: 44.1 us
  starting transfers between devices  26.6 us (60%)
  waiting for transfers between devices  8.54 us (19%)
  Pallas kernels  6.19 us (14%)
  other arithmetic  1.83 us (4%)
  local copies, waits for them, and re-layouts  0.77 us (2%)
    ppermute x12, starting transfers between devices, across(): return lax.ppermute(array, 'depth', [(i, i ^ step) for i in range(depth)])  20.4 us
    ppermute x12, waiting for transfers between devices, across(): return lax.ppermute(array, 'depth', [(i, i ^ step) for i in range(depth)])  6.23 us
    ppermute x3, starting transfers between devices, beside(): return lax.ppermute(array, ('tile', 'depth'), pairs)  5.67 us
    pallas_call x1, Pallas kernels, shards(): call(functools.partial(main_kernel, planes, view_rows), (shape(halves, F3...  3.31 us
    ppermute x3, waiting for transfers between devices, beside(): return lax.ppermute(array, ('tile', 'depth'), pairs)  2.31 us
    pallas_call x1, Pallas kernels, shards(): call(functools.partial(matrices_kernel, planes, strip), (shape((rows, spa...  1.88 us
    convert_element_type x1, other arithmetic, shards(): own = estimate.astype(BF16)  1.05 us
  transfers between devices with their start and end apart: 17, of which 7 were waited for; matrix products, arithmetic and copies ran while one was open for 3% of the time, Pallas kernels for 5%

profile of v8, /device:TPU:0, one launch (start us, length us, event | category | flops | bytes accessed | tf_op | source)
XLA Modules:
  0.0 44.1 jit_solution(11104271824806222354)
XLA Ops:
  0.0 0.0 copy-start.1
  0.0 1.1 %convert_element_type.4 = bf16[2,32,1024]{2,1,0:T(8,128)(2,1)S(1)} convert(f32[2,32,1024]{2,1,0:T(8,128)} %estimate_ref.1) | non-fusion elementwise | flops 65536 | bytes 393216 | tf_op jit(solution)/shard_map/convert_element_type | solution.py:257
  1.1 5.1 %collective-permute-start.2 = (bf16[2,16,1024]{2,1,0:T(8,128)(2,1)S(1)}, bf16[2,16,1024]{2,1,0:T(8,128)(2,1)S(1)}, u32[]{:S(2)}, u32[]{:S(2)}) collective-permute-start(bf16[2,16,1024]{2,1,0:T(8,128)(2,1)S(1)} %get-tuple-element.62), channel_id=1, source_target_pairs={{0,3},{1,2},{2,1},{3,0},{4,7},{5,6},{6,5},{7,4},{8,11},{9,10},{10,... | collective-permute-start | bytes 196616 | tf_op jit(solution)/shard_map/ppermute | solution.py:242
  6.2 0.0 collective-permute-start.1
  6.2 0.6 %collective-permute-start = (bf16[2,16,1024]{2,1,0:T(8,128)(2,1)S(1)}, bf16[2,16,1024]{2,1,0:T(8,128)(2,1)S(1)}, u32[]{:S(2)}, u32[]{:S(2)}) collective-permute-start(bf16[2,16,1024]{2,1,0:T(8,128)(2,1)S(1)} %get-tuple-element.62), channel_id=1, source_target_pairs={{0,1},{1,0},{2,3},{3,2},{4,5},{5,4},{6,7},{7,6},{8,9},{9,8},{10,11... | collective-permute-start | bytes 196616 | tf_op jit(solution)/shard_map/ppermute | solution.py:242
  6.8 0.7 %concatenate.9.device_ref.info_ref = s32[12]{0:T(128)S(1)} concatenate(s32[1]{0:T(128)} %bitcast, s32[1]{0:T(128)} %bitcast.1, s32[1]{0:T(128)} %bitcast.2, s32[1]{0:T(128)} %bitcast.3, s32[8]{0:T(128)} %param.11), dimensions={0} | concatenate | bytes 96 | tf_op jit(solution)/shard_map/concatenate | solution.py:238
  7.6 0.7 %pad_maximum_fusion.1.kernels_ref = f32[3,8,31]{2,1,0:T(8,128)S(1)} fusion(f32[1,8,31]{2,1,0:T(8,128)} %bitcast.9, f32[1,8,31]{2,1,0:T(8,128)} %bitcast.10, f32[1,8,31]{2,1,0:T(8,128)} %bitcast.11), kind=kLoop, calls=%fused_computation.3 | loop fusion | flops 1488 | bytes 5952 | tf_op jit(solution)/shard_map/stack | solution.py:264
  8.3 0.5 %collective-permute-done.2 = bf16[2,16,1024]{2,1,0:T(8,128)(2,1)S(1)} collective-permute-done((bf16[2,16,1024]{2,1,0:T(8,128)(2,1)S(1)}, bf16[2,16,1024]{2,1,0:T(8,128)(2,1)S(1)}, u32[]{:S(2)}, u32[]{:S(2)}) %collective-permute-start.2) | collective-permute-done | bytes 65568 | tf_op jit(solution)/shard_map/ppermute | solution.py:242
  8.8 4.2 %collective-permute-start.6 = (bf16[2,16,1024]{2,1,0:T(8,128)(2,1)S(1)}, bf16[2,16,1024]{2,1,0:T(8,128)(2,1)S(1)}, u32[]{:S(2)}, u32[]{:S(2)}) collective-permute-start(bf16[2,16,1024]{2,1,0:T(8,128)(2,1)S(1)} %get-tuple-element.36), channel_id=1, source_target_pairs={{0,3},{1,2},{2,1},{3,0},{4,7},{5,6},{6,5},{7,4},{8,11},{9,10},{10,... | collective-permute-start | bytes 196616 | tf_op jit(solution)/shard_map/ppermute | solution.py:242
  13.0 0.0 collective-permute-start.5
  13.0 0.6 %collective-permute-start.4 = (bf16[2,16,1024]{2,1,0:T(8,128)(2,1)S(1)}, bf16[2,16,1024]{2,1,0:T(8,128)(2,1)S(1)}, u32[]{:S(2)}, u32[]{:S(2)}) collective-permute-start(bf16[2,16,1024]{2,1,0:T(8,128)(2,1)S(1)} %get-tuple-element.36), channel_id=1, source_target_pairs={{0,1},{1,0},{2,3},{3,2},{4,5},{5,4},{6,7},{7,6},{8,9},{9,8},{10,11... | collective-permute-start | bytes 196616 | tf_op jit(solution)/shard_map/ppermute | solution.py:242
  13.5 0.0 collective-permute-done.1
  13.5 0.0 collective-permute-done
  13.6 1.5 %collective-permute-start.3 = (bf16[8,16,1024]{2,1,0:T(8,128)(2,1)S(1)}, bf16[8,16,1024]{2,1,0:T(8,128)(2,1)S(1)}, u32[]{:S(2)}, u32[]{:S(2)}) collective-permute-start(bf16[8,16,1024]{2,1,0:T(8,128)(2,1)S(1)} %pad_maximum_fusion.refs_1_), channel_id=1, source_target_pairs={{0,1},{4,8},{8,4},{12,16},{16,12},{20,24},{24,20},{28,29},{1,0},{5... | collective-permute-start | bytes 786440 | tf_op jit(solution)/shard_map/ppermute | solution.py:252
  15.1 1.9 %shard_map.64 = (bf16[512,512]{1,0:T(8,128)(2,1)S(1)}, bf16[512,512]{1,0:T(8,128)(2,1)S(1)}, bf16[8,512,256]{2,1,0:T(8,128)(2,1)S(1)}, bf16[8,512,256]{2,1,0:T(8,128)(2,1)S(1)}) custom-call(s32[12]{0:T(128)S(1)} %concatenate.9.device_ref.info_ref, f32[3,8,31]{2,1,0:T(8,128)S(1)} %pad_maximum_fusion.1.kernels_ref), custom_call_target="tpu_custom_call" | custom-call | flops 100000000 | bytes 5242880 | tf_op jit(solution)/shard_map/pallas_call | solution.py:265
  17.0 0.0 collective-permute-done.6
  17.0 1.3 %collective-permute-done.5 = bf16[2,16,1024]{2,1,0:T(8,128)(2,1)S(1)} collective-permute-done((bf16[2,16,1024]{2,1,0:T(8,128)(2,1)S(1)}, bf16[2,16,1024]{2,1,0:T(8,128)(2,1)S(1)}, u32[]{:S(2)}, u32[]{:S(2)}) %collective-permute-start.5) | collective-permute-done | bytes 65568 | tf_op jit(solution)/shard_map/ppermute | solution.py:242
  18.3 0.0 collective-permute-done.4
  18.4 0.1 collective-permute-start.7
  18.5 2.3 %collective-permute-done.3.refs_0_ = bf16[8,16,1024]{2,1,0:T(8,128)(2,1)S(1)} collective-permute-done((bf16[8,16,1024]{2,1,0:T(8,128)(2,1)S(1)}, bf16[8,16,1024]{2,1,0:T(8,128)(2,1)S(1)}, u32[]{:S(2)}, u32[]{:S(2)}) %collective-permute-start.3) | collective-permute-done | bytes 262176 | tf_op jit(solution)/shard_map/ppermute | solution.py:252
  20.8 0.0 collective-permute-done.7.refs_3_
  20.8 0.0 copy-done.1
  20.8 0.0 copy-start
  20.8 3.3 %shard_map.65 = (f32[8,16,1024]{2,1,0:T(8,128)S(1)}, bf16[8,16,1024]{2,1,0:T(8,128)(2,1)S(1)}, f32[4,16,1024]{2,1,0:T(8,128)S(1)}, f32[4,16,1024]{2,1,0:T(8,128)...) custom-call(s32[12]{0:T(128)S(1)} %concatenate.9.device_ref.info_ref, ...), custom_call_target="tpu_custom_call" | custom-call | flops 2000000000 | bytes 10485760 | tf_op jit(solution)/shard_map/pallas_call | solution.py:277
  24.1 0.5 %collective-permute-start.8 = (bf16[8,16,1024]{2,1,0:T(8,128)(2,1)S(1)}, bf16[8,16,1024]{2,1,0:T(8,128)(2,1)S(1)}, u32[]{:S(2)}, u32[]{:S(2)}) collective-permute-start(bf16[8,16,1024]{2,1,0:T(8,128)(2,1)S(1)} %get-tuple-element.46), channel_id=1, source_target_pairs={{0,4},{4,0},{8,12},{12,8},{16,20},{20,16},{24,28},{28,24},{1,5},{5... | collective-permute-start | bytes 786440 | tf_op jit(solution)/shard_map/ppermute | solution.py:255
  24.6 2.7 %collective-permute-start.12 = (bf16[4,16,1024]{2,1,0:T(8,128)(2,1)S(1)}, bf16[4,16,1024]{2,1,0:T(8,128)(2,1)S(1)}, u32[]{:S(2)}, u32[]{:S(2)}) collective-permute-start(bf16[4,16,1024]{2,1,0:T(8,128)(2,1)S(1)} %get-tuple-element.54), channel_id=1, source_target_pairs={{0,28},{4,8},{8,4},{12,16},{16,12},{20,24},{24,20},{28,0},{1,29},{... | collective-permute-start | bytes 393224 | tf_op jit(solution)/shard_map/ppermute | solution.py:252
  27.3 1.5 %collective-permute-start.13 = (bf16[4,16,1024]{2,1,0:T(8,128)(2,1)S(1)}, bf16[4,16,1024]{2,1,0:T(8,128)(2,1)S(1)}, u32[]{:S(2)}, u32[]{:S(2)}) collective-permute-start(bf16[4,16,1024]{2,1,0:T(8,128)(2,1)S(1)} %get-tuple-element.58), channel_id=1, source_target_pairs={{0,1},{4,8},{8,4},{12,16},{16,12},{20,24},{24,20},{28,29},{1,0},{5... | collective-permute-start | bytes 393224 | tf_op jit(solution)/shard_map/ppermute | solution.py:252
  28.7 0.0 collective-permute-done.8.other_ref
  28.7 0.1 shard_map.66
  28.8 0.6 %collective-permute-start.9 = (bf16[2,16,1024]{2,1,0:T(8,128)(2,1)S(1)}, bf16[2,16,1024]{2,1,0:T(8,128)(2,1)S(1)}, u32[]{:S(2)}, u32[]{:S(2)}) collective-permute-start(bf16[2,16,1024]{2,1,0:T(8,128)(2,1)S(1)} %get-tuple-element.48), channel_id=1, source_target_pairs={{0,1},{1,0},{2,3},{3,2},{4,5},{5,4},{6,7},{7,6},{8,9},{9,8},{10,11... | collective-permute-start | bytes 196616 | tf_op jit(solution)/shard_map/ppermute | solution.py:242
  29.4 2.4 %collective-permute-start.10 = (bf16[2,16,1024]{2,1,0:T(8,128)(2,1)S(1)}, bf16[2,16,1024]{2,1,0:T(8,128)(2,1)S(1)}, u32[]{:S(2)}, u32[]{:S(2)}) collective-permute-start(bf16[2,16,1024]{2,1,0:T(8,128)(2,1)S(1)} %get-tuple-element.49), channel_id=1, source_target_pairs={{0,2},{1,3},{2,0},{3,1},{4,6},{5,7},{6,4},{7,5},{8,10},{9,11},{10,... | collective-permute-start | bytes 196616 | tf_op jit(solution)/shard_map/ppermute | solution.py:242
  31.9 1.4 %collective-permute-start.11 = (bf16[2,16,1024]{2,1,0:T(8,128)(2,1)S(1)}, bf16[2,16,1024]{2,1,0:T(8,128)(2,1)S(1)}, u32[]{:S(2)}, u32[]{:S(2)}) collective-permute-start(bf16[2,16,1024]{2,1,0:T(8,128)(2,1)S(1)} %get-tuple-element.50), channel_id=1, source_target_pairs={{0,3},{1,2},{2,1},{3,0},{4,7},{5,6},{6,5},{7,4},{8,11},{9,10},{10,... | collective-permute-start | bytes 196616 | tf_op jit(solution)/shard_map/ppermute | solution.py:242
  33.3 0.4 collective-permute-done.9.refs_1_
  33.6 0.0 collective-permute-done.12.other_ref
  33.7 3.2 %collective-permute-start.15 = (bf16[2,16,1024]{2,1,0:T(8,128)(2,1)S(1)}, bf16[2,16,1024]{2,1,0:T(8,128)(2,1)S(1)}, u32[]{:S(2)}, u32[]{:S(2)}) collective-permute-start(bf16[2,16,1024]{2,1,0:T(8,128)(2,1)S(1)} %get-tuple-element.55), channel_id=1, source_target_pairs={{0,2},{1,3},{2,0},{3,1},{4,6},{5,7},{6,4},{7,5},{8,10},{9,11},{10,... | collective-permute-start | bytes 196616 | tf_op jit(solution)/shard_map/ppermute | solution.py:242
  36.9 1.1 %collective-permute-start.16 = (bf16[2,16,1024]{2,1,0:T(8,128)(2,1)S(1)}, bf16[2,16,1024]{2,1,0:T(8,128)(2,1)S(1)}, u32[]{:S(2)}, u32[]{:S(2)}) collective-permute-start(bf16[2,16,1024]{2,1,0:T(8,128)(2,1)S(1)} %get-tuple-element.56), channel_id=1, source_target_pairs={{0,3},{1,2},{2,1},{3,0},{4,7},{5,6},{6,5},{7,4},{8,11},{9,10},{10,... | collective-permute-start | bytes 196616 | tf_op jit(solution)/shard_map/ppermute | solution.py:242
  38.0 0.0 collective-permute-done.10.refs_2_
  38.0 0.0 collective-permute-done.13.other_ref
  38.0 1.1 %collective-permute-start.14 = (bf16[2,16,1024]{2,1,0:T(8,128)(2,1)S(1)}, bf16[2,16,1024]{2,1,0:T(8,128)(2,1)S(1)}, u32[]{:S(2)}, u32[]{:S(2)}) collective-permute-start(bf16[2,16,1024]{2,1,0:T(8,128)(2,1)S(1)} %get-tuple-element.60), channel_id=1, source_target_pairs={{0,1},{1,0},{2,3},{3,2},{4,5},{5,4},{6,7},{7,6},{8,9},{9,8},{10,11... | collective-permute-start | bytes 196616 | tf_op jit(solution)/shard_map/ppermute | solution.py:242
  39.1 0.0 collective-permute-done.11.refs_3_
  39.1 2.7 %collective-permute-done.15.refs_6_ = bf16[2,16,1024]{2,1,0:T(8,128)(2,1)S(1)} collective-permute-done((bf16[2,16,1024]{2,1,0:T(8,128)(2,1)S(1)}, bf16[2,16,1024]{2,1,0:T(8,128)(2,1)S(1)}, u32[]{:S(2)}, u32[]{:S(2)}) %collective-permute-start.15) | collective-permute-done | bytes 65568 | tf_op jit(solution)/shard_map/ppermute | solution.py:242
  41.8 1.3 %collective-permute-done.16.refs_7_ = bf16[2,16,1024]{2,1,0:T(8,128)(2,1)S(1)} collective-permute-done((bf16[2,16,1024]{2,1,0:T(8,128)(2,1)S(1)}, bf16[2,16,1024]{2,1,0:T(8,128)(2,1)S(1)}, u32[]{:S(2)}, u32[]{:S(2)}) %collective-permute-start.16) | collective-permute-done | bytes 65568 | tf_op jit(solution)/shard_map/ppermute | solution.py:242
  43.1 0.1 collective-permute-done.14.refs_5_
  43.2 0.0 copy-done
  43.2 0.8 %shard_map.69 = f32[2,32,1024]{2,1,0:T(8,128)} custom-call(f32[2,32,1024]{2,1,0:T(8,128)S(1)} %copy-done, f32[32,128]{1,0:T(8,128)S(1)} %get-tuple-element.43.scale_ref, s32[16,128]{1,0:T(8,128)S(1)} %get-tuple-element.44.odd_ref, f32[2,16,1024]{2,1,0:T(8,128)S(1)} %get-tuple-element.47.refs_0_, bf16[2,16,1024]{2,1,0:T(8,128)(2,1)S(1)} %collective-permute-done.9.refs_1_, ...), custom_call_target="tpu_custom_call" | custom-call | flops 1000000 | bytes 1048576 | tf_op jit(solution)/shard_map/pallas_call | solution.py:306
  (8 shorter events, 0.2 us)
Async XLA Ops:
  0.0 20.8 %copy-start.1 = (bf16[8,2,32,1024]{3,2,1,0:T(8,128)(2,1)S(1)}, bf16[8,2,32,1024]{3,2,1,0:T(8,128)(2,1)}, u32[]{:S(2)}) copy-start(bf16[8,2,32,1024]{3,2,1,0:T(8,128)(2,1)} %param.7) | copy-start | bytes 3145732
  1.1 7.7 %collective-permute-start.2 = (bf16[2,16,1024]{2,1,0:T(8,128)(2,1)S(1)}, bf16[2,16,1024]{2,1,0:T(8,128)(2,1)S(1)}, u32[]{:S(2)}, u32[]{:S(2)}) collective-permute-start(bf16[2,16,1024]{2,1,0:T(8,128)(2,1)S(1)} %get-tuple-element.62), channel_id=1, source_target_pairs={{0,3},{1,2},{2,1},{3,0},{4,7},{5,6},{6,5},{7,4},{8,11},{9,10},{10,... | collective-permute-start | bytes 196616 | tf_op jit(solution)/shard_map/ppermute | solution.py:242
  6.2 7.4 %collective-permute-start.1 = (bf16[2,16,1024]{2,1,0:T(8,128)(2,1)S(1)}, bf16[2,16,1024]{2,1,0:T(8,128)(2,1)S(1)}, u32[]{:S(2)}, u32[]{:S(2)}) collective-permute-start(bf16[2,16,1024]{2,1,0:T(8,128)(2,1)S(1)} %get-tuple-element.62), channel_id=1, source_target_pairs={{0,2},{1,3},{2,0},{3,1},{4,6},{5,7},{6,4},{7,5},{8,10},{9,11},{10,... | collective-permute-start | bytes 196616 | tf_op jit(solution)/shard_map/ppermute | solution.py:242
  6.2 7.4 %collective-permute-start = (bf16[2,16,1024]{2,1,0:T(8,128)(2,1)S(1)}, bf16[2,16,1024]{2,1,0:T(8,128)(2,1)S(1)}, u32[]{:S(2)}, u32[]{:S(2)}) collective-permute-start(bf16[2,16,1024]{2,1,0:T(8,128)(2,1)S(1)} %get-tuple-element.62), channel_id=1, source_target_pairs={{0,1},{1,0},{2,3},{3,2},{4,5},{5,4},{6,7},{7,6},{8,9},{9,8},{10,11... | collective-permute-start | bytes 196616 | tf_op jit(solution)/shard_map/ppermute | solution.py:242
  8.8 8.2 %collective-permute-start.6 = (bf16[2,16,1024]{2,1,0:T(8,128)(2,1)S(1)}, bf16[2,16,1024]{2,1,0:T(8,128)(2,1)S(1)}, u32[]{:S(2)}, u32[]{:S(2)}) collective-permute-start(bf16[2,16,1024]{2,1,0:T(8,128)(2,1)S(1)} %get-tuple-element.36), channel_id=1, source_target_pairs={{0,3},{1,2},{2,1},{3,0},{4,7},{5,6},{6,5},{7,4},{8,11},{9,10},{10,... | collective-permute-start | bytes 196616 | tf_op jit(solution)/shard_map/ppermute | solution.py:242
  13.0 5.3 %collective-permute-start.5 = (bf16[2,16,1024]{2,1,0:T(8,128)(2,1)S(1)}, bf16[2,16,1024]{2,1,0:T(8,128)(2,1)S(1)}, u32[]{:S(2)}, u32[]{:S(2)}) collective-permute-start(bf16[2,16,1024]{2,1,0:T(8,128)(2,1)S(1)} %get-tuple-element.36), channel_id=1, source_target_pairs={{0,2},{1,3},{2,0},{3,1},{4,6},{5,7},{6,4},{7,5},{8,10},{9,11},{10,... | collective-permute-start | bytes 196616 | tf_op jit(solution)/shard_map/ppermute | solution.py:242
  13.0 5.3 %collective-permute-start.4 = (bf16[2,16,1024]{2,1,0:T(8,128)(2,1)S(1)}, bf16[2,16,1024]{2,1,0:T(8,128)(2,1)S(1)}, u32[]{:S(2)}, u32[]{:S(2)}) collective-permute-start(bf16[2,16,1024]{2,1,0:T(8,128)(2,1)S(1)} %get-tuple-element.36), channel_id=1, source_target_pairs={{0,1},{1,0},{2,3},{3,2},{4,5},{5,4},{6,7},{7,6},{8,9},{9,8},{10,11... | collective-permute-start | bytes 196616 | tf_op jit(solution)/shard_map/ppermute | solution.py:242
  13.6 7.2 %collective-permute-start.3 = (bf16[8,16,1024]{2,1,0:T(8,128)(2,1)S(1)}, bf16[8,16,1024]{2,1,0:T(8,128)(2,1)S(1)}, u32[]{:S(2)}, u32[]{:S(2)}) collective-permute-start(bf16[8,16,1024]{2,1,0:T(8,128)(2,1)S(1)} %pad_maximum_fusion.refs_1_), channel_id=1, source_target_pairs={{0,1},{4,8},{8,4},{12,16},{16,12},{20,24},{24,20},{28,29},{1,0},{5... | collective-permute-start | bytes 786440 | tf_op jit(solution)/shard_map/ppermute | solution.py:252
  18.4 2.4 %collective-permute-start.7 = (bf16[8,16,1024]{2,1,0:T(8,128)(2,1)S(1)}, bf16[8,16,1024]{2,1,0:T(8,128)(2,1)S(1)}, u32[]{:S(2)}, u32[]{:S(2)}) collective-permute-start(bf16[8,16,1024]{2,1,0:T(8,128)(2,1)S(1)} %constant_dynamic-update-slice_fusion.refs_2_), channel_id=1, source_target_pairs={{0,4},{4,0},{8,12},{12,8},{16,20},{20,16},{24,28},{28,24},{1,5},{5... | collective-permute-start | bytes 786440 | tf_op jit(solution)/shard_map/ppermute | solution.py:255
  20.8 22.4 %copy-start = (f32[2,32,1024]{2,1,0:T(8,128)S(1)}, f32[2,32,1024]{2,1,0:T(8,128)}, u32[]{:S(2)}) copy-start(f32[2,32,1024]{2,1,0:T(8,128)} %estimate_ref.1) | copy-start | bytes 786436
  24.1 4.6 %collective-permute-start.8 = (bf16[8,16,1024]{2,1,0:T(8,128)(2,1)S(1)}, bf16[8,16,1024]{2,1,0:T(8,128)(2,1)S(1)}, u32[]{:S(2)}, u32[]{:S(2)}) collective-permute-start(bf16[8,16,1024]{2,1,0:T(8,128)(2,1)S(1)} %get-tuple-element.46), channel_id=1, source_target_pairs={{0,4},{4,0},{8,12},{12,8},{16,20},{20,16},{24,28},{28,24},{1,5},{5... | collective-permute-start | bytes 786440 | tf_op jit(solution)/shard_map/ppermute | solution.py:255
  24.6 9.1 %collective-permute-start.12 = (bf16[4,16,1024]{2,1,0:T(8,128)(2,1)S(1)}, bf16[4,16,1024]{2,1,0:T(8,128)(2,1)S(1)}, u32[]{:S(2)}, u32[]{:S(2)}) collective-permute-start(bf16[4,16,1024]{2,1,0:T(8,128)(2,1)S(1)} %get-tuple-element.54), channel_id=1, source_target_pairs={{0,28},{4,8},{8,4},{12,16},{16,12},{20,24},{24,20},{28,0},{1,29},{... | collective-permute-start | bytes 393224 | tf_op jit(solution)/shard_map/ppermute | solution.py:252
  27.3 10.7 %collective-permute-start.13 = (bf16[4,16,1024]{2,1,0:T(8,128)(2,1)S(1)}, bf16[4,16,1024]{2,1,0:T(8,128)(2,1)S(1)}, u32[]{:S(2)}, u32[]{:S(2)}) collective-permute-start(bf16[4,16,1024]{2,1,0:T(8,128)(2,1)S(1)} %get-tuple-element.58), channel_id=1, source_target_pairs={{0,1},{4,8},{8,4},{12,16},{16,12},{20,24},{24,20},{28,29},{1,0},{5... | collective-permute-start | bytes 393224 | tf_op jit(solution)/shard_map/ppermute | solution.py:252
  28.8 4.8 %collective-permute-start.9 = (bf16[2,16,1024]{2,1,0:T(8,128)(2,1)S(1)}, bf16[2,16,1024]{2,1,0:T(8,128)(2,1)S(1)}, u32[]{:S(2)}, u32[]{:S(2)}) collective-permute-start(bf16[2,16,1024]{2,1,0:T(8,128)(2,1)S(1)} %get-tuple-element.48), channel_id=1, source_target_pairs={{0,1},{1,0},{2,3},{3,2},{4,5},{5,4},{6,7},{7,6},{8,9},{9,8},{10,11... | collective-permute-start | bytes 196616 | tf_op jit(solution)/shard_map/ppermute | solution.py:242
  29.4 8.6 %collective-permute-start.10 = (bf16[2,16,1024]{2,1,0:T(8,128)(2,1)S(1)}, bf16[2,16,1024]{2,1,0:T(8,128)(2,1)S(1)}, u32[]{:S(2)}, u32[]{:S(2)}) collective-permute-start(bf16[2,16,1024]{2,1,0:T(8,128)(2,1)S(1)} %get-tuple-element.49), channel_id=1, source_target_pairs={{0,2},{1,3},{2,0},{3,1},{4,6},{5,7},{6,4},{7,5},{8,10},{9,11},{10,... | collective-permute-start | bytes 196616 | tf_op jit(solution)/shard_map/ppermute | solution.py:242
  31.9 7.3 %collective-permute-start.11 = (bf16[2,16,1024]{2,1,0:T(8,128)(2,1)S(1)}, bf16[2,16,1024]{2,1,0:T(8,128)(2,1)S(1)}, u32[]{:S(2)}, u32[]{:S(2)}) collective-permute-start(bf16[2,16,1024]{2,1,0:T(8,128)(2,1)S(1)} %get-tuple-element.50), channel_id=1, source_target_pairs={{0,3},{1,2},{2,1},{3,0},{4,7},{5,6},{6,5},{7,4},{8,11},{9,10},{10,... | collective-permute-start | bytes 196616 | tf_op jit(solution)/shard_map/ppermute | solution.py:242
  33.7 8.1 %collective-permute-start.15 = (bf16[2,16,1024]{2,1,0:T(8,128)(2,1)S(1)}, bf16[2,16,1024]{2,1,0:T(8,128)(2,1)S(1)}, u32[]{:S(2)}, u32[]{:S(2)}) collective-permute-start(bf16[2,16,1024]{2,1,0:T(8,128)(2,1)S(1)} %get-tuple-element.55), channel_id=1, source_target_pairs={{0,2},{1,3},{2,0},{3,1},{4,6},{5,7},{6,4},{7,5},{8,10},{9,11},{10,... | collective-permute-start | bytes 196616 | tf_op jit(solution)/shard_map/ppermute | solution.py:242
  36.9 6.2 %collective-permute-start.16 = (bf16[2,16,1024]{2,1,0:T(8,128)(2,1)S(1)}, bf16[2,16,1024]{2,1,0:T(8,128)(2,1)S(1)}, u32[]{:S(2)}, u32[]{:S(2)}) collective-permute-start(bf16[2,16,1024]{2,1,0:T(8,128)(2,1)S(1)} %get-tuple-element.56), channel_id=1, source_target_pairs={{0,3},{1,2},{2,1},{3,0},{4,7},{5,6},{6,5},{7,4},{8,11},{9,10},{10,... | collective-permute-start | bytes 196616 | tf_op jit(solution)/shard_map/ppermute | solution.py:242
  38.0 5.2 %collective-permute-start.14 = (bf16[2,16,1024]{2,1,0:T(8,128)(2,1)S(1)}, bf16[2,16,1024]{2,1,0:T(8,128)(2,1)S(1)}, u32[]{:S(2)}, u32[]{:S(2)}) collective-permute-start(bf16[2,16,1024]{2,1,0:T(8,128)(2,1)S(1)} %get-tuple-element.60), channel_id=1, source_target_pairs={{0,1},{1,0},{2,3},{3,2},{4,5},{5,4},{6,7},{7,6},{8,9},{9,8},{10,11... | collective-permute-start | bytes 196616 | tf_op jit(solution)/shard_map/ppermute | solution.py:242
